TPU v7x, 32 devices: a whole 2x2x4 slice. The times are simulated.
32 devices in a mesh: grp: 4 (over y, x), head: 8 (over z, core).
Axes of the slice: x: 2, y: 2, z: 4, core: 2. Of those that a mesh axis runs over, the one named last changes fastest.
Arguments:
- prefill_token_rows: bfloat16 [256, 8192], P('grp', 'head'), may hold values from -6 to 6
- decode_token_rows: bfloat16 [3, 128, 8192], P(None, 'grp', 'head'), may hold values from -6 to 6
- input_weight: bfloat16 [8192, 2048], P('head'), may hold values from -0.0625 to 0.0625
- lowrank_weight: bfloat16 [8192, 384], P('head'), may hold values from -0.0625 to 0.0625
- step_size_weight: bfloat16 [8192, 16], P('head'), may hold values from -0.0625 to 0.0625
- adapter_up_weight: bfloat16 [128, 1024], P(None, 'head'), may hold values from -1.5 to 1.5
- output_weight: bfloat16 [1024, 8192], P('head'), may hold values from -0.25 to 0.25
- head_decay_rate: float32 [16], P('head'), may hold values from 0.0005 to 0.1
- head_step_bias: float32 [16], P('head'), may hold values from -1 to 1
- head_skip_scale: float32 [16], P('head'), may hold values from 0 to 3
- gated_norm_scale: float32 [1024], P('head'), may hold values from 0.1 to 1.9
- prompt_start_state: float32 [8, 16, 64, 128], P('grp', 'head'), may hold values from -18 to 18
- prompt_at_position: int32 [8], replicated, may hold values from 0 to 7, each once
- slot_sample_index: int32 [128], P('grp'), may hold values from 0 to 127, each once
- prompt_adapter_index: int32 [8], replicated, may hold values from 0 to 7
Outputs:
- prefill_out: float32 [256, 8192], P('grp', 'head')
- decode_out: float32 [3, 128, 8192], P(None, 'grp', 'head')
Inputs may be any that keep to these rules, and one draw needn't show every extreme that they name: Position i of the prefill rows and of prompt_start_state holds prompt prompt_at_position[i]; every prompt stands once. Decode slot j carries sample slot_sample_index[j] of prompt slot_sample_index[j] // 16; every sample stands once. `prompt_adapter_index`: the adapter used by every row of that prompt and of its samples.
All inputs are finite; a program needn't handle non-finite values.
Results may differ from a plain program's by a relative error of at most 0.0027.
Values may be sent and summed in bfloat16 or wider, within the bound.
No kernel may reach another device: no remote copies, remote signals or barrier semaphores. Data moves between devices by JAX's collectives and lax.ppermute only.
A program may use at most 64 MiB of HBM per device.

v0:
```python
import jax
import jax.numpy as jnp
from jax import lax
from jax.sharding import PartitionSpec as P

HEAD_CHANNELS = 64
STATE = 128
HEAD_DEV = 2
STRETCH = 32
SAMPLES = 16
STEPS = 3
ADAPTER_RANK = 16


def block_pass(value_channels, write_vector, read_vector, head_step_length, initial, rate, skip):
    length = value_channels.shape[0]
    log_decay = -(head_step_length * rate[None, :])
    running = jnp.cumsum(log_decay, axis=0).T
    later = (
        jnp.arange(length, dtype=jnp.int32)[:, None] >= jnp.arange(length, dtype=jnp.int32)[None, :]
    )
    spread = jnp.where(later[None], running[:, :, None] - running[:, None, :], 0.0)
    weights = jnp.where(later[None], jnp.exp(spread), 0.0) * head_step_length.T[:, None, :]
    scores = jnp.dot(read_vector, write_vector.T, precision=lax.Precision.HIGHEST)
    mixed = weights * scores[None]
    result = jnp.einsum("hts,shp->thp", mixed, value_channels, precision=lax.Precision.HIGHEST)
    carried = jnp.einsum("hpn,tn->thp", initial, read_vector, precision=lax.Precision.HIGHEST)
    result = (
        result + jnp.exp(running).T[:, :, None] * carried + skip[None, :, None] * value_channels
    )
    ending = running[:, -1]
    tail = jnp.exp(ending[None, :] - running.T) * head_step_length
    final = jnp.exp(ending)[:, None, None] * initial + jnp.einsum(
        "sh,shp,sn->hpn", tail, value_channels, write_vector, precision=lax.Precision.HIGHEST
    )
    return (result, final)


def prepare_inputs(
    token_rows,
    adapter_index,
    columns,
    lowrank_weight,
    step_size_weight,
    adapter_up_weight,
    head_step_bias,
    heads_leading,
):
    token_count = token_rows.shape[0]
    proj = jnp.dot(
        lax.all_gather(token_rows, "head", axis=1, tiled=True),
        columns,
        preferred_element_type=jnp.float32,
    )
    low = jnp.dot(token_rows, lowrank_weight, preferred_element_type=jnp.float32)
    raw = jnp.dot(token_rows, step_size_weight, preferred_element_type=jnp.float32)
    low, raw = lax.psum((low, raw), "head")
    proj = proj.reshape(token_count, HEAD_DEV, 2, HEAD_CHANNELS)
    slot_lanes = jnp.arange(adapter_up_weight.shape[0], dtype=jnp.int32) // ADAPTER_RANK
    selected_rows = jnp.where(
        slot_lanes[None, :] == adapter_index[:, None], low[:, 2 * STATE :], 0.0
    ).astype(jnp.bfloat16)
    step_delta = jnp.dot(
        selected_rows, adapter_up_weight, preferred_element_type=jnp.float32
    ).reshape(token_count, HEAD_DEV, HEAD_CHANNELS)
    value_channels = proj[:, :, 0, :] + step_delta
    gate_branch = proj[:, :, 1, :]
    own_raw = lax.dynamic_slice_in_dim(raw, heads_leading, HEAD_DEV, 1)
    head_step_length = jax.nn.softplus(own_raw + head_step_bias[None, :])
    return (
        value_channels,
        gate_branch,
        low[:, :STATE],
        low[:, STATE : 2 * STATE],
        head_step_length,
    )


def finish(result, gate_branch, token_rows, gated_norm_scale, output_weight):
    token_count = result.shape[0]
    gated = (result * jax.nn.silu(gate_branch)).reshape(token_count, HEAD_DEV * HEAD_CHANNELS)
    scale = lax.rsqrt(jnp.mean(gated * gated, axis=1, keepdims=True) + 1e-05)
    normed = (gated * scale * gated_norm_scale[None, :]).astype(jnp.bfloat16)
    summed = lax.psum_scatter(
        lax.dot_general(
            output_weight, normed, (((0,), (1,)), ((), ())), preferred_element_type=jnp.float32
        ),
        "head",
        scatter_dimension=0,
        tiled=True,
    ).T
    return token_rows.astype(jnp.float32) + summed


def on_device(
    prefill_token_rows,
    decode_token_rows,
    input_weight,
    lowrank_weight,
    step_size_weight,
    adapter_up_weight,
    output_weight,
    head_decay_rate,
    head_step_bias,
    head_skip_scale,
    gated_norm_scale,
    prompt_start_state,
    prompt_at_position,
    slot_sample_index,
    prompt_adapter_index,
):
    group = lax.axis_index("grp")
    heads_leading = lax.axis_index("head") * HEAD_DEV
    owned = prompt_start_state.shape[0]
    catalog = jnp.arange(prompt_at_position.shape[0], dtype=jnp.int32)
    held = lax.dynamic_slice_in_dim(prompt_at_position, group * owned, owned, 0)
    prefill_tenant_index = jnp.sum(
        jnp.where(catalog[None, :] == held[:, None], prompt_adapter_index[None, :], 0), axis=1
    )
    prefill_tenant_index = jnp.repeat(prefill_tenant_index, STRETCH)
    columns = lax.all_to_all(input_weight, "head", split_axis=1, concat_axis=0, tiled=True)
    value_channels, gate_branch, write_vector, read_vector, head_step_length = prepare_inputs(
        prefill_token_rows,
        prefill_tenant_index,
        columns,
        lowrank_weight,
        step_size_weight,
        adapter_up_weight,
        head_step_bias,
        heads_leading,
    )
    shaped = (
        value_channels.reshape(owned, STRETCH, HEAD_DEV, HEAD_CHANNELS),
        write_vector.reshape(owned, STRETCH, STATE),
        read_vector.reshape(owned, STRETCH, STATE),
        head_step_length.reshape(owned, STRETCH, HEAD_DEV),
        prompt_start_state,
    )
    results, finals = lax.map(
        lambda group_args: block_pass(
            group_args[0],
            group_args[1],
            group_args[2],
            group_args[3],
            group_args[4],
            head_decay_rate,
            head_skip_scale,
        ),
        shaped,
    )
    prefill_out = finish(
        results.reshape(owned * STRETCH, HEAD_DEV, HEAD_CHANNELS),
        gate_branch,
        prefill_token_rows,
        gated_norm_scale,
        output_weight,
    )
    gathered = lax.all_gather(finals, "grp", axis=0, tiled=True)
    sample_prompt = slot_sample_index // SAMPLES
    place = jnp.sum(
        jnp.where(prompt_at_position[None, :] == sample_prompt[:, None], catalog[None, :], 0),
        axis=1,
    )
    row_adapter_index = jnp.sum(
        jnp.where(catalog[None, :] == sample_prompt[:, None], prompt_adapter_index[None, :], 0),
        axis=1,
    )
    state = jnp.take(gathered, place, axis=0)
    outputs = []
    for step in range(STEPS):
        token_rows = decode_token_rows[step]
        value_channels, gate_branch, write_vector, read_vector, head_step_length = prepare_inputs(
            token_rows,
            row_adapter_index,
            columns,
            lowrank_weight,
            step_size_weight,
            adapter_up_weight,
            head_step_bias,
            heads_leading,
        )
        decay = jnp.exp(-head_step_length * head_decay_rate[None, :])
        state = (
            decay[:, :, None, None] * state
            + (head_step_length[:, :, None] * value_channels)[:, :, :, None]
            * write_vector[:, None, None, :]
        )
        result = (
            jnp.einsum("rhpn,rn->rhp", state, read_vector, precision=lax.Precision.HIGHEST)
            + head_skip_scale[None, :, None] * value_channels
        )
        outputs.append(finish(result, gate_branch, token_rows, gated_norm_scale, output_weight))
    return (prefill_out, jnp.stack(outputs))


def solution(mesh):
    placed = (
        P("grp", "head"),
        P(None, "grp", "head"),
        P("head", None),
        P("head", None),
        P("head", None),
        P(None, "head"),
        P("head", None),
        P("head"),
        P("head"),
        P("head"),
        P("head"),
        P("grp", "head", None, None),
        P(),
        P("grp"),
        P(),
    )
    return jax.shard_map(
        on_device,
        mesh=mesh,
        in_specs=placed,
        out_specs=(P("grp", "head"), P(None, "grp", "head")),
        check_vma=False,
    )
```

profile of v0, /device:TPU:0, one launch (start us, length us, event | category | flops | bytes accessed | tf_op | source)
XLA Modules:
  0.0 381.2 jit_solution(13305376608019619099)
XLA Ops:
  7.2 6.5 %copy.141 = bf16[1024,2048]{0,1:T(8,128)(2,1)} copy(bf16[1024,2048]{1,0:T(8,128)(2,1)} %param.19) | data formatting | bytes 8388608 | tf_op args[2]
  13.7 6.5 %copy.142 = bf16[1024,8,256]{2,0,1:T(8,128)(2,1)} copy(bf16[1024,8,256]{0,2,1:T(8,128)(2,1)} %bitcast.263) | data formatting | bytes 8388608 | tf_op jit(solution)/shard_map/all_to_all | solution.py:121
  20.2 6.5 %all-to-all-start = ((bf16[1024,8,256]{2,0,1:T(8,128)(2,1)}), bf16[1024,8,256]{2,0,1:T(8,128)(2,1)}, u32[]{:S(2)}, u32[]{:S(2)}) async-start(bf16[1024,8,256]{2,0,1:T(8,128)(2,1)} %copy.142), calls=%async_computation | async-start | bytes 8388608 | tf_op jit(solution)/shard_map/all_to_all | solution.py:121
  34.7 97.0 %all-gather = bf16[1,32,8192]{2,1,0:T(8,128)(2,1)S(1)} all-gather(bf16[1,32,1024]{2,1,0:T(8,128)(2,1)S(1)} %get-tuple-element.153), channel_id=2, replica_groups=mesh['grp'=4,'head'=8] {'head'}, dimensions={2}, use_global_device_ids=true | all-gather | bytes 589824 | tf_op jit(solution)/shard_map/all_gather | solution.py:51
  131.7 15.9 %all-gather.1 = bf16[1,32,8192]{2,1,0:T(8,128)(2,1)} all-gather(bf16[1,32,1024]{2,1,0:T(8,128)(2,1)S(1)} %get-tuple-element.155), channel_id=3, replica_groups=mesh['grp'=4,'head'=8] {'head'}, dimensions={2}, use_global_device_ids=true | all-gather | bytes 589824 | tf_op jit(solution)/shard_map/all_gather | solution.py:51
  147.6 16.4 %all-gather.2 = bf16[1,32,8192]{2,1,0:T(8,128)(2,1)} all-gather(bf16[1,32,1024]{2,1,0:T(8,128)(2,1)S(1)} %get-tuple-element.154), channel_id=4, replica_groups=mesh['grp'=4,'head'=8] {'head'}, dimensions={2}, use_global_device_ids=true | all-gather | bytes 589824 | tf_op jit(solution)/shard_map/all_gather | solution.py:51
  165.9 1.3 all-reduce.6.cloned.1.call-done
  168.0 1.3 fusion.157
  172.0 1.4 fusion.155
  176.6 6.4 %copy.143 = bf16[8192,256]{0,1:T(8,128)(2,1)} copy(bf16[8192,256]{1,0:T(8,128)(2,1)} %bitcast.17) | data formatting | bytes 8388608 | tf_op jit(solution)/shard_map/all_to_all | solution.py:121
  183.0 4.4 %fusion.77 = f32[32,2,2,64]{3,0,2,1:T(8,128)S(1)} fusion(bf16[2,2,64,8192]{3,2,1,0:T(8,128)(2,1)} %bitcast.259, bf16[1,32,8192]{2,1,0:T(8,128)(2,1)S(1)} %all-gather), kind=kOutput, calls=%fused_computation.95 | convolution fusion | flops 134217728 | bytes 4751360 | tf_op jit(solution)/shard_map/dot_general | solution.py:50
  188.2 2.0 fusion.41
  190.9 2.0 fusion.39
  193.7 4.7 %fusion.49 = f32[64,2,2,64]{3,0,2,1:T(8,128)S(1)} fusion(bf16[2,2,64,8192]{3,2,1,0:T(8,128)(2,1)} %bitcast.260, bf16[64,8192]{1,0:T(8,128)(2,1)} %all-gather.5.cloned.1.call-done), kind=kOutput, calls=%fused_computation.67 | convolution fusion | flops 268435456 | bytes 5308416 | tf_op jit(solution)/shard_map/dot_general | solution.py:50
  198.4 4.6 %while.12 = (s32[]{:T(128)}, f32[2,32,2,64]{3,1,2,0:T(8,128)S(1)}, f32[2,2,64,128]{3,2,1,0:T(8,128)}, f32[2,32,2,64]{3,1,2,0:T(8,128)S(1)}, f32[2,32,2]{1,0,2:T(...) while((s32[]{:T(128)}, f32[2,32,2,64]{3,1,2,0:T(8,128)S(1)}, ...), condition=%wide.region_5.6_spmd, body=%wide.region_3.5_spmd.sunk | while | flops 15795394 | bytes 483505 | solution.py:139
  198.8 1.0 fusion.204
  201.1 1.0 fusion.204
  203.0 11.2 %all_gather.16 = f32[8,2,64,128]{3,2,1,0:T(8,128)S(1)} all-gather(f32[2,2,64,128]{3,2,1,0:T(8,128)} %get-tuple-element.56), channel_id=1, replica_groups=mesh['grp'=4,'head'=8] {'grp'}, dimensions={0}, use_global_device_ids=true | all-gather | bytes 655360 | tf_op jit(solution)/shard_map/all_gather | solution.py:158
  214.3 2.0 gather_fusion
  216.4 6.8 %fusion.48 = f32[32,1,2,64]{3,1,2,0:T(1,128)S(1)} fusion(f32[32,128,1,1]{1,2,3,0:T(1,128)S(1)} %bitcast.276, f32[32,2,64,128]{3,2,1,0:T(8,128)} %gather_fusion, f32[32,128]{1,0:T(8,128)S(1)} %copy-done.22, f32[32,2,64]{2,1,0:T(2,128)S(1)} %copy-done.11, f32[32,2]{1,0:T(8,128)S(1)} %copy-done.17, pred[32]{0:T(512)(128)(4,1)S(1)} %compare_and_fusion), kind=kOutput, calls=%fused_computation.66 | convolution fusion | flops 8388608 | bytes 2162976 | tf_op jit(solution)/shard_map/rhpn,rn->rhp/dot_general | solution.py:189
  223.2 6.1 %fusion.47 = f32[32,1,2,64]{3,1,2,0:T(1,128)S(1)} fusion(f32[32,128,1,1]{1,2,3,0:T(1,128)S(1)} %bitcast.275, f32[32,2,64,128]{3,2,1,0:T(8,128)S(1)} %copy-done.4, f32[32,128]{1,0:T(8,128)S(1)} %copy-done.23, f32[32,2,64]{2,1,0:T(2,128)S(1)} %copy-done.12, f32[32,2]{1,0:T(8,128)S(1)} %copy-done.18, f32[32,128]{1,0:T(8,128)S(1)} %copy-done.22, ...), kind=kOutput, calls=%fused_computation.65 | convolution fusion | flops 9961472 | bytes 2196000 | tf_op jit(solution)/shard_map/rhpn,rn->rhp/dot_general | solution.py:189
  229.4 6.7 %fusion.43 = f32[32,1,2,64]{3,1,2,0:T(1,128)S(1)} fusion(f32[32,128,1,1]{1,2,3,0:T(1,128)S(1)} %bitcast.274, f32[32,2,64,128]{3,2,1,0:T(8,128)S(1)} %copy-done.4, f32[32,128]{1,0:T(8,128)S(1)} %copy-done.20, f32[32,2,64]{2,1,0:T(2,128)S(1)} %copy-done.13, f32[32,2]{1,0:T(8,128)S(1)} %copy-done.19, f32[32,128]{1,0:T(8,128)S(1)} %copy-done.23, ...), kind=kOutput, calls=%fused_computation.59 | convolution fusion | flops 11534336 | bytes 2229024 | tf_op jit(solution)/shard_map/rhpn,rn->rhp/dot_general | solution.py:189
  236.5 1.5 convolution_bitcast_fusion.2
  238.1 1.4 convolution_bitcast_fusion.3
  239.8 1.5 convolution_bitcast_fusion.4
  241.9 1.8 convolution_bitcast_fusion.1
  243.7 26.9 %reduce-scatter.11.cloned.1.call-done = f32[1024,32]{0,1:T(8,128)} async-done(((f32[8192,32]{0,1:T(8,128)}), f32[1024,32]{0,1:T(8,128)}) %reduce-scatter.11.cloned.1.call-update) | async-done | bytes 131088 | tf_op jit(solution)/shard_map/reduce_scatter | solution.py:84
  270.6 32.8 %reduce-scatter.9.cloned.1.call-done = f32[1024,32]{0,1:T(8,128)} async-done(((f32[8192,32]{0,1:T(8,128)}), f32[1024,32]{0,1:T(8,128)}) %reduce-scatter.9.cloned.1.call-update) | async-done | bytes 131088 | tf_op jit(solution)/shard_map/reduce_scatter | solution.py:84
  303.4 32.8 %reduce-scatter.7.cloned.1.call-done = f32[1024,32]{0,1:T(8,128)} async-done(((f32[8192,32]{0,1:T(8,128)}), f32[1024,32]{0,1:T(8,128)}) %reduce-scatter.7.cloned.1.call-update) | async-done | bytes 131088 | tf_op jit(solution)/shard_map/reduce_scatter | solution.py:84
  336.3 1.1 fusion.81
  338.1 34.5 %reduce-scatter.5.cloned.1.call-done = f32[1024,64]{0,1:T(8,128)} async-done(((f32[8192,64]{0,1:T(8,128)}), f32[1024,64]{0,1:T(8,128)}) %reduce-scatter.5.cloned.1.call-update) | async-done | bytes 262160 | tf_op jit(solution)/shard_map/reduce_scatter | solution.py:84
  372.7 1.7 bitcast_add_fusion
  (171 shorter events, 23.3 us)
Async XLA Ops:
  7.2 229.3 %copy-start = (bf16[128,8192]{1,0:T(8,128)(2,1)S(1)}, bf16[128,8192]{1,0:T(8,128)(2,1)}, u32[]{:S(2)}) copy-start(bf16[128,8192]{1,0:T(8,128)(2,1)} %param.23) | copy-start | bytes 6291460
  20.2 6.6 %copy-start.2 = (bf16[1024,384]{1,0:T(8,128)(2,1)S(1)}, bf16[1024,384]{1,0:T(8,128)(2,1)}, u32[]{:S(2)}) copy-start(bf16[1024,384]{1,0:T(8,128)(2,1)} %param.20) | copy-start | bytes 2359300
  20.2 6.6 %copy-start.5 = (bf16[64,1024]{1,0:T(8,128)(2,1)S(1)}, bf16[64,1024]{1,0:T(8,128)(2,1)}, u32[]{:S(2)}) copy-start(bf16[64,1024]{1,0:T(8,128)(2,1)} %param.17) | copy-start | bytes 393220
  20.2 7.5 %copy-start.7 = (bf16[3,32,1024]{2,1,0:T(8,128)(2,1)S(1)}, bf16[3,32,1024]{2,1,0:T(8,128)(2,1)}, u32[]{:S(2)}) copy-start(bf16[3,32,1024]{2,1,0:T(8,128)(2,1)} %param.18) | copy-start | bytes 589828
  20.2 7.6 %copy-start.14 = (bf16[1024,16]{0,1:T(8,128)(2,1)S(1)}, bf16[1024,16]{0,1:T(8,128)(2,1)}, u32[]{:S(2)}) copy-start(bf16[1024,16]{0,1:T(8,128)(2,1)} %param.21) | copy-start | bytes 98308
  20.2 156.4 %all-to-all-start = ((bf16[1024,8,256]{2,0,1:T(8,128)(2,1)}), bf16[1024,8,256]{2,0,1:T(8,128)(2,1)}, u32[]{:S(2)}, u32[]{:S(2)}) async-start(bf16[1024,8,256]{2,0,1:T(8,128)(2,1)} %copy.142), calls=%async_computation | async-start | bytes 8388608 | tf_op jit(solution)/shard_map/all_to_all | solution.py:121
  26.7 7.4 %copy-start.29 = (s32[8]{0:T(128)S(1)}, s32[8]{0:T(128)}, u32[]{:S(2)}) copy-start(s32[8]{0:T(128)} %param.29) | copy-start | bytes 100
  26.7 7.5 %copy-start.28 = (s32[8]{0:T(128)S(1)}, s32[8]{0:T(128)}, u32[]{:S(2)}) copy-start(s32[8]{0:T(128)} %param.31) | copy-start | bytes 100
  26.7 7.8 %copy-start.30 = (s32[32]{0:T(128)S(1)}, s32[32]{0:T(128)}, u32[]{:S(2)}) copy-start(s32[32]{0:T(128)} %param.30) | copy-start | bytes 388
  26.7 137.3 %all-reduce.4.cloned.1.call-start = ((), (), s32[]{:S(2)}) async-start(), calls=%async_computation.6 | async-start | bytes 196608 | tf_op jit(solution)/shard_map/psum | solution.py:57
  27.7 139.5 %all-reduce.6.cloned.1.call-start = ((), (), s32[]{:S(2)}) async-start(), calls=%async_computation.11 | async-start | bytes 360448 | tf_op jit(solution)/shard_map/psum | solution.py:57
  30.9 133.2 %copy-start.10 = (bf16[128,128]{1,0:T(8,128)(2,1)S(1)}, bf16[128,128]{1,0:T(8,128)(2,1)}, u32[]{:S(2)}) copy-start(bf16[128,128]{1,0:T(8,128)(2,1)} %param.22) | copy-start | bytes 98308
  31.7 135.5 %copy-start.15 = (f32[2]{0:T(128)S(1)}, f32[2]{0:T(128)}, u32[]{:S(2)}) copy-start(f32[2]{0:T(128)} %param.24) | copy-start | bytes 28
  31.7 135.5 %copy-start.27 = (f32[2]{0:T(128)S(1)}, f32[2]{0:T(128)}, u32[]{:S(2)}) copy-start(f32[2]{0:T(128)} %param.25) | copy-start | bytes 28
  33.3 160.4 %all-gather.5.cloned.1.call-start = ((), (), s32[]{:S(2)}) async-start(), calls=%async_computation.5 | async-start | bytes 1179648 | tf_op jit(solution)/shard_map/all_gather | solution.py:51
  34.0 236.6 %reduce-scatter.11.cloned.1.call-start = ((), (), s32[]{:S(2)}) async-start(), calls=%async_computation.10 | async-start | bytes 1179648 | tf_op jit(solution)/shard_map/reduce_scatter | solution.py:84
  183.0 5.1 %copy-start.1 = (bf16[8192,256]{0,1:T(8,128)(2,1)S(1)}, bf16[8192,256]{0,1:T(8,128)(2,1)}, u32[]{:S(2)}) copy-start(bf16[8192,256]{0,1:T(8,128)(2,1)} %copy.143) | copy-start | bytes 12582916
  183.0 5.1 %copy-start.9 = (bf16[1,32,8192]{2,1,0:T(8,128)(2,1)S(1)}, bf16[1,32,8192]{2,1,0:T(8,128)(2,1)}, u32[]{:S(2)}) copy-start(bf16[1,32,8192]{2,1,0:T(8,128)(2,1)} %all-gather.1) | copy-start | bytes 1572868
  216.3 6.8 %copy-start.4 = (f32[32,2,64,128]{3,2,1,0:T(8,128)S(1)}, f32[32,2,64,128]{3,2,1,0:T(8,128)}, u32[]{:S(2)}) copy-start(f32[32,2,64,128]{3,2,1,0:T(8,128)} %gather_fusion) | copy-start | bytes 6291460
  216.3 6.8 %copy-start.12 = (f32[32,2,64]{2,1,0:T(2,128)S(1)}, f32[32,2,64]{2,1,0:T(2,128)}, u32[]{:S(2)}) copy-start(f32[32,2,64]{2,1,0:T(2,128)} %copy.159) | copy-start | bytes 49156
  216.3 6.8 %copy-start.18 = (f32[32,2]{1,0:T(8,128)S(1)}, f32[32,2]{1,0:T(8,128)}, u32[]{:S(2)}) copy-start(f32[32,2]{1,0:T(8,128)} %copy.156) | copy-start | bytes 772
  216.3 6.9 %copy-start.23 = (f32[32,128]{1,0:T(8,128)S(1)}, f32[32,128]{1,0:T(8,128)}, u32[]{:S(2)}) copy-start(f32[32,128]{1,0:T(8,128)} %get-tuple-element.174) | copy-start | bytes 49156
  216.3 6.9 %copy-start.24 = (f32[32,128]{1,0:T(8,128)S(1)}, f32[32,128]{1,0:T(8,128)}, u32[]{:S(2)}) copy-start(f32[32,128]{1,0:T(8,128)} %get-tuple-element.175) | copy-start | bytes 49156
  223.2 6.1 %copy-start.13 = (f32[32,2,64]{2,1,0:T(2,128)S(1)}, f32[32,2,64]{2,1,0:T(2,128)}, u32[]{:S(2)}) copy-start(f32[32,2,64]{2,1,0:T(2,128)} %copy.165) | copy-start | bytes 49156
  223.2 6.1 %copy-start.19 = (f32[32,2]{1,0:T(8,128)S(1)}, f32[32,2]{1,0:T(8,128)}, u32[]{:S(2)}) copy-start(f32[32,2]{1,0:T(8,128)} %copy.162) | copy-start | bytes 772
  223.2 6.1 %copy-start.20 = (f32[32,128]{1,0:T(8,128)S(1)}, f32[32,128]{1,0:T(8,128)}, u32[]{:S(2)}) copy-start(f32[32,128]{1,0:T(8,128)} %get-tuple-element.164) | copy-start | bytes 49156
  223.2 6.1 %copy-start.21 = (f32[32,128]{1,0:T(8,128)S(1)}, f32[32,128]{1,0:T(8,128)}, u32[]{:S(2)}) copy-start(f32[32,128]{1,0:T(8,128)} %get-tuple-element.165) | copy-start | bytes 49156
  229.4 7.1 %copy-start.26 = (f32[128]{0:T(128)S(1)}, f32[128]{0:T(128)}, u32[]{:S(2)}) copy-start(f32[128]{0:T(128)} %param.27) | copy-start | bytes 1540
  237.9 65.5 %reduce-scatter.9.cloned.1.call-start = ((), (), s32[]{:S(2)}) async-start(), calls=%async_computation.9 | async-start | bytes 1179648 | tf_op jit(solution)/shard_map/reduce_scatter | solution.py:84
  239.6 96.7 %reduce-scatter.7.cloned.1.call-start = ((), (), s32[]{:S(2)}) async-start(), calls=%async_computation.8 | async-start | bytes 1179648 | tf_op jit(solution)/shard_map/reduce_scatter | solution.py:84
  241.3 131.4 %reduce-scatter.5.cloned.1.call-start = ((), (), s32[]{:S(2)}) async-start(), calls=%async_computation.7 | async-start | bytes 2359296 | tf_op jit(solution)/shard_map/reduce_scatter | solution.py:84
  243.7 129.0 %copy-start.6 = (bf16[64,1024]{1,0:T(8,128)(2,1)S(1)}, bf16[64,1024]{1,0:T(8,128)(2,1)}, u32[]{:S(2)}) copy-start(bf16[64,1024]{1,0:T(8,128)(2,1)} %param.17) | copy-start | bytes 393220
  (7 other events, 20.5 us)
Sparse Core Ops, SparseCore 0:
  30.5 77.7 all-reduce.3
  111.4 55.6 all-reduce.5
  168.8 23.3 all-gather.4
  238.1 32.4 reduce-scatter.10
  272.7 30.6 reduce-scatter.8
  305.6 30.6 reduce-scatter.6
  338.6 34.0 reduce-scatter.4
where the time goes:
time: 382 us; the launch traced here: 381 us
  blocking collectives  141 us (37%)
  waiting for transfers between devices  129 us (34%)
  matrix products  52.2 us (14%)
  local copies, waits for them, and re-layouts  31.4 us (8%)
  between operations  14.6 us (4%)
  starting transfers between devices  6.76 us (2%)
  other arithmetic  6.32 us (2%)
    all_gather x3, blocking collectives, prepare_inputs(): lax.all_gather(token_rows, 'head', axis=1, tiled=True)  129 us
    reduce_scatter x4, waiting for transfers between devices, finish(): lax.psum_scatter(lax.dot_general(output_weight, normed, (((0,), (1,)), ((...  127 us
    dot_general x3, matrix products, on_device(): jnp.einsum('rhpn,rn->rhp', state, read_vector, precision=lax.Precision.HI...  19.6 us
    dot_general x4, matrix products, prepare_inputs(): jnp.dot(lax.all_gather(token_rows, 'head', axis=1, tiled=True), columns,...  13.1 us
    all_to_all x2, local copies, waits for them, and re-layouts, on_device(): lax.all_to_all(input_weight, 'head', split_axis=1, concat_axis=0, tiled=T...  12.9 us
    all_gather x1, blocking collectives, on_device(): gathered = lax.all_gather(finals, 'grp', axis=0, tiled=True)  11.2 us
  transfers between devices with their start and end apart: 8, of which 5 were waited for; matrix products, arithmetic and copies ran while one was open for 11% of the time, Pallas kernels for 0%

commit v1 on v0

v1 whole, which is shorter than its diff:
```python
import jax
import jax.numpy as jnp
from jax import lax
from jax.experimental import pallas as pl
from jax.experimental.pallas import tpu as pltpu
from jax.sharding import PartitionSpec as P

HEAD_CHANNELS = 64
STATE = 128
HEAD_DEV = 2
STRETCH = 32
SAMPLES = 16
STEPS = 3
ADAPTER_RANK = 16
LANES = 128
F32 = jnp.float32
BF16 = jnp.bfloat16
F16 = jnp.float16
EXACT = lax.Precision.HIGHEST
VMEM = pl.BlockSpec(memory_space=pltpu.VMEM)
SMEM = pl.BlockSpec(memory_space=pltpu.SMEM)
BIG = 48 * 1024 * 1024


def mxu(a, b):
    return jnp.dot(a, b, preferred_element_type=F32)


def dot_nt(a, b):
    return lax.dot_general(a, b, (((1,), (1,)), ((), ())), precision=EXACT, preferred_element_type=F32)


def dot_tn(a, b):
    return lax.dot_general(a, b, (((0,), (0,)), ((), ())), precision=EXACT, preferred_element_type=F32)


def lane_ids(rows):
    return lax.broadcasted_iota(jnp.int32, (rows, LANES), 1)


def row_ids(rows, width=1):
    return lax.broadcasted_iota(jnp.int32, (rows, width), 0)


def row_prompts(slots_ref, slots):
    rows = row_ids(slots)
    found = jnp.zeros((slots, 1), jnp.int32)
    for j in range(slots):
        found = jnp.where(rows == j, slots_ref[j] // SAMPLES, found)
    return found


def row_tenants(slots_ref, held_ref, tenants_ref, group, owned, slots):
    prompts = row_prompts(slots_ref, slots)
    decode = jnp.zeros((slots, 1), jnp.int32)
    for p in range(tenants_ref.shape[0]):
        decode = jnp.where(prompts == p, tenants_ref[p], decode)
    prefill = [
        jnp.full((STRETCH, 1), tenants_ref[held_ref[group * owned + i]], jnp.int32) for i in range(owned)
    ]
    return jnp.concatenate(prefill + [decode] * STEPS, axis=0)


def place_order(chips):
    bits = chips.bit_length() - 1
    order = []
    for p in range(chips):
        j = chips - 1 - p
        order.append(sum(((j >> b) & 1) << (bits - 1 - b) for b in range(bits)))
    return order


def project(where, prefill_rows, decode_rows, input_weight, lowrank_weight, step_weight, slots, held, tenants, owned):
    rows_prefill, depth = prefill_rows.shape
    rows = rows_prefill + decode_rows.shape[0]
    width = 2 * HEAD_DEV * HEAD_CHANNELS
    pieces = width // LANES
    chips = input_weight.shape[1] // width // 2
    bits = chips.bit_length() - 1
    low_width = lowrank_weight.shape[1]
    low_blocks = 2 * STATE // LANES + 1
    heads = step_weight.shape[1]
    slot_count = slots.shape[0]

    def column(i, odd, at_ref):
        j = chips - 1 - i
        rev = 0
        for b in range(bits):
            rev = rev + (((j >> b) & 1) << (bits - 1 - b))
        return (rev * 2 + odd) ^ at_ref[0]

    def send_body(at_ref, slots_ref, held_ref, tenants_ref, up_ref, ud_ref, w_ref, l_ref, s_ref, o_ref, u_ref):
        i = pl.program_id(0)

        @pl.when(i == 0)
        def _():
            u_ref[:rows_prefill] = up_ref[...]
            u_ref[rows_prefill:] = ud_ref[...]

        part = mxu(u_ref[...], w_ref[...])
        for k in range(pieces):
            o_ref[i * pieces + k] = part[:, k * LANES : (k + 1) * LANES]

        @pl.when(i == chips - 1)
        def _():
            low = mxu(u_ref[...], l_ref[...])
            base = chips * pieces
            for k in range(low_blocks - 1):
                o_ref[base + k] = low[:, k * LANES : (k + 1) * LANES]
            tenant = row_tenants(slots_ref, held_ref, tenants_ref, at_ref[1], owned, slot_count)
            lanes = lane_ids(rows)
            picked = jnp.where(lanes // ADAPTER_RANK == tenant, low[:, 2 * STATE :], 0.0)
            shift = LANES // 2
            while shift >= ADAPTER_RANK:
                picked = picked + pltpu.roll(picked, shift, 1)
                shift //= 2
            o_ref[base + low_blocks - 1] = picked
            o_ref[base + low_blocks - 1, :, ADAPTER_RANK : ADAPTER_RANK + heads] = mxu(u_ref[...], s_ref[...])

    def keep_body(at_ref, up_ref, ud_ref, w_ref, o_ref, u_ref):
        i = pl.program_id(0)

        @pl.when(i == 0)
        def _():
            u_ref[:rows_prefill] = up_ref[...]
            u_ref[rows_prefill:] = ud_ref[...]

        part = mxu(u_ref[...], w_ref[...])
        for k in range(pieces):
            o_ref[i * pieces + k] = part[:, k * LANES : (k + 1) * LANES]

    def whole(shape):
        return pl.BlockSpec(shape, lambda i, *_: (0,) * len(shape))

    def call(body, odd, prefetch, low, blocks, operands):
        specs = [
            whole(prefill_rows.shape),
            whole(decode_rows.shape),
            pl.BlockSpec((depth, width), lambda i, at_ref, *_: (0, column(i, odd, at_ref))),
        ]
        specs += [whole(lowrank_weight.shape), whole(step_weight.shape)] if low else []
        return pl.pallas_call(
            body,
            out_shape=jax.ShapeDtypeStruct((blocks, rows, LANES), F32),
            grid_spec=pltpu.PrefetchScalarGridSpec(
                num_scalar_prefetch=prefetch,
                grid=(chips,),
                in_specs=specs,
                out_specs=whole((blocks, rows, LANES)),
                scratch_shapes=[pltpu.VMEM((rows, depth), BF16)],
            ),
            compiler_params=pltpu.CompilerParams(vmem_limit_bytes=BIG),
            cost_estimate=pl.CostEstimate(
                flops=2 * rows * depth * width * chips, bytes_accessed=2 * depth * width * chips, transcendentals=0
            ),
        )(*operands)

    send = call(
        send_body, 1, 4, True, chips * pieces + low_blocks,
        (where, slots, held, tenants, prefill_rows, decode_rows, input_weight, lowrank_weight, step_weight),
    )
    keep = call(keep_body, 0, 1, False, chips * pieces, (where, prefill_rows, decode_rows, input_weight))
    return send, keep


def step_lengths(mixed, me, bias_ref):
    lanes = lane_ids(mixed.shape[0])
    lengths = []
    for h in range(HEAD_DEV):
        raw = jnp.sum(jnp.where(lanes == ADAPTER_RANK + me * HEAD_DEV + h, mixed, 0.0), axis=1, keepdims=True)
        raw = raw + bias_ref[h]
        lengths.append(jnp.maximum(raw, 0.0) + jnp.log1p(jnp.exp(-jnp.abs(raw))))
    return lengths


def by_head(first, second, rows):
    return jnp.where(lane_ids(rows) < HEAD_CHANNELS, first, second)


def prefill_decay(lengths, rate_ref, rows):
    t_at = lax.broadcasted_iota(jnp.int32, (rows, rows), 0)
    s_at = lax.broadcasted_iota(jnp.int32, (rows, rows), 1)
    same = t_at // STRETCH == s_at // STRETCH
    columns, lines, steps = [], [], []
    for h in range(HEAD_DEV):
        length = lengths[h][:rows]
        decay = -(length * rate_ref[h])
        line = jnp.sum(jnp.where(same & (t_at <= s_at), decay, 0.0), axis=0, keepdims=True)
        lines.append(line)
        columns.append(jnp.sum(jnp.where(t_at == s_at, line, 0.0), axis=1, keepdims=True))
        steps.append(jnp.sum(jnp.where(t_at == s_at, length, 0.0), axis=0, keepdims=True))
    return columns, lines, steps, same & (t_at >= s_at)


def end_states(where, summed, adapter_up, bias, rate, start, slots, held, tenants):
    rows = summed.shape[1]
    owned = start.shape[0]
    prefill = owned * STRETCH
    slot_count = slots.shape[0]

    def body(at_ref, slots_ref, held_ref, tenants_ref, bias_ref, rate_ref, x_ref, a_ref, s_ref, v_ref, f_ref):
        me, group = at_ref[0], at_ref[1]
        mixed = x_ref[4]
        lanes = lane_ids(rows)
        tenant = row_tenants(slots_ref, held_ref, tenants_ref, group, owned, slot_count)
        picked = jnp.where(lanes < ADAPTER_RANK, mixed, 0.0)
        shift = ADAPTER_RANK
        while shift < LANES:
            picked = picked + pltpu.roll(picked, shift, 1)
            shift *= 2
        picked = jnp.where(lanes // ADAPTER_RANK == tenant, picked, 0.0).astype(BF16)
        values = by_head(x_ref[0], pltpu.roll(x_ref[1], HEAD_CHANNELS, 1), rows)
        values = values + mxu(picked, a_ref[...])
        v_ref[...] = values
        lengths = step_lengths(mixed[:prefill], me, bias_ref)
        columns, _, _, _ = prefill_decay(lengths, rate_ref, prefill)
        for i in range(owned):
            lo, hi = i * STRETCH, (i + 1) * STRETCH
            ends = [columns[h][hi - 1 : hi] for h in range(HEAD_DEV)]
            tails = [jnp.exp(ends[h] - columns[h][lo:hi]) * lengths[h][lo:hi] for h in range(HEAD_DEV)]
            added = dot_tn(by_head(tails[0], tails[1], STRETCH) * values[lo:hi], x_ref[2, lo:hi])
            for h in range(HEAD_DEV):
                at = slice(h * HEAD_CHANNELS, (h + 1) * HEAD_CHANNELS)
                f_ref[i, at] = jnp.exp(ends[h]) * s_ref[i, at] + added[at]

    return pl.pallas_call(
        body,
        out_shape=(
            jax.ShapeDtypeStruct((rows, LANES), F32),
            jax.ShapeDtypeStruct((owned, LANES, STATE), F32),
        ),
        in_specs=[SMEM] * 6 + [VMEM] * 3,
        out_specs=(VMEM, VMEM),
        compiler_params=pltpu.CompilerParams(vmem_limit_bytes=BIG),
    )(where, slots, held, tenants, bias, rate, summed, adapter_up, start)


def normalise(result, gate, scale_ref):
    gated = result * (gate * (1.0 / (1.0 + jnp.exp(-gate))))
    spread = jnp.mean(gated * gated, axis=1, keepdims=True)
    return (gated * lax.rsqrt(spread + 1e-05) * scale_ref[...]).astype(BF16)


def gates(x_ref, at):
    first, second = x_ref[0, at], x_ref[1, at]
    return by_head(pltpu.roll(first, HEAD_CHANNELS, 1), second, first.shape[0])


def rows_within(where, summed, values, start, bias, rate, skip, norm_scale):
    rows = summed.shape[1]
    owned = start.shape[0]
    prefill = owned * STRETCH
    slot_count = (rows - prefill) // STEPS

    def body(at_ref, bias_ref, rate_ref, skip_ref, x_ref, v_ref, s_ref, g_ref, n_ref, y_ref):
        me = at_ref[0]
        lengths = step_lengths(x_ref[4], me, bias_ref)
        columns, lines, steps, later = prefill_decay(lengths, rate_ref, prefill)
        now = slice(0, prefill)
        values = v_ref[now]
        scores = dot_nt(x_ref[3, now], x_ref[2, now])
        sums = []
        for h in range(HEAD_DEV):
            weights = jnp.where(later, jnp.exp(jnp.where(later, columns[h] - lines[h], 0.0)), 0.0) * steps[h]
            sums.append(jnp.dot(weights * scores, values, precision=EXACT, preferred_element_type=F32))
        result = by_head(sums[0], sums[1], prefill)
        carried = jnp.concatenate(
            [dot_nt(x_ref[3, i * STRETCH : (i + 1) * STRETCH], s_ref[i]) for i in range(owned)], axis=0
        )
        kept = by_head(jnp.exp(columns[0]), jnp.exp(columns[1]), prefill)
        skipped = by_head(skip_ref[0], skip_ref[1], prefill)
        result = result + kept * carried + skipped * values
        n_ref[...] = normalise(result, gates(x_ref, now), g_ref)
        at = [slice(prefill + s * slot_count, prefill + (s + 1) * slot_count) for s in range(STEPS)]
        run = [[], []]
        for h in range(HEAD_DEV):
            total = jnp.zeros((slot_count, 1), F32)
            for s in range(STEPS):
                total = total - lengths[h][at[s]] * rate_ref[h]
                run[h].append(total)
        skipped = by_head(skip_ref[0], skip_ref[1], slot_count)
        for s in range(STEPS):
            total = skipped * v_ref[at[s]]
            for u in range(s + 1):
                score = jnp.sum(x_ref[3, at[s]] * x_ref[2, at[u]], axis=1, keepdims=True)
                factor = [jnp.exp(run[h][s] - run[h][u]) * lengths[h][at[u]] * score for h in range(HEAD_DEV)]
                total = total + by_head(factor[0], factor[1], slot_count) * v_ref[at[u]]
            y_ref[s * slot_count : (s + 1) * slot_count] = total

    return pl.pallas_call(
        body,
        out_shape=(
            jax.ShapeDtypeStruct((prefill, LANES), BF16),
            jax.ShapeDtypeStruct((rows - prefill, LANES), F32),
        ),
        in_specs=[SMEM] * 4 + [VMEM] * 4,
        out_specs=(VMEM, VMEM),
        compiler_params=pltpu.CompilerParams(vmem_limit_bytes=BIG),
    )(where, bias, rate, skip, summed, values, start, norm_scale)


def decode_rows_out(where, summed, within, prefill_normed, finals, bias, rate, norm_scale, slots, held):
    rows = summed.shape[1]
    prefill = prefill_normed.shape[0]
    owned = finals[0].shape[0]
    slot_count = slots.shape[0]
    parts = len(finals)

    def body(at_ref, slots_ref, held_ref, bias_ref, rate_ref, x_ref, y_ref, p_ref, g_ref, *rest):
        f_refs, n_ref = rest[:parts], rest[parts]
        me, group = at_ref[0], at_ref[1]
        now = slice(prefill, rows)
        prompts = row_prompts(slots_ref, slot_count)
        prompts = jnp.concatenate([prompts] * STEPS, axis=0)
        reader = x_ref[3, now]
        carried = jnp.zeros((rows - prefill, LANES), F32)
        for j in range(parts):
            for i in range(owned):
                mine = prompts == held_ref[(group ^ j) * owned + i]
                carried = carried + dot_nt(jnp.where(mine, reader, 0.0), f_refs[j][i])
        lengths = step_lengths(x_ref[4, now], me, bias_ref)
        kept = []
        for h in range(HEAD_DEV):
            total = jnp.zeros((slot_count, 1), F32)
            runs = []
            for s in range(STEPS):
                total = total - lengths[h][s * slot_count : (s + 1) * slot_count] * rate_ref[h]
                runs.append(total)
            kept.append(jnp.exp(jnp.concatenate(runs, axis=0)))
        result = y_ref[...] + by_head(kept[0], kept[1], rows - prefill) * carried
        n_ref[:prefill] = p_ref[...]
        n_ref[prefill:] = normalise(result, gates(x_ref, now), g_ref)

    return pl.pallas_call(
        body,
        out_shape=jax.ShapeDtypeStruct((rows, LANES), BF16),
        in_specs=[SMEM] * 5 + [VMEM] * (4 + parts),
        out_specs=VMEM,
        compiler_params=pltpu.CompilerParams(vmem_limit_bytes=BIG),
    )(where, slots, held, bias, rate, summed, within, prefill_normed, norm_scale, *finals)


def output_rows(where, near, far, weights, prefill_rows, decode_rows):
    chips, rows, _ = near.shape
    prefill, width = prefill_rows.shape
    parts = len(weights)
    per_part = chips // parts
    tile = width // 4 if width % 512 == 0 else width

    def body(at_ref, a_ref, b_ref, up_ref, ud_ref, *rest):
        w_refs, (op_ref, od_ref) = rest[:parts], rest[parts:]
        total = jnp.zeros((rows, tile), F32)
        for j in range(parts):
            for k in range(per_part):
                chip = (at_ref[1] ^ j) + parts * k
                pair = jnp.concatenate([a_ref[chip], b_ref[chip]], axis=1)
                total = total + mxu(pair, w_refs[j][k])
        op_ref[...] = up_ref[...].astype(F32) + total[:prefill]
        od_ref[...] = ud_ref[...].astype(F32) + total[prefill:]

    def column(shape):
        return pl.BlockSpec(shape, lambda i, *_: (0,) * (len(shape) - 1) + (i,))

    def whole(shape):
        return pl.BlockSpec(shape, lambda i, *_: (0,) * len(shape))

    return pl.pallas_call(
        body,
        out_shape=(
            jax.ShapeDtypeStruct(prefill_rows.shape, F32),
            jax.ShapeDtypeStruct(decode_rows.shape, F32),
        ),
        grid_spec=pltpu.PrefetchScalarGridSpec(
            num_scalar_prefetch=1,
            grid=(width // tile,),
            in_specs=[
                whole(near.shape),
                whole(far.shape),
                column((prefill, tile)),
                column((rows - prefill, tile)),
            ]
            + [column(w.shape[:-1] + (tile,)) for w in weights],
            out_specs=(column((prefill, tile)), column((rows - prefill, tile))),
        ),
        compiler_params=pltpu.CompilerParams(vmem_limit_bytes=BIG),
    )(where, near, far, prefill_rows, decode_rows, *weights)


def solution(mesh):
    groups, heads = mesh.shape["grp"], mesh.shape["head"]
    chips = heads // 2
    stages = [1 << b for b in range(chips.bit_length() - 1)]
    order = place_order(chips)

    def across(x, distance):
        return lax.ppermute(x, "head", [(i, i ^ distance) for i in range(heads)])

    def over_groups(x, distance):
        return lax.ppermute(x, "grp", [(i, i ^ distance) for i in range(groups)])

    def weight_columns(output_weight, head, group):
        own_rows = output_weight.shape[0]
        width = output_weight.shape[1] // heads
        core = head % 2
        pieces = []
        for k in range(chips // groups):
            target = (head // 2) ^ (group + groups * k)
            piece = lax.dynamic_slice_in_dim(output_weight, target * 2 * width, 2 * width, 1)
            pairs = [
                (g * heads + h, g * heads + (h ^ (2 * (g + groups * k)))) for g in range(groups) for h in range(heads)
            ]
            pieces.append(lax.ppermute(piece, ("grp", "head"), pairs))
        held = jnp.stack(pieces)
        own = lax.dynamic_slice_in_dim(held, core * width, width, 2)
        other = across(lax.dynamic_slice_in_dim(held, (1 - core) * width, width, 2), 1)
        both = jnp.concatenate([own, other], axis=1)
        return [both] + [over_groups(both, j) for j in range(1, groups)]

    def on_device(
        prefill_token_rows,
        decode_token_rows,
        input_weight,
        lowrank_weight,
        step_size_weight,
        adapter_up_weight,
        output_weight,
        head_decay_rate,
        head_step_bias,
        head_skip_scale,
        gated_norm_scale,
        prompt_start_state,
        prompt_at_position,
        slot_sample_index,
        prompt_adapter_index,
    ):
        head, group = lax.axis_index("head"), lax.axis_index("grp")
        where = jnp.stack([head, group]).astype(jnp.int32)
        owned = prompt_start_state.shape[0]
        slots = slot_sample_index.shape[0]
        start = prompt_start_state.reshape(owned, HEAD_DEV * HEAD_CHANNELS, STATE)
        decode_rows = decode_token_rows.reshape(STEPS * slots, decode_token_rows.shape[2])
        norm_scale = gated_norm_scale.reshape(1, HEAD_DEV * HEAD_CHANNELS)
        weights = weight_columns(output_weight, head, group)
        send, keep = project(
            where, prefill_token_rows, decode_rows, input_weight, lowrank_weight, step_size_weight,
            slot_sample_index, prompt_at_position, prompt_adapter_index, owned,
        )
        split = keep.shape[0]
        summed = jnp.concatenate([keep, send[split:]]) + across(send, 1)
        for distance in stages:
            half = split // 2
            outgoing = jnp.concatenate([summed[:half], summed[split:]]).astype(F16)
            summed = summed[half:] + across(outgoing, 2 * distance).astype(F32)
            split = half
        values, finals = end_states(
            where, summed, adapter_up_weight, head_step_bias, head_decay_rate, start,
            slot_sample_index, prompt_at_position, prompt_adapter_index,
        )
        all_finals = [finals] + [over_groups(finals, j) for j in range(1, groups)]
        prefill_normed, within = rows_within(
            where, summed, values, start, head_step_bias, head_decay_rate, head_skip_scale, norm_scale
        )
        normed = decode_rows_out(
            where, summed, within, prefill_normed, all_finals, head_step_bias, head_decay_rate, norm_scale,
            slot_sample_index, prompt_at_position,
        )
        near = normed[None]
        have = [0]
        for distance in reversed(stages):
            near = jnp.concatenate([near, across(near, 2 * distance)])
            have = have + [c ^ distance for c in have]
        near = jnp.concatenate([near[have.index(c)][None] for c in range(chips)])
        far = across(near, 1)
        prefill_out, decode_out = output_rows(where, near, far, weights, prefill_token_rows, decode_rows)
        return prefill_out, decode_out.reshape(decode_token_rows.shape)

    placed = (
        P("grp", "head"),
        P(None, "grp", "head"),
        P("head", None),
        P("head", None),
        P("head", None),
        P(None, "head"),
        P("head", None),
        P("head"),
        P("head"),
        P("head"),
        P("head"),
        P("grp", "head", None, None),
        P(),
        P("grp"),
        P(),
    )
    return jax.shard_map(
        on_device,
        mesh=mesh,
        in_specs=placed,
        out_specs=(P("grp", "head"), P(None, "grp", "head")),
        check_vma=False,
    )
```

time: 382 us -> 101 us (0.26)
  blocking collectives: 141 us -> 0 us
  waiting for transfers between devices: 129 us -> 38.5 us
  matrix products: 52.2 us -> 0 us
  starting transfers between devices: 6.76 us -> 36 us
  local copies, waits for them, and re-layouts: 31.4 us -> 8.16 us
  Pallas kernels: 0 us -> 14 us
  between operations: 14.6 us -> 0.94 us
    all_gather x4 -> x0, blocking collectives: 141 us -> none  [the longest x3 129 us: prepare_inputs(): lax.all_gather(token_rows, 'head', axis=1, tiled=True)]
    reduce_scatter x4 -> x0, waiting for transfers between devices: 127 us -> none  [finish(): lax.psum_scatter(lax.dot_general(output_weight, normed, (((0,), (1,)), ((...]
    dot_general x31 -> x0, matrix products: 52.2 us -> none  [the longest x3 19.6 us: on_device(): jnp.einsum('rhpn,rn->rhp', state, read_vector, precision=lax.Precision.HI...]
    ppermute x0 -> x14, waiting for transfers between devices: none -> 38.5 us  [the longest x6 22.5 us: over_groups(): return lax.ppermute(x, 'grp', [(i, i ^ distance) for i in range(groups)])]
    ppermute x0 -> x14, starting transfers between devices: none -> 36 us  [the longest x6 24 us: over_groups(): return lax.ppermute(x, 'grp', [(i, i ^ distance) for i in range(groups)])]
    pallas_call x0 -> x6, Pallas kernels: none -> 14 us  [the longest x2 6.37 us: call(): pl.pallas_call(body, out_shape=jax.ShapeDtypeStruct((blocks, rows, LANES)...]
    all_to_all x2 -> x0, local copies, waits for them, and re-layouts: 12.9 us -> none  [on_device(): lax.all_to_all(input_weight, 'head', split_axis=1, concat_axis=0, tiled=T...]
    all_to_all x1 -> x0, starting transfers between devices: 6.47 us -> none  [on_device(): lax.all_to_all(input_weight, 'head', split_axis=1, concat_axis=0, tiled=T...]
  transfers between devices with their start and end apart: 8 -> 14, of which waited for: 5 -> 9; matrix products, arithmetic and copies ran while one was open for 11% -> 4% of each run, Pallas kernels for 0% -> 7%
where the time goes in v1:
time: 101 us
  waiting for transfers between devices  38.5 us (38%)
  starting transfers between devices  36 us (36%)
  Pallas kernels  14 us (14%)
  local copies, waits for them, and re-layouts  8.16 us (8%)
  other arithmetic  3.11 us (3%)
    ppermute x6, starting transfers between devices, over_groups(): return lax.ppermute(x, 'grp', [(i, i ^ distance) for i in range(groups)])  24 us
    ppermute x6, waiting for transfers between devices, over_groups(): return lax.ppermute(x, 'grp', [(i, i ^ distance) for i in range(groups)])  22.5 us
    ppermute x7, waiting for transfers between devices, across(): return lax.ppermute(x, 'head', [(i, i ^ distance) for i in range(heads)])  16 us
    ppermute x7, starting transfers between devices, across(): return lax.ppermute(x, 'head', [(i, i ^ distance) for i in range(heads)])  6.7 us
    pallas_call x2, Pallas kernels, call(): pl.pallas_call(body, out_shape=jax.ShapeDtypeStruct((blocks, rows, LANES)...  6.37 us
    unnamed x39, local copies, waits for them, and re-layouts  6.07 us
    ppermute x1, starting transfers between devices, weight_columns(): pieces.append(lax.ppermute(piece, ('grp', 'head'), pairs))  5.37 us
    pallas_call x1, Pallas kernels, output_rows(): pl.pallas_call(body, out_shape=(jax.ShapeDtypeStruct(prefill_rows.shape,...  2.96 us
  transfers between devices with their start and end apart: 14, of which 9 were waited for; matrix products, arithmetic and copies ran while one was open for 4% of the time, Pallas kernels for 7%

profile of v1, /device:TPU:0, one launch (start us, length us, event | category | flops | bytes accessed | tf_op | source)
XLA Modules:
  0.0 100.7 jit_solution(8050579400612639022)
XLA Ops:
  0.7 1.1 %copy.17.s_ref = bf16[1024,16]{1,0:T(8,128)(2,1)S(1)} copy(bf16[1024,16]{0,1:T(8,128)(2,1)} %param.19) | data formatting | bytes 65536 | tf_op args[4]
  1.8 0.9 copy-done.2
  2.7 0.9 copy-done.4
  3.6 1.1 %copy-done.6 = bf16[1024,384]{1,0:T(8,128)(2,1)S(1)} copy-done((bf16[1024,384]{1,0:T(8,128)(2,1)S(1)}, bf16[1024,384]{1,0:T(8,128)(2,1)}, u32[]{:S(2)}) %copy-start.6) | copy-done | bytes 786456
  6.7 4.4 %shard_map.159 = f32[11,160,128]{2,1,0:T(8,128)S(1)} custom-call(s32[2]{0:T(128)S(1)} %pad_add_fusion.at_ref, s32[32]{0:T(128)S(1)} %copy-done.9, s32[8]{0:T(128)S(1)} %copy-done.11, s32[8]{0:T(128)S(1)} %copy-done.16, bf16[64,1024]{1,0:T(8,128)(2,1)S(1)} %copy-done.4, bf16[96,1024]{1,0:T(8,128)(2,1)S(1)} %bitcast.11, bf16[1024,2048]{1,0:T(8,128)(2,1)} %w_ref.3, ...), custom_call_target="tpu_custom_call" | custom-call | flops 335544320 | bytes 2097152 | tf_op jit(solution)/shard_map/pallas_call | solution.py:142
  11.7 2.0 %shard_map.158 = f32[8,160,128]{2,1,0:T(8,128)S(1)} custom-call(s32[2]{0:T(128)S(1)} %pad_add_fusion.at_ref, bf16[64,1024]{1,0:T(8,128)(2,1)S(1)} %copy-done.4, bf16[96,1024]{1,0:T(8,128)(2,1)S(1)} %bitcast.12, bf16[1024,2048]{1,0:T(8,128)(2,1)S(1)} %copy-done.1), custom_call_target="tpu_custom_call" | custom-call | flops 335544320 | bytes 2097152 | tf_op jit(solution)/shard_map/pallas_call | solution.py:142
  14.0 0.8 pad_maximum_fusion.1
  14.8 2.9 %collective-permute-start.1 = (f16[7,160,128]{2,1,0:T(8,128)(2,1)}, f16[7,160,128]{2,1,0:T(8,128)(2,1)S(1)}, u32[]{:S(2)}, u32[]{:S(2)}) collective-permute-start(f16[7,160,128]{2,1,0:T(8,128)(2,1)} %pad_maximum_fusion.1), channel_id=1, source_target_pairs={{0,2},{1,3},{2,0},{3,1},{4,6},{5,7},{6,4},{7,5},{8,10},{9,11},{10,... | collective-permute-start | bytes 860168 | tf_op jit(solution)/shard_map/ppermute | solution.py:396
  17.8 0.9 constant_dynamic-slice_fusion
  18.6 5.4 %collective-permute-start.9 = (bf16[128,2048]{1,0:T(8,128)(2,1)}, bf16[128,2048]{1,0:T(8,128)(2,1)}, u32[]{:S(2)}, u32[]{:S(2)}) collective-permute-start(bf16[128,2048]{1,0:T(8,128)(2,1)} %constant_dynamic-slice_fusion), channel_id=1, source_target_pairs={{0,0},{1,1},{2,2},{3,3},{4,4},{5,5},{6,6},{7,7},{8,10},{9,11},{10,... | collective-permute-start | bytes 1572872 | tf_op jit(solution)/shard_map/ppermute | solution.py:412
  24.0 1.0 %collective-permute-done.1 = f16[7,160,128]{2,1,0:T(8,128)(2,1)S(1)} collective-permute-done((f16[7,160,128]{2,1,0:T(8,128)(2,1)}, f16[7,160,128]{2,1,0:T(8,128)(2,1)S(1)}, u32[]{:S(2)}, u32[]{:S(2)}) %collective-permute-start.1) | collective-permute-done | bytes 286752 | tf_op jit(solution)/shard_map/ppermute | solution.py:396
  25.0 0.9 fusion
  26.1 2.8 %collective-permute-start.2 = (f16[5,160,128]{2,1,0:T(8,128)(2,1)S(1)}, f16[5,160,128]{2,1,0:T(8,128)(2,1)S(1)}, u32[]{:S(2)}, u32[]{:S(2)}) collective-permute-start(f16[5,160,128]{2,1,0:T(8,128)(2,1)S(1)} %pad_maximum_fusion.2), channel_id=1, source_target_pairs={{0,4},{1,5},{2,6},{3,7},{4,0},{5,1},{6,2},{7,3},{8,12},{9,13},{10,... | collective-permute-start | bytes 614408 | tf_op jit(solution)/shard_map/ppermute | solution.py:396
  28.9 9.1 %collective-permute-done.2 = f16[5,160,128]{2,1,0:T(8,128)(2,1)S(1)} collective-permute-done((f16[5,160,128]{2,1,0:T(8,128)(2,1)S(1)}, f16[5,160,128]{2,1,0:T(8,128)(2,1)S(1)}, u32[]{:S(2)}, u32[]{:S(2)}) %collective-permute-start.2) | collective-permute-done | bytes 204832 | tf_op jit(solution)/shard_map/ppermute | solution.py:396
  38.0 1.1 %slice_add_fusion.1.x_ref = f32[5,160,128]{2,1,0:T(8,128)S(1)} fusion(f32[7,160,128]{2,1,0:T(8,128)} %get-tuple-element.15, f16[5,160,128]{2,1,0:T(8,128)(2,1)S(1)} %collective-permute-done.2), kind=kLoop, calls=%fused_computation.3 | loop fusion | flops 204800 | bytes 1024000 | tf_op jit(solution)/shard_map/add | solution.py:453
  39.2 1.4 %shard_map.160 = (f32[160,128]{1,0:T(8,128)S(1)}, f32[2,128,128]{2,1,0:T(8,128)S(1)}) custom-call(s32[2]{0:T(128)S(1)} %pad_add_fusion.at_ref, s32[32]{0:T(128)S(1)} %copy-done.10, s32[8]{0:T(128)S(1)} %copy-done.12, s32[8]{0:T(128)S(1)} %copy-done.17, f32[2]{0:T(128)S(1)} %copy-done.13, f32[2]{0:T(128)S(1)} %copy-done.14, ...), custom_call_target="tpu_custom_call" | custom-call | tf_op jit(solution)/shard_map/pallas_call | solution.py:226
  40.6 3.4 %collective-permute-start.3 = (f32[2,128,128]{2,1,0:T(8,128)S(1)}, f32[2,128,128]{2,1,0:T(8,128)S(1)}, u32[]{:S(2)}, u32[]{:S(2)}) collective-permute-start(f32[2,128,128]{2,1,0:T(8,128)S(1)} %get-tuple-element.11.rest_0_), channel_id=1, source_target_pairs={{0,8},{8,0},{16,24},{24,16},{1,9},{9,1},{17,25},{25,17},{2,10},{10... | collective-permute-start | bytes 393224 | tf_op jit(solution)/shard_map/ppermute | solution.py:399
  44.0 16.9 %collective-permute-start.4 = (f32[2,128,128]{2,1,0:T(8,128)S(1)}, f32[2,128,128]{2,1,0:T(8,128)S(1)}, u32[]{:S(2)}, u32[]{:S(2)}) collective-permute-start(f32[2,128,128]{2,1,0:T(8,128)S(1)} %get-tuple-element.11.rest_0_), channel_id=1, source_target_pairs={{0,16},{8,24},{16,0},{24,8},{1,17},{9,25},{17,1},{25,9},{2,18},{10... | collective-permute-start | bytes 393224 | tf_op jit(solution)/shard_map/ppermute | solution.py:399
  61.0 1.1 %dynamic-slice_bitcast_fusion.1 = (bf16[1,128,1024]{2,1,0:T(8,128)(2,1)S(1)}, bf16[1,128,1024]{2,1,0:T(8,128)(2,1)S(1)}) fusion(bf16[128,2048]{1,0:T(8,128)(2,1)} %collective-permute-done.9, s32[]{:T(128)S(6)} %select_n.23, s32[]{:T(128)S(6)} %select_n.24), kind=kLoop, calls=%fused_computation.6 | loop fusion | bytes 1048584 | tf_op jit(solution)/shard_map/dynamic_slice | solution.py:414
  62.2 1.3 %shard_map.161 = (bf16[64,128]{1,0:T(8,128)(2,1)S(1)}, f32[96,128]{1,0:T(8,128)S(1)}) custom-call(s32[2]{0:T(128)S(1)} %pad_add_fusion.at_ref, f32[2]{0:T(128)S(1)} %copy-done.13, f32[2]{0:T(128)S(1)} %copy-done.14, f32[2]{0:T(128)S(1)} %copy-done.18, f32[5,160,128]{2,1,0:T(8,128)S(1)} %slice_add_fusion.1.x_ref, f32[160,128]{1,0:T(8,128)S(1)} %get-tuple-element.8.v_ref, ...), custom_call_target="tpu_custom_call" | custom-call | tf_op jit(solution)/shard_map/pallas_call | solution.py:290
  63.5 2.2 %collective-permute-done.4.rest_2_ = f32[2,128,128]{2,1,0:T(8,128)S(1)} collective-permute-done((f32[2,128,128]{2,1,0:T(8,128)S(1)}, f32[2,128,128]{2,1,0:T(8,128)S(1)}, u32[]{:S(2)}, u32[]{:S(2)}) %collective-permute-start.4) | collective-permute-done | bytes 131104 | tf_op jit(solution)/shard_map/ppermute | solution.py:399
  65.7 1.1 %collective-permute-done.5.rest_3_ = f32[2,128,128]{2,1,0:T(8,128)S(1)} collective-permute-done((f32[2,128,128]{2,1,0:T(8,128)S(1)}, f32[2,128,128]{2,1,0:T(8,128)S(1)}, u32[]{:S(2)}, u32[]{:S(2)}) %collective-permute-start.5) | collective-permute-done | bytes 131104 | tf_op jit(solution)/shard_map/ppermute | solution.py:399
  66.8 2.0 %shard_map.162 = bf16[160,128]{1,0:T(8,128)(2,1)S(1)} custom-call(s32[2]{0:T(128)S(1)} %pad_add_fusion.at_ref, s32[32]{0:T(128)S(1)} %copy-done.10, s32[8]{0:T(128)S(1)} %copy-done.12, f32[2]{0:T(128)S(1)} %copy-done.13, f32[2]{0:T(128)S(1)} %copy-done.14, f32[5,160,128]{2,1,0:T(8,128)S(1)} %slice_add_fusion.1.x_ref, f32[96,128]{1,0:T(8,128)S(1)} %get-tuple-element.9.y_ref, ...), custom_call_target="tpu_custom_call" | custom-call | tf_op jit(solution)/shard_map/pallas_call | solution.py:334
  68.9 5.0 %collective-permute-done.6 = bf16[1,160,128]{2,1,0:T(8,128)(2,1)S(1)} collective-permute-done((bf16[1,160,128]{2,1,0:T(8,128)(2,1)S(1)}, bf16[1,160,128]{2,1,0:T(8,128)(2,1)S(1)}, u32[]{:S(2)}, u32[]{:S(2)}) %collective-permute-start.6) | collective-permute-done | bytes 40992 | tf_op jit(solution)/shard_map/ppermute | solution.py:396
  74.2 0.9 collective-permute-start.11
  75.1 0.7 collective-permute-start.12
  75.8 1.9 %collective-permute-start.13 = (bf16[1,256,1024]{2,1,0:T(8,128)(2,1)S(1)}, bf16[1,256,1024]{2,1,0:T(8,128)(2,1)S(1)}, u32[]{:S(2)}, u32[]{:S(2)}) collective-permute-start(bf16[1,256,1024]{2,1,0:T(8,128)(2,1)S(1)} %pad_maximum_fusion.rest_0_), channel_id=1, source_target_pairs={{0,24},{8,16},{16,8},{24,0},{1,25},{9,17},{17,9},{25,1},{2,26},{10... | collective-permute-start | bytes 1572872 | tf_op jit(solution)/shard_map/ppermute | solution.py:399
  77.7 0.7 collective-permute-done.7
  78.5 10.6 %collective-permute-done.11.rest_1_ = bf16[1,256,1024]{2,1,0:T(8,128)(2,1)S(1)} collective-permute-done((bf16[1,256,1024]{2,1,0:T(8,128)(2,1)S(1)}, bf16[1,256,1024]{2,1,0:T(8,128)(2,1)S(1)}, u32[]{:S(2)}, u32[]{:S(2)}) %collective-permute-start.11) | collective-permute-done | bytes 524320 | tf_op jit(solution)/shard_map/ppermute | solution.py:399
  89.1 7.1 %collective-permute-done.12.rest_2_ = bf16[1,256,1024]{2,1,0:T(8,128)(2,1)S(1)} collective-permute-done((bf16[1,256,1024]{2,1,0:T(8,128)(2,1)S(1)}, bf16[1,256,1024]{2,1,0:T(8,128)(2,1)S(1)}, u32[]{:S(2)}, u32[]{:S(2)}) %collective-permute-start.12) | collective-permute-done | bytes 524320 | tf_op jit(solution)/shard_map/ppermute | solution.py:399
  96.2 1.5 %collective-permute-done.13.rest_3_ = bf16[1,256,1024]{2,1,0:T(8,128)(2,1)S(1)} collective-permute-done((bf16[1,256,1024]{2,1,0:T(8,128)(2,1)S(1)}, bf16[1,256,1024]{2,1,0:T(8,128)(2,1)S(1)}, u32[]{:S(2)}, u32[]{:S(2)}) %collective-permute-start.13) | collective-permute-done | bytes 524320 | tf_op jit(solution)/shard_map/ppermute | solution.py:399
  97.8 3.0 %shard_map.163 = (f32[64,1024]{1,0:T(8,128)}, f32[96,1024]{1,0:T(8,128)}) custom-call(s32[2]{0:T(128)S(1)} %pad_add_fusion.at_ref, bf16[4,160,128]{2,1,0:T(8,128)(2,1)S(1)} %pad_maximum_fusion.3.a_ref, bf16[4,160,128]{2,1,0:T(8,128)(2,1)S(1)} %collective-permute-done.8.b_ref, bf16[64,1024]{1,0:T(8,128)(2,1)S(1)} %copy-done.5, bf16[96,1024]{1,0:T(8,128)(2,1)S(1)} %bitcast.13, ...), custom_call_target="tpu_custom_call" | custom-call | tf_op jit(solution)/shard_map/pallas_call | solution.py:367
  (58 shorter events, 3.6 us)
Async XLA Ops:
  0.6 17.1 %copy-start = (bf16[128,8192]{1,0:T(8,128)(2,1)S(1)}, bf16[128,8192]{1,0:T(8,128)(2,1)}, u32[]{:S(2)}) copy-start(bf16[128,8192]{1,0:T(8,128)(2,1)} %param.21) | copy-start | bytes 6291460
  1.8 0.9 copy-start.2
  2.7 0.9 copy-start.4
  3.6 1.1 %copy-start.6 = (bf16[1024,384]{1,0:T(8,128)(2,1)S(1)}, bf16[1024,384]{1,0:T(8,128)(2,1)}, u32[]{:S(2)}) copy-start(bf16[1024,384]{1,0:T(8,128)(2,1)} %l_ref.1) | copy-start | bytes 2359300
  4.8 0.7 copy-start.9
  5.4 0.7 copy-start.11
  6.7 4.9 %copy-start.1 = (bf16[1024,2048]{1,0:T(8,128)(2,1)S(1)}, bf16[1024,2048]{1,0:T(8,128)(2,1)}, u32[]{:S(2)}) copy-start(bf16[1024,2048]{1,0:T(8,128)(2,1)} %w_ref.3) | copy-start | bytes 12582916
  11.1 2.6 %collective-permute-start = (f32[11,160,128]{2,1,0:T(8,128)S(1)}, f32[11,160,128]{2,1,0:T(8,128)S(1)}, u32[]{:S(2)}, u32[]{:S(2)}) collective-permute-start(f32[11,160,128]{2,1,0:T(8,128)S(1)} %shard_map.159), channel_id=1, source_target_pairs={{0,1},{1,0},{2,3},{3,2},{4,5},{5,4},{6,7},{7,6},{8,9},{9,8},{10,11... | collective-permute-start | bytes 2703368 | tf_op jit(solution)/shard_map/ppermute | solution.py:396
  14.8 10.3 %collective-permute-start.1 = (f16[7,160,128]{2,1,0:T(8,128)(2,1)}, f16[7,160,128]{2,1,0:T(8,128)(2,1)S(1)}, u32[]{:S(2)}, u32[]{:S(2)}) collective-permute-start(f16[7,160,128]{2,1,0:T(8,128)(2,1)} %pad_maximum_fusion.1), channel_id=1, source_target_pairs={{0,2},{1,3},{2,0},{3,1},{4,6},{5,7},{6,4},{7,5},{8,10},{9,11},{10,... | collective-permute-start | bytes 860168 | tf_op jit(solution)/shard_map/ppermute | solution.py:396
  17.7 21.4 %copy-start.7 = (f32[2,2,64,128]{3,2,1,0:T(8,128)S(1)}, f32[2,2,64,128]{3,2,1,0:T(8,128)}, u32[]{:S(2)}) copy-start(f32[2,2,64,128]{3,2,1,0:T(8,128)} %param.26) | copy-start | bytes 393220
  17.7 21.4 %copy-start.8 = (bf16[128,128]{1,0:T(8,128)(2,1)S(1)}, bf16[128,128]{1,0:T(8,128)(2,1)}, u32[]{:S(2)}) copy-start(bf16[128,128]{1,0:T(8,128)(2,1)} %a_ref.1) | copy-start | bytes 98308
  17.7 21.4 %copy-start.10 = (s32[32]{0:T(128)S(1)}, s32[32]{0:T(128)}, u32[]{:S(2)}) copy-start(s32[32]{0:T(128)} %slots_ref.5) | copy-start | bytes 388
  17.7 21.4 %copy-start.12 = (s32[8]{0:T(128)S(1)}, s32[8]{0:T(128)}, u32[]{:S(2)}) copy-start(s32[8]{0:T(128)} %held_ref.5) | copy-start | bytes 100
  17.7 21.4 %copy-start.13 = (f32[2]{0:T(128)S(1)}, f32[2]{0:T(128)}, u32[]{:S(2)}) copy-start(f32[2]{0:T(128)} %bias_ref.5) | copy-start | bytes 28
  17.7 21.4 %copy-start.14 = (f32[2]{0:T(128)S(1)}, f32[2]{0:T(128)}, u32[]{:S(2)}) copy-start(f32[2]{0:T(128)} %rate_ref.5) | copy-start | bytes 28
  17.7 21.4 %copy-start.17 = (s32[8]{0:T(128)S(1)}, s32[8]{0:T(128)}, u32[]{:S(2)}) copy-start(s32[8]{0:T(128)} %tenants_ref.3) | copy-start | bytes 100
  18.6 42.3 %collective-permute-start.9 = (bf16[128,2048]{1,0:T(8,128)(2,1)}, bf16[128,2048]{1,0:T(8,128)(2,1)}, u32[]{:S(2)}, u32[]{:S(2)}) collective-permute-start(bf16[128,2048]{1,0:T(8,128)(2,1)} %constant_dynamic-slice_fusion), channel_id=1, source_target_pairs={{0,0},{1,1},{2,2},{3,3},{4,4},{5,5},{6,6},{7,7},{8,10},{9,11},{10,... | collective-permute-start | bytes 1572872 | tf_op jit(solution)/shard_map/ppermute | solution.py:412
  25.9 36.2 %copy-start.15 = (f32[128]{0:T(128)S(1)}, f32[128]{0:T(128)}, u32[]{:S(2)}) copy-start(f32[128]{0:T(128)} %param.25) | copy-start | bytes 1540
  25.9 36.2 %copy-start.18 = (f32[2]{0:T(128)S(1)}, f32[2]{0:T(128)}, u32[]{:S(2)}) copy-start(f32[2]{0:T(128)} %skip_ref.1) | copy-start | bytes 28
  26.1 12.0 %collective-permute-start.2 = (f16[5,160,128]{2,1,0:T(8,128)(2,1)S(1)}, f16[5,160,128]{2,1,0:T(8,128)(2,1)S(1)}, u32[]{:S(2)}, u32[]{:S(2)}) collective-permute-start(f16[5,160,128]{2,1,0:T(8,128)(2,1)S(1)} %pad_maximum_fusion.2), channel_id=1, source_target_pairs={{0,4},{1,5},{2,6},{3,7},{4,0},{5,1},{6,2},{7,3},{8,12},{9,13},{10,... | collective-permute-start | bytes 614408 | tf_op jit(solution)/shard_map/ppermute | solution.py:396
  40.6 57.2 %copy-start.3 = (bf16[3,32,1024]{2,1,0:T(8,128)(2,1)S(1)}, bf16[3,32,1024]{2,1,0:T(8,128)(2,1)}, u32[]{:S(2)}) copy-start(bf16[3,32,1024]{2,1,0:T(8,128)(2,1)} %param.16) | copy-start | bytes 589828
  40.6 57.2 %copy-start.5 = (bf16[64,1024]{1,0:T(8,128)(2,1)S(1)}, bf16[64,1024]{1,0:T(8,128)(2,1)}, u32[]{:S(2)}) copy-start(bf16[64,1024]{1,0:T(8,128)(2,1)} %up_ref.5) | copy-start | bytes 393220
  40.6 22.9 %collective-permute-start.3 = (f32[2,128,128]{2,1,0:T(8,128)S(1)}, f32[2,128,128]{2,1,0:T(8,128)S(1)}, u32[]{:S(2)}, u32[]{:S(2)}) collective-permute-start(f32[2,128,128]{2,1,0:T(8,128)S(1)} %get-tuple-element.11.rest_0_), channel_id=1, source_target_pairs={{0,8},{8,0},{16,24},{24,16},{1,9},{9,1},{17,25},{25,17},{2,10},{10... | collective-permute-start | bytes 393224 | tf_op jit(solution)/shard_map/ppermute | solution.py:399
  44.0 21.6 %collective-permute-start.4 = (f32[2,128,128]{2,1,0:T(8,128)S(1)}, f32[2,128,128]{2,1,0:T(8,128)S(1)}, u32[]{:S(2)}, u32[]{:S(2)}) collective-permute-start(f32[2,128,128]{2,1,0:T(8,128)S(1)} %get-tuple-element.11.rest_0_), channel_id=1, source_target_pairs={{0,16},{8,24},{16,0},{24,8},{1,17},{9,25},{17,1},{25,9},{2,18},{10... | collective-permute-start | bytes 393224 | tf_op jit(solution)/shard_map/ppermute | solution.py:399
  60.9 5.9 %collective-permute-start.5 = (f32[2,128,128]{2,1,0:T(8,128)S(1)}, f32[2,128,128]{2,1,0:T(8,128)S(1)}, u32[]{:S(2)}, u32[]{:S(2)}) collective-permute-start(f32[2,128,128]{2,1,0:T(8,128)S(1)} %get-tuple-element.11.rest_0_), channel_id=1, source_target_pairs={{0,24},{8,16},{16,8},{24,0},{1,25},{9,17},{17,9},{25,1},{2,26},{10... | collective-permute-start | bytes 393224 | tf_op jit(solution)/shard_map/ppermute | solution.py:399
  62.1 12.1 %collective-permute-start.10 = (bf16[1,128,1024]{2,1,0:T(8,128)(2,1)S(1)}, bf16[1,128,1024]{2,1,0:T(8,128)(2,1)S(1)}, u32[]{:S(2)}, u32[]{:S(2)}) collective-permute-start(bf16[1,128,1024]{2,1,0:T(8,128)(2,1)S(1)} %get-tuple-element.19), channel_id=1, source_target_pairs={{0,1},{1,0},{2,3},{3,2},{4,5},{5,4},{6,7},{7,6},{8,9},{9,8},{10,11... | collective-permute-start | bytes 786440 | tf_op jit(solution)/shard_map/ppermute | solution.py:396
  68.8 5.1 %collective-permute-start.6 = (bf16[1,160,128]{2,1,0:T(8,128)(2,1)S(1)}, bf16[1,160,128]{2,1,0:T(8,128)(2,1)S(1)}, u32[]{:S(2)}, u32[]{:S(2)}) collective-permute-start(bf16[1,160,128]{2,1,0:T(8,128)(2,1)S(1)} %bitcast.16), channel_id=1, source_target_pairs={{0,4},{1,5},{2,6},{3,7},{4,0},{5,1},{6,2},{7,3},{8,12},{9,13},{10,... | collective-permute-start | bytes 122888 | tf_op jit(solution)/shard_map/ppermute | solution.py:396
  73.9 4.5 %collective-permute-start.7 = (bf16[2,160,128]{2,1,0:T(8,128)(2,1)S(1)}, bf16[2,160,128]{2,1,0:T(8,128)(2,1)S(1)}, u32[]{:S(2)}, u32[]{:S(2)}) collective-permute-start(bf16[2,160,128]{2,1,0:T(8,128)(2,1)S(1)} %pad_maximum_fusion.4), channel_id=1, source_target_pairs={{0,2},{1,3},{2,0},{3,1},{4,6},{5,7},{6,4},{7,5},{8,10},{9,11},{10,... | collective-permute-start | bytes 245768 | tf_op jit(solution)/shard_map/ppermute | solution.py:396
  74.2 14.9 %collective-permute-start.11 = (bf16[1,256,1024]{2,1,0:T(8,128)(2,1)S(1)}, bf16[1,256,1024]{2,1,0:T(8,128)(2,1)S(1)}, u32[]{:S(2)}, u32[]{:S(2)}) collective-permute-start(bf16[1,256,1024]{2,1,0:T(8,128)(2,1)S(1)} %pad_maximum_fusion.rest_0_), channel_id=1, source_target_pairs={{0,8},{8,0},{16,24},{24,16},{1,9},{9,1},{17,25},{25,17},{2,10},{10... | collective-permute-start | bytes 1572872 | tf_op jit(solution)/shard_map/ppermute | solution.py:399
  75.1 21.1 %collective-permute-start.12 = (bf16[1,256,1024]{2,1,0:T(8,128)(2,1)S(1)}, bf16[1,256,1024]{2,1,0:T(8,128)(2,1)S(1)}, u32[]{:S(2)}, u32[]{:S(2)}) collective-permute-start(bf16[1,256,1024]{2,1,0:T(8,128)(2,1)S(1)} %pad_maximum_fusion.rest_0_), channel_id=1, source_target_pairs={{0,16},{8,24},{16,0},{24,8},{1,17},{9,25},{17,1},{25,9},{2,18},{10... | collective-permute-start | bytes 1572872 | tf_op jit(solution)/shard_map/ppermute | solution.py:399
  75.8 22.0 %collective-permute-start.13 = (bf16[1,256,1024]{2,1,0:T(8,128)(2,1)S(1)}, bf16[1,256,1024]{2,1,0:T(8,128)(2,1)S(1)}, u32[]{:S(2)}, u32[]{:S(2)}) collective-permute-start(bf16[1,256,1024]{2,1,0:T(8,128)(2,1)S(1)} %pad_maximum_fusion.rest_0_), channel_id=1, source_target_pairs={{0,24},{8,16},{16,8},{24,0},{1,25},{9,17},{17,9},{25,1},{2,26},{10... | collective-permute-start | bytes 1572872 | tf_op jit(solution)/shard_map/ppermute | solution.py:399
  78.5 19.3 %collective-permute-start.8 = (bf16[4,160,128]{2,1,0:T(8,128)(2,1)S(1)}, bf16[4,160,128]{2,1,0:T(8,128)(2,1)S(1)}, u32[]{:S(2)}, u32[]{:S(2)}) collective-permute-start(bf16[4,160,128]{2,1,0:T(8,128)(2,1)S(1)} %pad_maximum_fusion.3.a_ref), channel_id=1, source_target_pairs={{0,1},{1,0},{2,3},{3,2},{4,5},{5,4},{6,7},{7,6},{8,9},{9,8},{10,11... | collective-permute-start | bytes 491528 | tf_op jit(solution)/shard_map/ppermute | solution.py:396
  (1 other events, 0.7 us)

commit v2 on v1

v2 whole, which is shorter than its diff:
```python
import itertools

import jax
import jax.numpy as jnp
from jax import lax
from jax.experimental import pallas as pl
from jax.experimental.pallas import tpu as pltpu
from jax.sharding import PartitionSpec as P

HEAD_CHANNELS = 64
STATE = 128
HEAD_DEV = 2
STRETCH = 32
SAMPLES = 16
STEPS = 3
ADAPTER_RANK = 16
LANES = 128
F32 = jnp.float32
BF16 = jnp.bfloat16
F16 = jnp.float16
EXACT = lax.Precision.HIGHEST
VMEM = pl.BlockSpec(memory_space=pltpu.VMEM)
BIG = 24 * 1024 * 1024


def mxu(a, b):
    return jnp.dot(a, b, preferred_element_type=F32)


def in_hbm(x):
    return pltpu.with_memory_space_constraint(x, pltpu.HBM)


def dot_nt(a, b):
    return lax.dot_general(a, b, (((1,), (1,)), ((), ())), precision=EXACT, preferred_element_type=F32)


def dot_tn(a, b):
    return lax.dot_general(a, b, (((0,), (0,)), ((), ())), precision=EXACT, preferred_element_type=F32)


def lane_ids(rows):
    return lax.broadcasted_iota(jnp.int32, (rows, LANES), 1)


def row_ids(rows, width=1):
    return lax.broadcasted_iota(jnp.int32, (rows, width), 0)


def as_row(ref):
    return ref[...].reshape(1, ref.shape[0])


def entry(row, at):
    lanes = lax.broadcasted_iota(jnp.int32, row.shape, 1)
    return jnp.sum(jnp.where(lanes == at, row, 0.0), axis=1, keepdims=True)


def numbers(ref):
    return as_row(ref).astype(F32)


def row_prompts(slots_ref, slots):
    row = (as_row(slots_ref) // SAMPLES).astype(F32)
    return jnp.sum(jnp.where(row_ids(slots, slots) == lax.broadcasted_iota(jnp.int32, (slots, slots), 1), row, 0.0), axis=1, keepdims=True)


def row_tenants(slots_ref, held_ref, tenants_ref, group, owned, slots):
    prompts = row_prompts(slots_ref, slots)
    tenants, held = numbers(tenants_ref), numbers(held_ref)
    lanes = lax.broadcasted_iota(jnp.int32, tenants.shape, 1).astype(F32)
    decode = jnp.sum(jnp.where(lanes == prompts, tenants, 0.0), axis=1, keepdims=True)
    prefill = []
    for i in range(owned):
        prompt = entry(held, group * owned + i)
        tenant = jnp.sum(jnp.where(lanes == prompt, tenants, 0.0), axis=1, keepdims=True)
        prefill.append(jnp.broadcast_to(tenant, (STRETCH, 1)))
    return jnp.concatenate(prefill + [decode] * STEPS, axis=0)


def tenant_lanes(rows):
    return (lane_ids(rows) // ADAPTER_RANK).astype(F32)


def place_order(chips):
    bits = chips.bit_length() - 1
    order = []
    for p in range(chips):
        j = chips - 1 - p
        order.append(sum(((j >> b) & 1) << (bits - 1 - b) for b in range(bits)))
    return order


def packing(rows, heads):
    lanes = ADAPTER_RANK + heads
    pack = 1
    while 2 * pack * lanes <= LANES and rows % (2 * pack * 8) == 0:
        pack *= 2
    return pack


def pack_rows(mixed, pack):
    part, span = mixed.shape[0] // pack, LANES // pack
    total = mixed[:part]
    for q in range(1, pack):
        total = total + pltpu.roll(mixed[q * part : (q + 1) * part], q * span, 1)
    return total


def unpack_rows(packed, pack):
    span = LANES // pack
    parts = [packed] + [pltpu.roll(packed, LANES - q * span, 1) for q in range(1, pack)]
    return jnp.concatenate(parts, axis=0)


def project(prefill_rows, decode_rows, input_weight, lowrank_weight, step_lines, slots, held, tenants, owned):
    rows_prefill, depth = prefill_rows.shape
    rows = rows_prefill + decode_rows.shape[0]
    width = 2 * HEAD_DEV * HEAD_CHANNELS
    pieces = width // LANES
    chips = input_weight.shape[1] // width // 2
    order = place_order(chips)
    low_blocks = 2 * STATE // LANES
    heads = step_lines.shape[0]
    pack = packing(rows, heads)
    packed = rows // pack
    base = chips * pieces * rows
    total = base + low_blocks * rows + packed
    slot_count = slots.shape[0]

    def fetches(up_ref, ud_ref, w_ref, u_ref, w_all, sems, odd):
        me = lax.axis_index("head")
        copies = [
            pltpu.make_async_copy(up_ref, u_ref.at[:rows_prefill], sems.at[0]),
            pltpu.make_async_copy(ud_ref, u_ref.at[rows_prefill:], sems.at[1]),
        ]
        for i in range(chips):
            column = pl.multiple_of(((order[i] * 2 + odd) ^ me) * width, width)
            copies.append(pltpu.make_async_copy(w_ref.at[:, pl.ds(column, width)], w_all.at[i], sems.at[2 + i]))
        return copies

    def products(copies, u_ref, w_all, o_ref):
        for i in range(chips):
            copies[2 + i].wait()
            part = mxu(u_ref[...], w_all[i])
            for k in range(pieces):
                at = (i * pieces + k) * rows
                o_ref[at : at + rows] = part[:, k * LANES : (k + 1) * LANES]

    def send_body(
        slots_hbm, held_hbm, tenants_hbm, up_ref, ud_ref, w_ref, l_ref, s_ref, o_ref,
        u_ref, w_all, l_all, s_all, m_ref, slots_ref, held_ref, tenants_ref, sems,
    ):
        copies = fetches(up_ref, ud_ref, w_ref, u_ref, w_all, sems, 1)
        low_copies = [
            pltpu.make_async_copy(l_ref, l_all, sems.at[2 + chips]),
            pltpu.make_async_copy(s_ref, s_all, sems.at[3 + chips]),
        ]
        index_copies = [
            pltpu.make_async_copy(slots_hbm, slots_ref, sems.at[4 + chips]),
            pltpu.make_async_copy(held_hbm, held_ref, sems.at[5 + chips]),
            pltpu.make_async_copy(tenants_hbm, tenants_ref, sems.at[6 + chips]),
        ]
        for copy in index_copies + copies[:2] + low_copies + copies[2:]:
            copy.start()
        for copy in index_copies:
            copy.wait()
        lanes = tenant_lanes(rows)
        mine = lanes == row_tenants(slots_ref, held_ref, tenants_ref, lax.axis_index("grp"), owned, slot_count)
        for copy in copies[:2] + low_copies:
            copy.wait()
        low = mxu(u_ref[...], l_all[...])
        for k in range(low_blocks):
            o_ref[base + k * rows : base + (k + 1) * rows] = low[:, k * LANES : (k + 1) * LANES]
        picked = jnp.where(mine, low[:, 2 * STATE :], 0.0)
        shift = LANES // 2
        while shift >= ADAPTER_RANK:
            picked = picked + pltpu.roll(picked, shift, 1)
            shift //= 2
        m_ref[...] = jnp.where(lane_ids(rows) < ADAPTER_RANK, picked, 0.0)
        m_ref[:, ADAPTER_RANK : ADAPTER_RANK + heads] = lax.dot_general(
            u_ref[...], s_all[...], (((1,), (1,)), ((), ())), preferred_element_type=F32
        )
        o_ref[base + low_blocks * rows :] = pack_rows(m_ref[...], pack)
        products(copies, u_ref, w_all, o_ref)

    def keep_body(up_ref, ud_ref, w_ref, o_ref, u_ref, w_all, sems):
        copies = fetches(up_ref, ud_ref, w_ref, u_ref, w_all, sems, 0)
        for copy in copies:
            copy.start()
        for copy in copies[:2]:
            copy.wait()
        products(copies, u_ref, w_all, o_ref)

    hbm = pl.BlockSpec(memory_space=pltpu.HBM)
    scratch = [pltpu.VMEM((rows, depth), BF16), pltpu.VMEM((chips, depth, width), BF16)]
    cost = pl.CostEstimate(
        flops=2 * rows * depth * width * chips, bytes_accessed=2 * depth * width * chips, transcendentals=0
    )
    params = pltpu.CompilerParams(vmem_limit_bytes=BIG)
    send = pl.pallas_call(
        send_body,
        out_shape=jax.ShapeDtypeStruct((total, LANES), F32),
        in_specs=[hbm] * 8,
        out_specs=VMEM,
        scratch_shapes=scratch
        + [
            pltpu.VMEM(lowrank_weight.shape, BF16),
            pltpu.VMEM(step_lines.shape, BF16),
            pltpu.VMEM((rows, LANES), F32),
            pltpu.VMEM(slots.shape, jnp.int32),
            pltpu.VMEM(held.shape, jnp.int32),
            pltpu.VMEM(tenants.shape, jnp.int32),
            pltpu.SemaphoreType.DMA((chips + 7,)),
        ],
        compiler_params=params,
        cost_estimate=cost,
    )(
        *[
            in_hbm(x)
            for x in (slots, held, tenants, prefill_rows, decode_rows, input_weight, lowrank_weight, step_lines)
        ]
    )
    keep = pl.pallas_call(
        keep_body,
        out_shape=jax.ShapeDtypeStruct((base, LANES), F32),
        in_specs=[hbm] * 3,
        out_specs=VMEM,
        scratch_shapes=scratch + [pltpu.SemaphoreType.DMA((chips + 2,))],
        compiler_params=params,
        cost_estimate=cost,
    )(*[in_hbm(x) for x in (prefill_rows, decode_rows, input_weight)])
    return send, keep


def line_load(route):
    steps = [0] * (2 * len(route))
    for a, b in enumerate(route):
        for link in range(min(a, b), max(a, b)):
            steps[2 * link + (a < b)] += 1
    return max(steps)


def chip_routes(chips, groups):
    wanted = [tuple(z ^ shift for z in range(chips)) for shift in range(chips)]
    if chips <= 4:
        ranked = sorted(itertools.permutations(range(chips)), key=lambda route: (line_load(route), route))

        def fill(rows, most):
            if len(rows) == chips:
                return rows
            for route in ranked:
                if line_load(route) <= most and all(a != b for row in rows for a, b in zip(row, route)):
                    found = fill(rows + [route], most)
                    if found:
                        return found
            return None

        for most in range(chips + 1):
            found = fill([], most)
            if found:
                wanted = found
                break
    return [wanted[groups * k : groups * (k + 1)] for k in range(chips // groups)]


def piece(x_ref, k, rows, at=slice(None)):
    low, high, _ = at.indices(rows)
    return x_ref[k * rows + low : k * rows + high]


def mixed_rows(x_ref, rows):
    return unpack_rows(x_ref[4 * rows :], rows // (x_ref.shape[0] - 4 * rows))


def looked_up(table, group, chip):
    found = jnp.int32(0)
    for g, row in enumerate(table):
        for z, value in enumerate(row):
            found = jnp.where((group == g) & (chip == z), value, found)
    return found


def weight_pieces(output_weight, routes, heads):
    own_rows, all_width = output_weight.shape
    width = all_width // heads
    count = len(routes)

    def body(w_ref, o_ref, sems):
        group, head = lax.axis_index("grp"), lax.axis_index("head")
        copies = []
        for k, rows in enumerate(routes):
            target = looked_up(rows, group, head // 2)
            for side in range(2):
                column = pl.multiple_of((2 * target + ((head % 2) ^ side)) * width, width)
                copies.append(
                    pltpu.make_async_copy(w_ref.at[:, pl.ds(column, width)], o_ref.at[k, side], sems.at[2 * k + side])
                )
        for copy in copies:
            copy.start()
        for copy in copies:
            copy.wait()

    return pl.pallas_call(
        body,
        out_shape=jax.ShapeDtypeStruct((count, 2, own_rows, width), BF16),
        in_specs=[pl.BlockSpec(memory_space=pltpu.HBM)],
        out_specs=VMEM,
        scratch_shapes=[pltpu.SemaphoreType.DMA((2 * count,))],
        compiler_params=pltpu.CompilerParams(vmem_limit_bytes=BIG),
    )(in_hbm(output_weight))


def step_lengths(mixed, bias_ref):
    lanes = lane_ids(mixed.shape[0])
    me = lax.axis_index("head")
    bias = as_row(bias_ref)
    lengths = []
    for h in range(HEAD_DEV):
        raw = jnp.sum(jnp.where(lanes == ADAPTER_RANK + me * HEAD_DEV + h, mixed, 0.0), axis=1, keepdims=True)
        raw = raw + bias[:, h : h + 1]
        lengths.append(jnp.maximum(raw, 0.0) + jnp.log1p(jnp.exp(-jnp.abs(raw))))
    return lengths


def by_head(first, second, rows):
    return jnp.where(lane_ids(rows) < HEAD_CHANNELS, first, second)


def prefill_decay(lengths, rate_ref, rows):
    t_at = lax.broadcasted_iota(jnp.int32, (rows, rows), 0)
    s_at = lax.broadcasted_iota(jnp.int32, (rows, rows), 1)
    same = t_at // STRETCH == s_at // STRETCH
    columns, lines, steps = [], [], []
    rate = as_row(rate_ref)
    for h in range(HEAD_DEV):
        length = lengths[h][:rows]
        decay = -(length * rate[:, h : h + 1])
        line = jnp.sum(jnp.where(same & (t_at <= s_at), decay, 0.0), axis=0, keepdims=True)
        lines.append(line)
        columns.append(jnp.sum(jnp.where(t_at == s_at, line, 0.0), axis=1, keepdims=True))
        steps.append(jnp.sum(jnp.where(t_at == s_at, length, 0.0), axis=0, keepdims=True))
    return columns, lines, steps, same & (t_at >= s_at)


def end_states(rows, summed, adapter_up, bias, rate, start, slots, held, tenants):
    owned = start.shape[0]
    prefill = owned * STRETCH
    slot_count = slots.shape[0]

    def body(slots_ref, held_ref, tenants_ref, bias_ref, rate_ref, x_ref, a_ref, s_ref, v_ref, f_ref):
        group = lax.axis_index("grp")
        mixed = mixed_rows(x_ref, rows)
        lanes = lane_ids(rows)
        mine = tenant_lanes(rows) == row_tenants(slots_ref, held_ref, tenants_ref, group, owned, slot_count)
        picked = jnp.where(lanes < ADAPTER_RANK, mixed, 0.0)
        shift = ADAPTER_RANK
        while shift < LANES:
            picked = picked + pltpu.roll(picked, shift, 1)
            shift *= 2
        picked = jnp.where(mine, picked, 0.0).astype(BF16)
        values = by_head(piece(x_ref, 0, rows), pltpu.roll(piece(x_ref, 1, rows), HEAD_CHANNELS, 1), rows)
        values = values + mxu(picked, a_ref[...])
        v_ref[...] = values
        lengths = step_lengths(mixed[:prefill], bias_ref)
        columns, _, _, _ = prefill_decay(lengths, rate_ref, prefill)
        for i in range(owned):
            lo, hi = i * STRETCH, (i + 1) * STRETCH
            ends = [columns[h][hi - 1 : hi] for h in range(HEAD_DEV)]
            tails = [jnp.exp(ends[h] - columns[h][lo:hi]) * lengths[h][lo:hi] for h in range(HEAD_DEV)]
            added = dot_tn(by_head(tails[0], tails[1], STRETCH) * values[lo:hi], piece(x_ref, 2, rows, slice(lo, hi)))
            for h in range(HEAD_DEV):
                at = slice(h * HEAD_CHANNELS, (h + 1) * HEAD_CHANNELS)
                f_ref[i, at] = jnp.exp(ends[h]) * s_ref[i, at] + added[at]

    return pl.pallas_call(
        body,
        out_shape=(
            jax.ShapeDtypeStruct((rows, LANES), F32),
            jax.ShapeDtypeStruct((owned, LANES, STATE), F32),
        ),
        in_specs=[VMEM] * 8,
        out_specs=(VMEM, VMEM),
        compiler_params=pltpu.CompilerParams(vmem_limit_bytes=BIG),
    )(slots, held, tenants, bias, rate, summed, adapter_up, start)


def normalise(result, gate, scale_ref):
    gated = result * (gate * (1.0 / (1.0 + jnp.exp(-gate))))
    spread = jnp.mean(gated * gated, axis=1, keepdims=True)
    return (gated * lax.rsqrt(spread + 1e-05) * scale_ref[...]).astype(BF16)


def gates(x_ref, rows, at):
    first, second = piece(x_ref, 0, rows, at), piece(x_ref, 1, rows, at)
    return by_head(pltpu.roll(first, HEAD_CHANNELS, 1), second, first.shape[0])


def rows_within(summed, values, start, bias, rate, skip, norm_scale):
    rows = values.shape[0]
    owned = start.shape[0]
    prefill = owned * STRETCH
    slot_count = (rows - prefill) // STEPS

    def body(bias_ref, rate_ref, skip_ref, x_ref, v_ref, s_ref, g_ref, n_ref, y_ref):
        rate, skip = as_row(rate_ref), as_row(skip_ref)
        lengths = step_lengths(mixed_rows(x_ref, rows), bias_ref)
        columns, lines, steps, later = prefill_decay(lengths, rate_ref, prefill)
        now = slice(0, prefill)
        values = v_ref[now]
        scores = dot_nt(piece(x_ref, 3, rows, now), piece(x_ref, 2, rows, now))
        sums = []
        for h in range(HEAD_DEV):
            weights = jnp.where(later, jnp.exp(jnp.where(later, columns[h] - lines[h], 0.0)), 0.0) * steps[h]
            sums.append(jnp.dot(weights * scores, values, precision=EXACT, preferred_element_type=F32))
        result = by_head(sums[0], sums[1], prefill)
        carried = jnp.concatenate(
            [dot_nt(piece(x_ref, 3, rows, slice(i * STRETCH, (i + 1) * STRETCH)), s_ref[i]) for i in range(owned)], axis=0
        )
        kept = by_head(jnp.exp(columns[0]), jnp.exp(columns[1]), prefill)
        skipped = by_head(skip[:, :1], skip[:, 1:], prefill)
        result = result + kept * carried + skipped * values
        n_ref[...] = normalise(result, gates(x_ref, rows, now), g_ref)
        at = [slice(prefill + s * slot_count, prefill + (s + 1) * slot_count) for s in range(STEPS)]
        run = [[], []]
        for h in range(HEAD_DEV):
            total = jnp.zeros((slot_count, 1), F32)
            for s in range(STEPS):
                total = total - lengths[h][at[s]] * rate[:, h : h + 1]
                run[h].append(total)
        skipped = by_head(skip[:, :1], skip[:, 1:], slot_count)
        for s in range(STEPS):
            total = skipped * v_ref[at[s]]
            for u in range(s + 1):
                score = jnp.sum(piece(x_ref, 3, rows, at[s]) * piece(x_ref, 2, rows, at[u]), axis=1, keepdims=True)
                factor = [jnp.exp(run[h][s] - run[h][u]) * lengths[h][at[u]] * score for h in range(HEAD_DEV)]
                total = total + by_head(factor[0], factor[1], slot_count) * v_ref[at[u]]
            y_ref[s * slot_count : (s + 1) * slot_count] = total

    return pl.pallas_call(
        body,
        out_shape=(
            jax.ShapeDtypeStruct((prefill, LANES), BF16),
            jax.ShapeDtypeStruct((rows - prefill, LANES), F32),
        ),
        in_specs=[VMEM] * 7,
        out_specs=(VMEM, VMEM),
        compiler_params=pltpu.CompilerParams(vmem_limit_bytes=BIG),
    )(bias, rate, skip, summed, values, start, norm_scale)


def decode_rows_out(summed, within, prefill_normed, finals, bias, rate, norm_scale, slots, held):
    prefill = prefill_normed.shape[0]
    rows = prefill + within.shape[0]
    owned = finals[0].shape[0]
    slot_count = slots.shape[0]
    parts = len(finals)

    def body(slots_ref, held_ref, bias_ref, rate_ref, x_ref, y_ref, p_ref, g_ref, *rest):
        f_refs, n_ref = rest[:parts], rest[parts]
        group = lax.axis_index("grp")
        held, rate = numbers(held_ref), as_row(rate_ref)
        now = slice(prefill, rows)
        prompts = row_prompts(slots_ref, slot_count)
        prompts = jnp.concatenate([prompts] * STEPS, axis=0)
        reader = piece(x_ref, 3, rows, now)
        carried = jnp.zeros((rows - prefill, LANES), F32)
        for j in range(parts):
            for i in range(owned):
                mine = prompts == entry(held, (group ^ j) * owned + i)
                carried = carried + dot_nt(jnp.where(mine, reader, 0.0), f_refs[j][i])
        lengths = step_lengths(mixed_rows(x_ref, rows)[now], bias_ref)
        kept = []
        for h in range(HEAD_DEV):
            total = jnp.zeros((slot_count, 1), F32)
            runs = []
            for s in range(STEPS):
                total = total - lengths[h][s * slot_count : (s + 1) * slot_count] * rate[:, h : h + 1]
                runs.append(total)
            kept.append(jnp.exp(jnp.concatenate(runs, axis=0)))
        result = y_ref[...] + by_head(kept[0], kept[1], rows - prefill) * carried
        n_ref[:prefill] = p_ref[...]
        n_ref[prefill:] = normalise(result, gates(x_ref, rows, now), g_ref)

    return pl.pallas_call(
        body,
        out_shape=jax.ShapeDtypeStruct((rows, LANES), BF16),
        in_specs=[VMEM] * (8 + parts),
        out_specs=VMEM,
        compiler_params=pltpu.CompilerParams(vmem_limit_bytes=BIG),
    )(slots, held, bias, rate, summed, within, prefill_normed, norm_scale, *finals)


def output_rows(sources, near, far, weights, prefill_rows, decode_rows):
    chips, rows, _ = near.shape
    prefill, width = prefill_rows.shape
    parts = len(weights)
    per_part = chips // parts
    tile = width // 4 if width % 512 == 0 else width
    flat = [w for part in weights for w in part]

    def body(a_ref, b_ref, up_ref, ud_ref, *rest):
        w_refs, (op_ref, od_ref) = list(rest[: len(flat)]), rest[len(flat) :]
        total = jnp.zeros((rows, tile), F32)
        for j in range(parts):
            mine = [w_refs.pop(0) for _ in weights[j]]
            for k in range(per_part):
                chip = looked_up(sources[k], lax.axis_index("grp") ^ j, lax.axis_index("head") // 2)
                if len(mine) == 1:
                    pair = jnp.concatenate([a_ref[chip], b_ref[chip]], axis=1)
                    total = total + mxu(pair, mine[0][k].reshape(pair.shape[1], tile))
                else:
                    total = total + mxu(a_ref[chip], mine[0][k]) + mxu(b_ref[chip], mine[1][k])
        op_ref[...] = up_ref[...].astype(F32) + total[:prefill]
        od_ref[...] = ud_ref[...].astype(F32) + total[prefill:]

    def column(shape):
        return pl.BlockSpec(shape, lambda i, *_: (0,) * (len(shape) - 1) + (i,))

    def whole(shape):
        return pl.BlockSpec(shape, lambda i, *_: (0,) * len(shape))

    return pl.pallas_call(
        body,
        out_shape=(
            jax.ShapeDtypeStruct(prefill_rows.shape, F32),
            jax.ShapeDtypeStruct(decode_rows.shape, F32),
        ),
        grid=(width // tile,),
        in_specs=[whole(near.shape), whole(far.shape), column((prefill, tile)), column((rows - prefill, tile))]
        + [column(w.shape[:-1] + (tile,)) for w in flat],
        out_specs=(column((prefill, tile)), column((rows - prefill, tile))),
        compiler_params=pltpu.CompilerParams(vmem_limit_bytes=BIG),
    )(near, far, prefill_rows, decode_rows, *flat)


def solution(mesh):
    groups, heads = mesh.shape["grp"], mesh.shape["head"]
    chips = heads // 2
    stages = [1 << b for b in range(chips.bit_length() - 1)]

    def across(x, distance):
        return lax.ppermute(x, "head", [(i, i ^ distance) for i in range(heads)])

    def over_groups(x, distance):
        return lax.ppermute(x, "grp", [(i, i ^ distance) for i in range(groups)])

    routes = chip_routes(chips, groups)

    def weights_over_head(output_weight):
        pieces = weight_pieces(output_weight, routes, heads)
        parts = []
        for k, rows in enumerate(routes):
            pairs = [
                (g * heads + h, g * heads + 2 * rows[g][h // 2] + h % 2) for g in range(groups) for h in range(heads)
            ]
            parts.append(lax.ppermute(pieces[k], ("grp", "head"), pairs))
        return parts

    def weights_over_groups(parts):
        both = jnp.stack([piece.at[1].set(across(piece[1], 1)) for piece in parts])
        if groups != 4:
            return [(both,)] + [(over_groups(both, j),) for j in range(1, groups)]
        near, side = over_groups(both, 1), over_groups(both, 2)
        return [(both,), (near,), (side,), (over_groups(side[:, 0], 1), over_groups(near[:, 1], 2))]

    sources = [[[z ^ row.index(z) for z in range(chips)] for row in rows] for rows in routes]

    def on_device(
        prefill_token_rows,
        decode_token_rows,
        input_weight,
        lowrank_weight,
        step_size_weight,
        adapter_up_weight,
        output_weight,
        head_decay_rate,
        head_step_bias,
        head_skip_scale,
        gated_norm_scale,
        prompt_start_state,
        prompt_at_position,
        slot_sample_index,
        prompt_adapter_index,
    ):
        owned = prompt_start_state.shape[0]
        slots = slot_sample_index.shape[0]
        start = prompt_start_state.reshape(owned, HEAD_DEV * HEAD_CHANNELS, STATE)
        decode_rows = decode_token_rows.reshape(STEPS * slots, decode_token_rows.shape[2])
        norm_scale = gated_norm_scale.reshape(1, HEAD_DEV * HEAD_CHANNELS)
        parts = weights_over_head(output_weight)
        send, keep = project(
            prefill_token_rows, decode_rows, input_weight, lowrank_weight, step_size_weight.T,
            slot_sample_index, prompt_at_position, prompt_adapter_index, owned,
        )
        rows = prefill_token_rows.shape[0] + decode_rows.shape[0]
        split = keep.shape[0]
        summed = jnp.concatenate([keep, send[split:]]) + across(send, 1)
        for distance in stages:
            half = split // 2
            outgoing = jnp.concatenate([summed[:half], summed[split:]]).astype(F16)
            summed = summed[half:] + across(outgoing, 2 * distance).astype(F32)
            split = half
        weights = weights_over_groups(parts)
        values, finals = end_states(
            rows, summed, adapter_up_weight, head_step_bias, head_decay_rate, start,
            slot_sample_index, prompt_at_position, prompt_adapter_index,
        )
        all_finals = [finals] + [over_groups(finals, j) for j in range(1, groups)]
        prefill_normed, within = rows_within(
            summed, values, start, head_step_bias, head_decay_rate, head_skip_scale, norm_scale
        )
        normed = decode_rows_out(
            summed, within, prefill_normed, all_finals, head_step_bias, head_decay_rate, norm_scale,
            slot_sample_index, prompt_at_position,
        )
        near = normed[None]
        have = [0]
        for distance in reversed(stages):
            near = jnp.concatenate([near, across(near, 2 * distance)])
            have = have + [c ^ distance for c in have]
        near = jnp.concatenate([near[have.index(c)][None] for c in range(chips)])
        far = across(near, 1)
        prefill_out, decode_out = output_rows(sources, near, far, weights, prefill_token_rows, decode_rows)
        return prefill_out, decode_out.reshape(decode_token_rows.shape)

    placed = (
        P("grp", "head"),
        P(None, "grp", "head"),
        P("head", None),
        P("head", None),
        P("head", None),
        P(None, "head"),
        P("head", None),
        P("head"),
        P("head"),
        P("head"),
        P("head"),
        P("grp", "head", None, None),
        P(),
        P("grp"),
        P(),
    )
    return jax.shard_map(
        on_device,
        mesh=mesh,
        in_specs=placed,
        out_specs=(P("grp", "head"), P(None, "grp", "head")),
        check_vma=False,
    )
```

time: 101 us -> 70.7 us (0.70)
  waiting for transfers between devices: 38.5 us -> 18.8 us
  local copies, waits for them, and re-layouts: 8.16 us -> 0.26 us
  other arithmetic: 3.11 us -> 0.4 us
  starting transfers between devices: 36 us -> 37.3 us
  Pallas kernels: 14 us -> 12.8 us
    ppermute x6 -> x7, waiting for transfers between devices: 22.5 us -> 9.65 us  [over_groups(): return lax.ppermute(x, 'grp', [(i, i ^ distance) for i in range(groups)])]
    ppermute x7, starting transfers between devices: 6.7 us -> 14.2 us  [across(): return lax.ppermute(x, 'head', [(i, i ^ distance) for i in range(heads)])]
    ppermute x7, waiting for transfers between devices: 16 us -> 9.17 us  [across(): return lax.ppermute(x, 'head', [(i, i ^ distance) for i in range(heads)])]
    unnamed x39 -> x22, local copies, waits for them, and re-layouts: 6.07 us -> 0.07 us
    ppermute x1, starting transfers between devices: 5.37 us -> 0.69 us  [weights_over_head(): parts.append(lax.ppermute(pieces[k], ('grp', 'head'), pairs))]
    dynamic_slice x2 -> x0, local copies, waits for them, and re-layouts: 1.95 us -> none  [the longest x1 1.06 us: weight_columns(): own = lax.dynamic_slice_in_dim(held, core * width, width, 2)]
    ppermute x6 -> x7, starting transfers between devices: 24 us -> 22.4 us  [over_groups(): return lax.ppermute(x, 'grp', [(i, i ^ distance) for i in range(groups)])]
    pallas_call x2 -> x3, Pallas kernels: 6.37 us -> 7.02 us  [the longest x1 3.44 us: project(): pl.pallas_call(send_body, out_shape=jax.ShapeDtypeStruct((total, LANES),...]
  transfers between devices with their start and end apart: 14 -> 15, of which waited for: 9 -> 6; matrix products, arithmetic and copies ran while one was open for 4% -> 1% of each run, Pallas kernels for 7% -> 10%
where the time goes in v2:
time: 70.7 us; the launch traced here: 70.5 us
  starting transfers between devices  37.3 us (53%)
  waiting for transfers between devices  18.8 us (27%)
  Pallas kernels  12.8 us (18%)
  between operations  0.97 us (1%)
    ppermute x7, starting transfers between devices, over_groups(): return lax.ppermute(x, 'grp', [(i, i ^ distance) for i in range(groups)])  22.4 us
    ppermute x7, starting transfers between devices, across(): return lax.ppermute(x, 'head', [(i, i ^ distance) for i in range(heads)])  14.2 us
    ppermute x7, waiting for transfers between devices, over_groups(): return lax.ppermute(x, 'grp', [(i, i ^ distance) for i in range(groups)])  9.65 us
    ppermute x7, waiting for transfers between devices, across(): return lax.ppermute(x, 'head', [(i, i ^ distance) for i in range(heads)])  9.17 us
    pallas_call x1, Pallas kernels, project(): pl.pallas_call(send_body, out_shape=jax.ShapeDtypeStruct((total, LANES),...  3.44 us
    pallas_call x1, Pallas kernels, output_rows(): pl.pallas_call(body, out_shape=(jax.ShapeDtypeStruct(prefill_rows.shape,...  2.56 us
    pallas_call x1, Pallas kernels, project(): pl.pallas_call(keep_body, out_shape=jax.ShapeDtypeStruct((base, LANES), F...  2.54 us
  transfers between devices with their start and end apart: 15, of which 6 were waited for; matrix products, arithmetic and copies ran while one was open for 1% of the time, Pallas kernels for 10%

profile of v2, /device:TPU:0, one launch (start us, length us, event | category | flops | bytes accessed | tf_op | source)
XLA Modules:
  0.0 70.5 jit_solution(6558678823448758254)
XLA Ops:
  0.6 3.4 %shard_map.159 = f32[1640,128]{1,0:T(8,128)S(1)} custom-call(s32[32]{0:T(128)} %slots_ref.3, s32[8]{0:T(128)} %held_ref.3, s32[8]{0:T(128)} %tenants_ref.1, bf16[64,1024]{1,0:T(8,128)(2,1)} %up_ref.5, bf16[96,1024]{1,0:T(8,128)(2,1)} %bitcast.16, bf16[1024,2048]{1,0:T(8,128)(2,1)} %w_ref.4, bf16[1024,384]{1,0:T(8,128)(2,1)} %l_ref.1, bf16[16,1024]{1,0:T(8,128)(2,1)} %bitcast.28), custom_call_target="tpu_custom_call" | custom-call | flops 335544320 | bytes 2097152 | tf_op jit(solution)/shard_map/pallas_call | solution.py:201
  4.1 0.5 collective-permute-start
  4.6 1.0 %shard_map.163 = bf16[1,2,128,1024]{3,2,1,0:T(8,128)(2,1)S(1)} custom-call(bf16[128,8192]{1,0:T(8,128)(2,1)} %w_ref.5), custom_call_target="tpu_custom_call" | custom-call | tf_op jit(solution)/shard_map/pallas_call | solution.py:304
  5.6 0.7 collective-permute-start.9
  6.4 2.5 %shard_map.158 = f32[1280,128]{1,0:T(8,128)S(1)} custom-call(bf16[64,1024]{1,0:T(8,128)(2,1)} %up_ref.5, bf16[96,1024]{1,0:T(8,128)(2,1)} %bitcast.17, bf16[1024,2048]{1,0:T(8,128)(2,1)} %w_ref.4), custom_call_target="tpu_custom_call" | custom-call | flops 335544320 | bytes 2097152 | tf_op jit(solution)/shard_map/pallas_call | solution.py:224
  9.0 0.1 fusion.1
  9.3 0.1 pad_maximum_fusion
  9.3 5.5 %collective-permute-start.1 = (f16[1000,128]{1,0:T(8,128)(2,1)S(1)}, f16[1000,128]{1,0:T(8,128)(2,1)S(1)}, u32[]{:S(2)}, u32[]{:S(2)}) collective-permute-start(f16[1000,128]{1,0:T(8,128)(2,1)S(1)} %pad_maximum_fusion), channel_id=1, source_target_pairs={{0,2},{1,3},{2,0},{3,1},{4,6},{5,7},{6,4},{7,5},{8,10},{9,11},{10,... | collective-permute-start | bytes 768008 | tf_op jit(solution)/shard_map/ppermute | solution.py:543
  14.8 0.1 collective-permute-start.10
  14.9 6.4 %collective-permute-done.1 = f16[1000,128]{1,0:T(8,128)(2,1)S(1)} collective-permute-done((f16[1000,128]{1,0:T(8,128)(2,1)S(1)}, f16[1000,128]{1,0:T(8,128)(2,1)S(1)}, u32[]{:S(2)}, u32[]{:S(2)}) %collective-permute-start.1) | collective-permute-done | bytes 256032 | tf_op jit(solution)/shard_map/ppermute | solution.py:543
  21.3 0.1 fusion
  21.5 0.1 pad_maximum_fusion.1
  21.5 4.3 %collective-permute-start.2 = (f16[680,128]{1,0:T(8,128)(2,1)S(1)}, f16[680,128]{1,0:T(8,128)(2,1)S(1)}, u32[]{:S(2)}, u32[]{:S(2)}) collective-permute-start(f16[680,128]{1,0:T(8,128)(2,1)S(1)} %pad_maximum_fusion.1), channel_id=1, source_target_pairs={{0,4},{1,5},{2,6},{3,7},{4,0},{5,1},{6,2},{7,3},{8,12},{9,13},{10,... | collective-permute-start | bytes 522248 | tf_op jit(solution)/shard_map/ppermute | solution.py:543
  25.9 6.8 %collective-permute-start.12 = (bf16[1,2,128,1024]{3,2,1,0:T(8,128)(2,1)S(1)}, bf16[1,2,128,1024]{3,2,1,0:T(8,128)(2,1)S(1)}, u32[]{:S(2)}, u32[]{:S(2)}) collective-permute-start(bf16[1,2,128,1024]{3,2,1,0:T(8,128)(2,1)S(1)} %bitcast_dynamic-update-slice_fusion.rest_0_), channel_id=1, source_target_pairs={{0,16},{8,24},{16,0},{24,8},{1,17},{9,25},{17,1},{25,9},{2,18},{10... | collective-permute-start | bytes 1572872 | tf_op jit(solution)/shard_map/ppermute | solution.py:546
  32.7 2.5 %collective-permute-start.11 = (bf16[1,2,128,1024]{3,2,1,0:T(8,128)(2,1)S(1)}, bf16[1,2,128,1024]{3,2,1,0:T(8,128)(2,1)S(1)}, u32[]{:S(2)}, u32[]{:S(2)}) collective-permute-start(bf16[1,2,128,1024]{3,2,1,0:T(8,128)(2,1)S(1)} %bitcast_dynamic-update-slice_fusion.rest_0_), channel_id=1, source_target_pairs={{0,8},{8,0},{16,24},{24,16},{1,9},{9,1},{17,25},{25,17},{2,10},{10... | collective-permute-start | bytes 1572872 | tf_op jit(solution)/shard_map/ppermute | solution.py:546
  35.2 0.1 slice_add_fusion.1.x_ref
  35.3 0.8 %shard_map.160 = (f32[160,128]{1,0:T(8,128)S(1)}, f32[2,128,128]{2,1,0:T(8,128)S(1)}) custom-call(s32[32]{0:T(128)S(1)} %copy-done.4, s32[8]{0:T(128)S(1)} %copy-done.5, s32[8]{0:T(128)S(1)} %copy-done.9, f32[2]{0:T(128)S(1)} %copy-done.6, f32[2]{0:T(128)S(1)} %copy-done.7, f32[680,128]{1,0:T(8,128)S(1)} %slice_add_fusion.1.x_ref, ...), custom_call_target="tpu_custom_call" | custom-call | tf_op jit(solution)/shard_map/pallas_call | solution.py:376
  36.2 6.9 %collective-permute-start.3 = (f32[2,128,128]{2,1,0:T(8,128)S(1)}, f32[2,128,128]{2,1,0:T(8,128)S(1)}, u32[]{:S(2)}, u32[]{:S(2)}) collective-permute-start(f32[2,128,128]{2,1,0:T(8,128)S(1)} %get-tuple-element.23.rest_0_), channel_id=1, source_target_pairs={{0,8},{8,0},{16,24},{24,16},{1,9},{9,1},{17,25},{25,17},{2,10},{10... | collective-permute-start | bytes 393224 | tf_op jit(solution)/shard_map/ppermute | solution.py:546
  43.0 2.5 %collective-permute-start.4 = (f32[2,128,128]{2,1,0:T(8,128)S(1)}, f32[2,128,128]{2,1,0:T(8,128)S(1)}, u32[]{:S(2)}, u32[]{:S(2)}) collective-permute-start(f32[2,128,128]{2,1,0:T(8,128)S(1)} %get-tuple-element.23.rest_0_), channel_id=1, source_target_pairs={{0,16},{8,24},{16,0},{24,8},{1,17},{9,25},{17,1},{25,9},{2,18},{10... | collective-permute-start | bytes 393224 | tf_op jit(solution)/shard_map/ppermute | solution.py:546
  45.5 1.0 %shard_map.161 = (bf16[64,128]{1,0:T(8,128)(2,1)S(1)}, f32[96,128]{1,0:T(8,128)S(1)}) custom-call(f32[2]{0:T(128)S(1)} %copy-done.6, f32[2]{0:T(128)S(1)} %copy-done.7, f32[2]{0:T(128)S(1)} %copy-done.10, f32[680,128]{1,0:T(8,128)S(1)} %slice_add_fusion.1.x_ref, f32[160,128]{1,0:T(8,128)S(1)} %get-tuple-element.20.v_ref, f32[2,128,128]{2,1,0:T(8,128)S(1)} %bitcast.22, ...), custom_call_target="tpu_custom_call" | custom-call | tf_op jit(solution)/shard_map/pallas_call | solution.py:440
  46.5 4.3 %collective-permute-done.3.rest_1_ = f32[2,128,128]{2,1,0:T(8,128)S(1)} collective-permute-done((f32[2,128,128]{2,1,0:T(8,128)S(1)}, f32[2,128,128]{2,1,0:T(8,128)S(1)}, u32[]{:S(2)}, u32[]{:S(2)}) %collective-permute-start.3) | collective-permute-done | bytes 131104 | tf_op jit(solution)/shard_map/ppermute | solution.py:546
  50.8 1.4 %collective-permute-done.5.rest_3_ = f32[2,128,128]{2,1,0:T(8,128)S(1)} collective-permute-done((f32[2,128,128]{2,1,0:T(8,128)S(1)}, f32[2,128,128]{2,1,0:T(8,128)S(1)}, u32[]{:S(2)}, u32[]{:S(2)}) %collective-permute-start.5) | collective-permute-done | bytes 131104 | tf_op jit(solution)/shard_map/ppermute | solution.py:546
  52.2 1.4 %shard_map.162 = bf16[160,128]{1,0:T(8,128)(2,1)S(1)} custom-call(s32[32]{0:T(128)S(1)} %copy-done.4, s32[8]{0:T(128)S(1)} %copy-done.5, f32[2]{0:T(128)S(1)} %copy-done.6, f32[2]{0:T(128)S(1)} %copy-done.7, f32[680,128]{1,0:T(8,128)S(1)} %slice_add_fusion.1.x_ref, f32[96,128]{1,0:T(8,128)S(1)} %get-tuple-element.21.y_ref, ...), custom_call_target="tpu_custom_call" | custom-call | tf_op jit(solution)/shard_map/pallas_call | solution.py:485
  53.6 1.4 %collective-permute-start.6 = (bf16[1,160,128]{2,1,0:T(8,128)(2,1)S(1)}, bf16[1,160,128]{2,1,0:T(8,128)(2,1)S(1)}, u32[]{:S(2)}, u32[]{:S(2)}) collective-permute-start(bf16[1,160,128]{2,1,0:T(8,128)(2,1)S(1)} %bitcast.23), channel_id=1, source_target_pairs={{0,4},{1,5},{2,6},{3,7},{4,0},{5,1},{6,2},{7,3},{8,12},{9,13},{10,... | collective-permute-start | bytes 122888 | tf_op jit(solution)/shard_map/ppermute | solution.py:543
  55.0 1.8 %collective-permute-start.13 = (bf16[1,128,1024]{2,1,0:T(8,128)(2,1)S(1)}, bf16[1,128,1024]{2,1,0:T(8,128)(2,1)S(1)}, u32[]{:S(2)}, u32[]{:S(2)}) collective-permute-start(bf16[1,128,1024]{2,1,0:T(8,128)(2,1)S(1)} %slice_bitcast_fusion.1), channel_id=1, source_target_pairs={{0,8},{8,0},{16,24},{24,16},{1,9},{9,1},{17,25},{25,17},{2,10},{10... | collective-permute-start | bytes 786440 | tf_op jit(solution)/shard_map/ppermute | solution.py:546
  56.8 2.2 %collective-permute-done.6 = bf16[1,160,128]{2,1,0:T(8,128)(2,1)S(1)} collective-permute-done((bf16[1,160,128]{2,1,0:T(8,128)(2,1)S(1)}, bf16[1,160,128]{2,1,0:T(8,128)(2,1)S(1)}, u32[]{:S(2)}, u32[]{:S(2)}) %collective-permute-start.6) | collective-permute-done | bytes 40992 | tf_op jit(solution)/shard_map/ppermute | solution.py:543
  59.0 2.4 %collective-permute-start.7 = (bf16[2,160,128]{2,1,0:T(8,128)(2,1)S(1)}, bf16[2,160,128]{2,1,0:T(8,128)(2,1)S(1)}, u32[]{:S(2)}, u32[]{:S(2)}) collective-permute-start(bf16[2,160,128]{2,1,0:T(8,128)(2,1)S(1)} %pad_maximum_fusion.3), channel_id=1, source_target_pairs={{0,2},{1,3},{2,0},{3,1},{4,6},{5,7},{6,4},{7,5},{8,10},{9,11},{10,... | collective-permute-start | bytes 245768 | tf_op jit(solution)/shard_map/ppermute | solution.py:543
  61.5 1.9 %collective-permute-start.14 = (bf16[1,128,1024]{2,1,0:T(8,128)(2,1)S(1)}, bf16[1,128,1024]{2,1,0:T(8,128)(2,1)S(1)}, u32[]{:S(2)}, u32[]{:S(2)}) collective-permute-start(bf16[1,128,1024]{2,1,0:T(8,128)(2,1)S(1)} %slice_bitcast_fusion), channel_id=1, source_target_pairs={{0,16},{8,24},{16,0},{24,8},{1,17},{9,25},{17,1},{25,9},{2,18},{10... | collective-permute-start | bytes 786440 | tf_op jit(solution)/shard_map/ppermute | solution.py:546
  63.3 0.5 collective-permute-done.7
  63.9 0.1 collective-permute-start.8
  64.0 3.9 %collective-permute-done.14.rest_4_ = bf16[1,128,1024]{2,1,0:T(8,128)(2,1)S(1)} collective-permute-done((bf16[1,128,1024]{2,1,0:T(8,128)(2,1)S(1)}, bf16[1,128,1024]{2,1,0:T(8,128)(2,1)S(1)}, u32[]{:S(2)}, u32[]{:S(2)}) %collective-permute-start.14) | collective-permute-done | bytes 262176 | tf_op jit(solution)/shard_map/ppermute | solution.py:546
  67.9 2.6 %shard_map.164 = (f32[64,1024]{1,0:T(8,128)}, f32[96,1024]{1,0:T(8,128)}) custom-call(bf16[4,160,128]{2,1,0:T(8,128)(2,1)S(1)} %pad_maximum_fusion.2.a_ref, bf16[4,160,128]{2,1,0:T(8,128)(2,1)S(1)} %collective-permute-done.8.b_ref, bf16[64,1024]{1,0:T(8,128)(2,1)S(1)} %copy-done.1, bf16[96,1024]{1,0:T(8,128)(2,1)S(1)} %bitcast.18, ...), custom_call_target="tpu_custom_call" | custom-call | tf_op jit(solution)/shard_map/pallas_call | solution.py:523
  (44 shorter events, 0.3 us)
Async XLA Ops:
  4.1 5.0 %collective-permute-start = (f32[1640,128]{1,0:T(8,128)S(1)}, f32[1640,128]{1,0:T(8,128)S(1)}, u32[]{:S(2)}, u32[]{:S(2)}) collective-permute-start(f32[1640,128]{1,0:T(8,128)S(1)} %shard_map.159), channel_id=1, source_target_pairs={{0,1},{1,0},{2,3},{3,2},{4,5},{5,4},{6,7},{7,6},{8,9},{9,8},{10,11... | collective-permute-start | bytes 2519048 | tf_op jit(solution)/shard_map/ppermute | solution.py:543
  5.6 9.2 %collective-permute-start.9 = (bf16[2,128,1024]{2,1,0:T(8,128)(2,1)S(1)}, bf16[2,128,1024]{2,1,0:T(8,128)(2,1)S(1)}, u32[]{:S(2)}, u32[]{:S(2)}) collective-permute-start(bf16[2,128,1024]{2,1,0:T(8,128)(2,1)S(1)} %bitcast.20), channel_id=1, source_target_pairs={{0,0},{1,1},{2,4},{3,5},{4,2},{5,3},{6,6},{7,7},{8,10},{9,11},{10,... | collective-permute-start | bytes 1572872 | tf_op jit(solution)/shard_map/ppermute | solution.py:557
  8.9 26.4 %copy-start.2 = (f32[2,2,64,128]{3,2,1,0:T(8,128)S(1)}, f32[2,2,64,128]{3,2,1,0:T(8,128)}, u32[]{:S(2)}) copy-start(f32[2,2,64,128]{3,2,1,0:T(8,128)} %param.28) | copy-start | bytes 393220
  8.9 26.4 %copy-start.3 = (bf16[128,128]{1,0:T(8,128)(2,1)S(1)}, bf16[128,128]{1,0:T(8,128)(2,1)}, u32[]{:S(2)}) copy-start(bf16[128,128]{1,0:T(8,128)(2,1)} %a_ref.1) | copy-start | bytes 98308
  8.9 26.4 %copy-start.4 = (s32[32]{0:T(128)S(1)}, s32[32]{0:T(128)}, u32[]{:S(2)}) copy-start(s32[32]{0:T(128)} %slots_ref.3) | copy-start | bytes 388
  9.0 26.4 %copy-start.5 = (s32[8]{0:T(128)S(1)}, s32[8]{0:T(128)}, u32[]{:S(2)}) copy-start(s32[8]{0:T(128)} %held_ref.3) | copy-start | bytes 100
  9.0 26.3 %copy-start.6 = (f32[2]{0:T(128)S(1)}, f32[2]{0:T(128)}, u32[]{:S(2)}) copy-start(f32[2]{0:T(128)} %bias_ref.5) | copy-start | bytes 28
  9.0 26.3 %copy-start.7 = (f32[2]{0:T(128)S(1)}, f32[2]{0:T(128)}, u32[]{:S(2)}) copy-start(f32[2]{0:T(128)} %rate_ref.5) | copy-start | bytes 28
  9.0 26.3 %copy-start.9 = (s32[8]{0:T(128)S(1)}, s32[8]{0:T(128)}, u32[]{:S(2)}) copy-start(s32[8]{0:T(128)} %tenants_ref.1) | copy-start | bytes 100
  9.0 36.5 %copy-start.8 = (f32[128]{0:T(128)S(1)}, f32[128]{0:T(128)}, u32[]{:S(2)}) copy-start(f32[128]{0:T(128)} %param.27) | copy-start | bytes 1540
  9.0 36.5 %copy-start.10 = (f32[2]{0:T(128)S(1)}, f32[2]{0:T(128)}, u32[]{:S(2)}) copy-start(f32[2]{0:T(128)} %skip_ref.1) | copy-start | bytes 28
  9.2 58.7 %copy-start = (bf16[3,32,1024]{2,1,0:T(8,128)(2,1)S(1)}, bf16[3,32,1024]{2,1,0:T(8,128)(2,1)}, u32[]{:S(2)}) copy-start(bf16[3,32,1024]{2,1,0:T(8,128)(2,1)} %param.18) | copy-start | bytes 589828
  9.2 58.7 %copy-start.1 = (bf16[64,1024]{1,0:T(8,128)(2,1)S(1)}, bf16[64,1024]{1,0:T(8,128)(2,1)}, u32[]{:S(2)}) copy-start(bf16[64,1024]{1,0:T(8,128)(2,1)} %up_ref.5) | copy-start | bytes 393220
  9.3 12.0 %collective-permute-start.1 = (f16[1000,128]{1,0:T(8,128)(2,1)S(1)}, f16[1000,128]{1,0:T(8,128)(2,1)S(1)}, u32[]{:S(2)}, u32[]{:S(2)}) collective-permute-start(f16[1000,128]{1,0:T(8,128)(2,1)S(1)} %pad_maximum_fusion), channel_id=1, source_target_pairs={{0,2},{1,3},{2,0},{3,1},{4,6},{5,7},{6,4},{7,5},{8,10},{9,11},{10,... | collective-permute-start | bytes 768008 | tf_op jit(solution)/shard_map/ppermute | solution.py:543
  14.8 11.0 %collective-permute-start.10 = (bf16[128,1024]{1,0:T(8,128)(2,1)S(1)}, bf16[128,1024]{1,0:T(8,128)(2,1)S(1)}, u32[]{:S(2)}, u32[]{:S(2)}) collective-permute-start(bf16[128,1024]{1,0:T(8,128)(2,1)S(1)} %slice_bitcast_fusion.2), channel_id=1, source_target_pairs={{0,1},{1,0},{2,3},{3,2},{4,5},{5,4},{6,7},{7,6},{8,9},{9,8},{10,11... | collective-permute-start | bytes 786440 | tf_op jit(solution)/shard_map/ppermute | solution.py:543
  21.5 13.7 %collective-permute-start.2 = (f16[680,128]{1,0:T(8,128)(2,1)S(1)}, f16[680,128]{1,0:T(8,128)(2,1)S(1)}, u32[]{:S(2)}, u32[]{:S(2)}) collective-permute-start(f16[680,128]{1,0:T(8,128)(2,1)S(1)} %pad_maximum_fusion.1), channel_id=1, source_target_pairs={{0,4},{1,5},{2,6},{3,7},{4,0},{5,1},{6,2},{7,3},{8,12},{9,13},{10,... | collective-permute-start | bytes 522248 | tf_op jit(solution)/shard_map/ppermute | solution.py:543
  25.9 29.1 %collective-permute-start.12 = (bf16[1,2,128,1024]{3,2,1,0:T(8,128)(2,1)S(1)}, bf16[1,2,128,1024]{3,2,1,0:T(8,128)(2,1)S(1)}, u32[]{:S(2)}, u32[]{:S(2)}) collective-permute-start(bf16[1,2,128,1024]{3,2,1,0:T(8,128)(2,1)S(1)} %bitcast_dynamic-update-slice_fusion.rest_0_), channel_id=1, source_target_pairs={{0,16},{8,24},{16,0},{24,8},{1,17},{9,25},{17,1},{25,9},{2,18},{10... | collective-permute-start | bytes 1572872 | tf_op jit(solution)/shard_map/ppermute | solution.py:546
  32.7 28.7 %collective-permute-start.11 = (bf16[1,2,128,1024]{3,2,1,0:T(8,128)(2,1)S(1)}, bf16[1,2,128,1024]{3,2,1,0:T(8,128)(2,1)S(1)}, u32[]{:S(2)}, u32[]{:S(2)}) collective-permute-start(bf16[1,2,128,1024]{3,2,1,0:T(8,128)(2,1)S(1)} %bitcast_dynamic-update-slice_fusion.rest_0_), channel_id=1, source_target_pairs={{0,8},{8,0},{16,24},{24,16},{1,9},{9,1},{17,25},{25,17},{2,10},{10... | collective-permute-start | bytes 1572872 | tf_op jit(solution)/shard_map/ppermute | solution.py:546
  36.2 14.7 %collective-permute-start.3 = (f32[2,128,128]{2,1,0:T(8,128)S(1)}, f32[2,128,128]{2,1,0:T(8,128)S(1)}, u32[]{:S(2)}, u32[]{:S(2)}) collective-permute-start(f32[2,128,128]{2,1,0:T(8,128)S(1)} %get-tuple-element.23.rest_0_), channel_id=1, source_target_pairs={{0,8},{8,0},{16,24},{24,16},{1,9},{9,1},{17,25},{25,17},{2,10},{10... | collective-permute-start | bytes 393224 | tf_op jit(solution)/shard_map/ppermute | solution.py:546
  43.0 7.8 %collective-permute-start.4 = (f32[2,128,128]{2,1,0:T(8,128)S(1)}, f32[2,128,128]{2,1,0:T(8,128)S(1)}, u32[]{:S(2)}, u32[]{:S(2)}) collective-permute-start(f32[2,128,128]{2,1,0:T(8,128)S(1)} %get-tuple-element.23.rest_0_), channel_id=1, source_target_pairs={{0,16},{8,24},{16,0},{24,8},{1,17},{9,25},{17,1},{25,9},{2,18},{10... | collective-permute-start | bytes 393224 | tf_op jit(solution)/shard_map/ppermute | solution.py:546
  45.5 6.7 %collective-permute-start.5 = (f32[2,128,128]{2,1,0:T(8,128)S(1)}, f32[2,128,128]{2,1,0:T(8,128)S(1)}, u32[]{:S(2)}, u32[]{:S(2)}) collective-permute-start(f32[2,128,128]{2,1,0:T(8,128)S(1)} %get-tuple-element.23.rest_0_), channel_id=1, source_target_pairs={{0,24},{8,16},{16,8},{24,0},{1,25},{9,17},{17,9},{25,1},{2,26},{10... | collective-permute-start | bytes 393224 | tf_op jit(solution)/shard_map/ppermute | solution.py:546
  53.6 5.4 %collective-permute-start.6 = (bf16[1,160,128]{2,1,0:T(8,128)(2,1)S(1)}, bf16[1,160,128]{2,1,0:T(8,128)(2,1)S(1)}, u32[]{:S(2)}, u32[]{:S(2)}) collective-permute-start(bf16[1,160,128]{2,1,0:T(8,128)(2,1)S(1)} %bitcast.23), channel_id=1, source_target_pairs={{0,4},{1,5},{2,6},{3,7},{4,0},{5,1},{6,2},{7,3},{8,12},{9,13},{10,... | collective-permute-start | bytes 122888 | tf_op jit(solution)/shard_map/ppermute | solution.py:543
  55.0 9.0 %collective-permute-start.13 = (bf16[1,128,1024]{2,1,0:T(8,128)(2,1)S(1)}, bf16[1,128,1024]{2,1,0:T(8,128)(2,1)S(1)}, u32[]{:S(2)}, u32[]{:S(2)}) collective-permute-start(bf16[1,128,1024]{2,1,0:T(8,128)(2,1)S(1)} %slice_bitcast_fusion.1), channel_id=1, source_target_pairs={{0,8},{8,0},{16,24},{24,16},{1,9},{9,1},{17,25},{25,17},{2,10},{10... | collective-permute-start | bytes 786440 | tf_op jit(solution)/shard_map/ppermute | solution.py:546
  59.0 4.8 %collective-permute-start.7 = (bf16[2,160,128]{2,1,0:T(8,128)(2,1)S(1)}, bf16[2,160,128]{2,1,0:T(8,128)(2,1)S(1)}, u32[]{:S(2)}, u32[]{:S(2)}) collective-permute-start(bf16[2,160,128]{2,1,0:T(8,128)(2,1)S(1)} %pad_maximum_fusion.3), channel_id=1, source_target_pairs={{0,2},{1,3},{2,0},{3,1},{4,6},{5,7},{6,4},{7,5},{8,10},{9,11},{10,... | collective-permute-start | bytes 245768 | tf_op jit(solution)/shard_map/ppermute | solution.py:543
  61.5 6.4 %collective-permute-start.14 = (bf16[1,128,1024]{2,1,0:T(8,128)(2,1)S(1)}, bf16[1,128,1024]{2,1,0:T(8,128)(2,1)S(1)}, u32[]{:S(2)}, u32[]{:S(2)}) collective-permute-start(bf16[1,128,1024]{2,1,0:T(8,128)(2,1)S(1)} %slice_bitcast_fusion), channel_id=1, source_target_pairs={{0,16},{8,24},{16,0},{24,8},{1,17},{9,25},{17,1},{25,9},{2,18},{10... | collective-permute-start | bytes 786440 | tf_op jit(solution)/shard_map/ppermute | solution.py:546
  63.9 4.0 %collective-permute-start.8 = (bf16[4,160,128]{2,1,0:T(8,128)(2,1)S(1)}, bf16[4,160,128]{2,1,0:T(8,128)(2,1)S(1)}, u32[]{:S(2)}, u32[]{:S(2)}) collective-permute-start(bf16[4,160,128]{2,1,0:T(8,128)(2,1)S(1)} %pad_maximum_fusion.2.a_ref), channel_id=1, source_target_pairs={{0,1},{1,0},{2,3},{3,2},{4,5},{5,4},{6,7},{7,6},{8,9},{9,8},{10,11... | collective-permute-start | bytes 491528 | tf_op jit(solution)/shard_map/ppermute | solution.py:543

commit v3 on v2

--- a/solution.py
+++ b/solution.py
@@ -113,7 +113,9 @@
     return jnp.concatenate(parts, axis=0)
 
 
-def project(prefill_rows, decode_rows, input_weight, lowrank_weight, step_lines, slots, held, tenants, owned):
+def project(
+    routes, prefill_rows, decode_rows, input_weight, lowrank_weight, step_lines, slots, held, tenants, output_weight, owned
+):
     rows_prefill, depth = prefill_rows.shape
     rows = rows_prefill + decode_rows.shape[0]
     width = 2 * HEAD_DEV * HEAD_CHANNELS
@@ -127,6 +129,22 @@
     base = chips * pieces * rows
     total = base + low_blocks * rows + packed
     slot_count = slots.shape[0]
+    count = len(routes)
+    column_width = output_weight.shape[1] // (2 * chips)
+
+    def piece_copies(v_ref, p_ref, sems):
+        group, head = lax.axis_index("grp"), lax.axis_index("head")
+        copies = []
+        for k, rows_of in enumerate(routes):
+            target = looked_up(rows_of, group, head // 2)
+            for side in range(2):
+                column = pl.multiple_of((2 * target + ((head % 2) ^ side)) * column_width, column_width)
+                copies.append(
+                    pltpu.make_async_copy(
+                        v_ref.at[:, pl.ds(column, column_width)], p_ref.at[k, side], sems.at[2 * k + side]
+                    )
+                )
+        return copies
 
     def fetches(up_ref, ud_ref, w_ref, u_ref, w_all, sems, odd):
         me = lax.axis_index("head")
@@ -148,8 +166,8 @@
                 o_ref[at : at + rows] = part[:, k * LANES : (k + 1) * LANES]
 
     def send_body(
-        slots_hbm, held_hbm, tenants_hbm, up_ref, ud_ref, w_ref, l_ref, s_ref, o_ref,
-        u_ref, w_all, l_all, s_all, m_ref, slots_ref, held_ref, tenants_ref, sems,
+        slots_hbm, held_hbm, tenants_hbm, up_ref, ud_ref, w_ref, l_ref, s_ref, v_ref, o_ref, p_ref,
+        u_ref, w_all, l_all, s_all, m_ref, slots_ref, held_ref, tenants_ref, sems, piece_sems,
     ):
         copies = fetches(up_ref, ud_ref, w_ref, u_ref, w_all, sems, 1)
         low_copies = [
@@ -161,7 +179,8 @@
             pltpu.make_async_copy(held_hbm, held_ref, sems.at[5 + chips]),
             pltpu.make_async_copy(tenants_hbm, tenants_ref, sems.at[6 + chips]),
         ]
-        for copy in index_copies + copies[:2] + low_copies + copies[2:]:
+        moved = piece_copies(v_ref, p_ref, piece_sems)
+        for copy in index_copies + copies[:2] + low_copies + copies[2:] + moved:
             copy.start()
         for copy in index_copies:
             copy.wait()
@@ -183,6 +202,8 @@
         )
         o_ref[base + low_blocks * rows :] = pack_rows(m_ref[...], pack)
         products(copies, u_ref, w_all, o_ref)
+        for copy in moved:
+            copy.wait()
 
     def keep_body(up_ref, ud_ref, w_ref, o_ref, u_ref, w_all, sems):
         copies = fetches(up_ref, ud_ref, w_ref, u_ref, w_all, sems, 0)
@@ -198,11 +219,14 @@
         flops=2 * rows * depth * width * chips, bytes_accessed=2 * depth * width * chips, transcendentals=0
     )
     params = pltpu.CompilerParams(vmem_limit_bytes=BIG)
-    send = pl.pallas_call(
+    send, pieces_out = pl.pallas_call(
         send_body,
-        out_shape=jax.ShapeDtypeStruct((total, LANES), F32),
-        in_specs=[hbm] * 8,
-        out_specs=VMEM,
+        out_shape=(
+            jax.ShapeDtypeStruct((total, LANES), F32),
+            jax.ShapeDtypeStruct((count, 2, output_weight.shape[0], column_width), BF16),
+        ),
+        in_specs=[hbm] * 9,
+        out_specs=(VMEM, VMEM),
         scratch_shapes=scratch
         + [
             pltpu.VMEM(lowrank_weight.shape, BF16),
@@ -212,13 +236,16 @@
             pltpu.VMEM(held.shape, jnp.int32),
             pltpu.VMEM(tenants.shape, jnp.int32),
             pltpu.SemaphoreType.DMA((chips + 7,)),
+            pltpu.SemaphoreType.DMA((2 * count,)),
         ],
         compiler_params=params,
         cost_estimate=cost,
     )(
         *[
             in_hbm(x)
-            for x in (slots, held, tenants, prefill_rows, decode_rows, input_weight, lowrank_weight, step_lines)
+            for x in (
+                slots, held, tenants, prefill_rows, decode_rows, input_weight, lowrank_weight, step_lines, output_weight
+            )
         ]
     )
     keep = pl.pallas_call(
@@ -230,7 +257,7 @@
         compiler_params=params,
         cost_estimate=cost,
     )(*[in_hbm(x) for x in (prefill_rows, decode_rows, input_weight)])
-    return send, keep
+    return send, keep, pieces_out
 
 
 def line_load(route):
@@ -262,6 +289,32 @@
                 wanted = found
                 break
     return [wanted[groups * k : groups * (k + 1)] for k in range(chips // groups)]
+
+
+def piece(x_ref, k, rows, at=slice(None)):
+    low, high, _ = at.indices(rows)
+    return x_ref[k * rows + low : k * rows + high]
+
+
+def mixed_rows(x_ref, rows):
+    return unpack_rows(x_ref[4 * rows :], rows // (x_ref.shape[0] - 4 * rows))
+
+
+def piece(x_ref, k, rows, at=slice(None)):
+    low, high, _ = at.indices(rows)
+    return x_ref[k * rows + low : k * rows + high]
+
+
+def mixed_rows(x_ref, rows):
+    return unpack_rows(x_ref[4 * rows :], rows // (x_ref.shape[0] - 4 * rows))
+
+
+def looked_up(table, group, chip):
+    found = jnp.int32(0)
+    for g, row in enumerate(table):
+        for z, value in enumerate(row):
+            found = jnp.where((group == g) & (chip == z), value, found)
+    return found
 
 
 def piece(x_ref, k, rows, at=slice(None)):
@@ -547,22 +600,27 @@
 
     routes = chip_routes(chips, groups)
 
-    def weights_over_head(output_weight):
-        pieces = weight_pieces(output_weight, routes, heads)
+    def weights_over_head(pieces):
         parts = []
         for k, rows in enumerate(routes):
             pairs = [
                 (g * heads + h, g * heads + 2 * rows[g][h // 2] + h % 2) for g in range(groups) for h in range(heads)
             ]
-            parts.append(lax.ppermute(pieces[k], ("grp", "head"), pairs))
+            crossed = [(a, b ^ 1) for a, b in pairs]
+            parts.append(
+                jnp.stack(
+                    [lax.ppermute(pieces[k, 0], ("grp", "head"), pairs), lax.ppermute(pieces[k, 1], ("grp", "head"), crossed)]
+                )
+            )
         return parts
 
-    def weights_over_groups(parts):
-        both = jnp.stack([piece.at[1].set(across(piece[1], 1)) for piece in parts])
+    def weights_over_groups(parts, summed):
+        both = jnp.stack(parts)
         if groups != 4:
-            return [(both,)] + [(over_groups(both, j),) for j in range(1, groups)]
+            return [(both,)] + [(over_groups(both, j),) for j in range(1, groups)], summed
         near, side = over_groups(both, 1), over_groups(both, 2)
-        return [(both,), (near,), (side,), (over_groups(side[:, 0], 1), over_groups(near[:, 1], 2))]
+        summed, near, side = lax.optimization_barrier((summed, near, side))
+        return [(both,), (near,), (side,), (over_groups(side[:, 0], 1), over_groups(near[:, 1], 2))], summed
 
     sources = [[[z ^ row.index(z) for z in range(chips)] for row in rows] for rows in routes]
 
@@ -588,11 +646,11 @@
         start = prompt_start_state.reshape(owned, HEAD_DEV * HEAD_CHANNELS, STATE)
         decode_rows = decode_token_rows.reshape(STEPS * slots, decode_token_rows.shape[2])
         norm_scale = gated_norm_scale.reshape(1, HEAD_DEV * HEAD_CHANNELS)
-        parts = weights_over_head(output_weight)
-        send, keep = project(
-            prefill_token_rows, decode_rows, input_weight, lowrank_weight, step_size_weight.T,
-            slot_sample_index, prompt_at_position, prompt_adapter_index, owned,
+        send, keep, pieces = project(
+            routes, prefill_token_rows, decode_rows, input_weight, lowrank_weight, step_size_weight.T,
+            slot_sample_index, prompt_at_position, prompt_adapter_index, output_weight, owned,
         )
+        parts = weights_over_head(pieces)
         rows = prefill_token_rows.shape[0] + decode_rows.shape[0]
         split = keep.shape[0]
         summed = jnp.concatenate([keep, send[split:]]) + across(send, 1)
@@ -601,7 +659,7 @@
             outgoing = jnp.concatenate([summed[:half], summed[split:]]).astype(F16)
             summed = summed[half:] + across(outgoing, 2 * distance).astype(F32)
             split = half
-        weights = weights_over_groups(parts)
+        weights, summed = weights_over_groups(parts, summed)
         values, finals = end_states(
             rows, summed, adapter_up_weight, head_step_bias, head_decay_rate, start,
             slot_sample_index, prompt_at_position, prompt_adapter_index,

time: 70.7 us -> 66.6 us (0.942)
  starting transfers between devices: 37.3 us -> 27.5 us
  waiting for transfers between devices: 18.8 us -> 25.6 us
  Pallas kernels: 12.8 us -> 11.7 us
    ppermute x7 -> x6, waiting for transfers between devices: 9.17 us -> 17.6 us  [across(): return lax.ppermute(x, 'head', [(i, i ^ distance) for i in range(heads)])]
    ppermute x7 -> x6, starting transfers between devices: 14.2 us -> 6.53 us  [across(): return lax.ppermute(x, 'head', [(i, i ^ distance) for i in range(heads)])]
    ppermute x7, starting transfers between devices: 22.4 us -> 20.2 us  [over_groups(): return lax.ppermute(x, 'grp', [(i, i ^ distance) for i in range(groups)])]
    ppermute x7, waiting for transfers between devices: 9.65 us -> 7.94 us  [over_groups(): return lax.ppermute(x, 'grp', [(i, i ^ distance) for i in range(groups)])]
    pallas_call x2 -> x1, Pallas kernels: 4.48 us -> 3.46 us  [project(): pl.pallas_call(send_body, out_shape=(jax.ShapeDtypeStruct((total, LANES),...]
  transfers between devices with their start and end apart: 15 -> 15, of which waited for: 6 -> 8; matrix products, arithmetic and copies ran while one was open for 1% -> 1% of each run, Pallas kernels for 10% -> 5%
where the time goes in v3:
time: 66.6 us; the launch traced here: 66.4 us
  starting transfers between devices  27.5 us (41%)
  waiting for transfers between devices  25.6 us (38%)
  Pallas kernels  11.7 us (18%)
  between operations  0.95 us (1%)
    ppermute x7, starting transfers between devices, over_groups(): return lax.ppermute(x, 'grp', [(i, i ^ distance) for i in range(groups)])  20.2 us
    ppermute x6, waiting for transfers between devices, across(): return lax.ppermute(x, 'head', [(i, i ^ distance) for i in range(heads)])  17.6 us
    ppermute x7, waiting for transfers between devices, over_groups(): return lax.ppermute(x, 'grp', [(i, i ^ distance) for i in range(groups)])  7.94 us
    ppermute x6, starting transfers between devices, across(): return lax.ppermute(x, 'head', [(i, i ^ distance) for i in range(heads)])  6.53 us
    pallas_call x1, Pallas kernels, project(): pl.pallas_call(send_body, out_shape=(jax.ShapeDtypeStruct((total, LANES),...  3.46 us
    pallas_call x1, Pallas kernels, output_rows(): pl.pallas_call(body, out_shape=(jax.ShapeDtypeStruct(prefill_rows.shape,...  2.56 us
    pallas_call x1, Pallas kernels, project(): pl.pallas_call(keep_body, out_shape=jax.ShapeDtypeStruct((base, LANES), F...  2.54 us
    pallas_call x1, Pallas kernels, decode_rows_out(): pl.pallas_call(body, out_shape=jax.ShapeDtypeStruct((rows, LANES), BF16),...  1.41 us
  transfers between devices with their start and end apart: 15, of which 8 were waited for; matrix products, arithmetic and copies ran while one was open for 1% of the time, Pallas kernels for 5%

profile of v3, /device:TPU:0, one launch (start us, length us, event | category | flops | bytes accessed | tf_op | source)
XLA Modules:
  0.0 66.4 jit_solution(13639293331313986340)
XLA Ops:
  0.6 3.5 %shard_map.159 = (f32[1640,128]{1,0:T(8,128)S(1)}, bf16[1,2,128,1024]{3,2,1,0:T(8,128)(2,1)S(1)}) custom-call(s32[32]{0:T(128)} %slots_ref.3, s32[8]{0:T(128)} %held_ref.3, s32[8]{0:T(128)} %tenants_ref.1, bf16[64,1024]{1,0:T(8,128)(2,1)} %up_ref.5, bf16[96,1024]{1,0:T(8,128)(2,1)} %bitcast.18, bf16[1024,2048]{1,0:T(8,128)(2,1)} %w_ref.3, ...), custom_call_target="tpu_custom_call" | custom-call | flops 335544320 | bytes 2097152 | tf_op jit(solution)/shard_map/pallas_call | solution.py:222
  4.1 0.5 collective-permute-start
  4.7 0.7 %collective-permute-start.3 = (bf16[128,1024]{1,0:T(8,128)(2,1)S(1)}, bf16[128,1024]{1,0:T(8,128)(2,1)S(1)}, u32[]{:S(2)}, u32[]{:S(2)}) collective-permute-start(bf16[128,1024]{1,0:T(8,128)(2,1)S(1)} %get-tuple-element.28), channel_id=1, source_target_pairs={{0,0},{1,1},{2,4},{3,5},{4,2},{5,3},{6,6},{7,7},{8,10},{9,11},{10,... | collective-permute-start | bytes 786440 | tf_op jit(solution)/shard_map/ppermute | solution.py:612
  5.3 0.1 collective-permute-start.4
  5.5 2.5 %shard_map.158 = f32[1280,128]{1,0:T(8,128)S(1)} custom-call(bf16[64,1024]{1,0:T(8,128)(2,1)} %up_ref.5, bf16[96,1024]{1,0:T(8,128)(2,1)} %bitcast.19, bf16[1024,2048]{1,0:T(8,128)(2,1)} %w_ref.3), custom_call_target="tpu_custom_call" | custom-call | flops 335544320 | bytes 2097152 | tf_op jit(solution)/shard_map/pallas_call | solution.py:251
  8.1 0.1 fusion.1
  8.3 0.1 pad_maximum_fusion
  8.4 5.7 %collective-permute-start.1 = (f16[1000,128]{1,0:T(8,128)(2,1)S(1)}, f16[1000,128]{1,0:T(8,128)(2,1)S(1)}, u32[]{:S(2)}, u32[]{:S(2)}) collective-permute-start(f16[1000,128]{1,0:T(8,128)(2,1)S(1)} %pad_maximum_fusion), channel_id=1, source_target_pairs={{0,2},{1,3},{2,0},{3,1},{4,6},{5,7},{6,4},{7,5},{8,10},{9,11},{10,... | collective-permute-start | bytes 768008 | tf_op jit(solution)/shard_map/ppermute | solution.py:596
  14.2 9.9 %collective-permute-start.5 = (bf16[1,2,128,1024]{3,2,1,0:T(8,128)(2,1)S(1)}, bf16[1,2,128,1024]{3,2,1,0:T(8,128)(2,1)S(1)}, u32[]{:S(2)}, u32[]{:S(2)}) collective-permute-start(bf16[1,2,128,1024]{3,2,1,0:T(8,128)(2,1)S(1)} %maximum_bitcast_fusion.rest_0_), channel_id=1, source_target_pairs={{0,8},{8,0},{16,24},{24,16},{1,9},{9,1},{17,25},{25,17},{2,10},{10... | collective-permute-start | bytes 1572872 | tf_op jit(solution)/shard_map/ppermute | solution.py:599
  24.1 2.6 %collective-permute-start.6 = (bf16[1,2,128,1024]{3,2,1,0:T(8,128)(2,1)S(1)}, bf16[1,2,128,1024]{3,2,1,0:T(8,128)(2,1)S(1)}, u32[]{:S(2)}, u32[]{:S(2)}) collective-permute-start(bf16[1,2,128,1024]{3,2,1,0:T(8,128)(2,1)S(1)} %maximum_bitcast_fusion.rest_0_), channel_id=1, source_target_pairs={{0,16},{8,24},{16,0},{24,8},{1,17},{9,25},{17,1},{25,9},{2,18},{10... | collective-permute-start | bytes 1572872 | tf_op jit(solution)/shard_map/ppermute | solution.py:599
  26.7 0.1 fusion
  26.8 0.1 pad_maximum_fusion.1
  26.9 0.1 collective-permute-start.2
  26.9 10.7 %collective-permute-done.2 = f16[680,128]{1,0:T(8,128)(2,1)S(1)} collective-permute-done((f16[680,128]{1,0:T(8,128)(2,1)S(1)}, f16[680,128]{1,0:T(8,128)(2,1)S(1)}, u32[]{:S(2)}, u32[]{:S(2)}) %collective-permute-start.2) | collective-permute-done | bytes 174112 | tf_op jit(solution)/shard_map/ppermute | solution.py:596
  37.7 1.1 %collective-permute-done.6.rest_2_ = bf16[1,2,128,1024]{3,2,1,0:T(8,128)(2,1)S(1)} collective-permute-done((bf16[1,2,128,1024]{3,2,1,0:T(8,128)(2,1)S(1)}, bf16[1,2,128,1024]{3,2,1,0:T(8,128)(2,1)S(1)}, u32[]{:S(2)}, u32[]{:S(2)}) %collective-permute-start.6) | collective-permute-done | bytes 524320 | tf_op jit(solution)/shard_map/ppermute | solution.py:599
  38.9 0.8 %shard_map.160 = (f32[160,128]{1,0:T(8,128)S(1)}, f32[2,128,128]{2,1,0:T(8,128)S(1)}) custom-call(s32[32]{0:T(128)S(1)} %copy-done.4, s32[8]{0:T(128)S(1)} %copy-done.5, s32[8]{0:T(128)S(1)} %copy-done.9, f32[2]{0:T(128)S(1)} %copy-done.6, f32[2]{0:T(128)S(1)} %copy-done.7, f32[680,128]{1,0:T(8,128)S(1)} %slice_add_fusion.1.x_ref, ...), custom_call_target="tpu_custom_call" | custom-call | tf_op jit(solution)/shard_map/pallas_call | solution.py:429
  39.7 2.3 %collective-permute-start.7 = (f32[2,128,128]{2,1,0:T(8,128)S(1)}, f32[2,128,128]{2,1,0:T(8,128)S(1)}, u32[]{:S(2)}, u32[]{:S(2)}) collective-permute-start(f32[2,128,128]{2,1,0:T(8,128)S(1)} %get-tuple-element.19.rest_0_), channel_id=1, source_target_pairs={{0,8},{8,0},{16,24},{24,16},{1,9},{9,1},{17,25},{25,17},{2,10},{10... | collective-permute-start | bytes 393224 | tf_op jit(solution)/shard_map/ppermute | solution.py:599
  42.0 2.5 %collective-permute-start.8 = (f32[2,128,128]{2,1,0:T(8,128)S(1)}, f32[2,128,128]{2,1,0:T(8,128)S(1)}, u32[]{:S(2)}, u32[]{:S(2)}) collective-permute-start(f32[2,128,128]{2,1,0:T(8,128)S(1)} %get-tuple-element.19.rest_0_), channel_id=1, source_target_pairs={{0,16},{8,24},{16,0},{24,8},{1,17},{9,25},{17,1},{25,9},{2,18},{10... | collective-permute-start | bytes 393224 | tf_op jit(solution)/shard_map/ppermute | solution.py:599
  44.5 1.0 %shard_map.161 = (bf16[64,128]{1,0:T(8,128)(2,1)S(1)}, f32[96,128]{1,0:T(8,128)S(1)}) custom-call(f32[2]{0:T(128)S(1)} %copy-done.6, f32[2]{0:T(128)S(1)} %copy-done.7, f32[2]{0:T(128)S(1)} %copy-done.10, f32[680,128]{1,0:T(8,128)S(1)} %slice_add_fusion.1.x_ref, f32[160,128]{1,0:T(8,128)S(1)} %get-tuple-element.16.v_ref, f32[2,128,128]{2,1,0:T(8,128)S(1)} %bitcast.22, ...), custom_call_target="tpu_custom_call" | custom-call | tf_op jit(solution)/shard_map/pallas_call | solution.py:493
  45.5 0.1 collective-permute-done.7.rest_1_
  45.6 3.6 %collective-permute-done.8.rest_2_ = f32[2,128,128]{2,1,0:T(8,128)S(1)} collective-permute-done((f32[2,128,128]{2,1,0:T(8,128)S(1)}, f32[2,128,128]{2,1,0:T(8,128)S(1)}, u32[]{:S(2)}, u32[]{:S(2)}) %collective-permute-start.8) | collective-permute-done | bytes 131104 | tf_op jit(solution)/shard_map/ppermute | solution.py:599
  49.2 1.2 %collective-permute-done.9.rest_3_ = f32[2,128,128]{2,1,0:T(8,128)S(1)} collective-permute-done((f32[2,128,128]{2,1,0:T(8,128)S(1)}, f32[2,128,128]{2,1,0:T(8,128)S(1)}, u32[]{:S(2)}, u32[]{:S(2)}) %collective-permute-start.9) | collective-permute-done | bytes 131104 | tf_op jit(solution)/shard_map/ppermute | solution.py:599
  50.4 1.4 %shard_map.162 = bf16[160,128]{1,0:T(8,128)(2,1)S(1)} custom-call(s32[32]{0:T(128)S(1)} %copy-done.4, s32[8]{0:T(128)S(1)} %copy-done.5, f32[2]{0:T(128)S(1)} %copy-done.6, f32[2]{0:T(128)S(1)} %copy-done.7, f32[680,128]{1,0:T(8,128)S(1)} %slice_add_fusion.1.x_ref, f32[96,128]{1,0:T(8,128)S(1)} %get-tuple-element.17.y_ref, ...), custom_call_target="tpu_custom_call" | custom-call | tf_op jit(solution)/shard_map/pallas_call | solution.py:538
  51.8 0.1 collective-permute-start.10
  51.9 1.1 %collective-permute-start.13 = (bf16[1,128,1024]{2,1,0:T(8,128)(2,1)S(1)}, bf16[1,128,1024]{2,1,0:T(8,128)(2,1)S(1)}, u32[]{:S(2)}, u32[]{:S(2)}) collective-permute-start(bf16[1,128,1024]{2,1,0:T(8,128)(2,1)S(1)} %slice_bitcast_fusion.1), channel_id=1, source_target_pairs={{0,8},{8,0},{16,24},{24,16},{1,9},{9,1},{17,25},{25,17},{2,10},{10... | collective-permute-start | bytes 786440 | tf_op jit(solution)/shard_map/ppermute | solution.py:599
  53.0 4.3 %collective-permute-done.10 = bf16[1,160,128]{2,1,0:T(8,128)(2,1)S(1)} collective-permute-done((bf16[1,160,128]{2,1,0:T(8,128)(2,1)S(1)}, bf16[1,160,128]{2,1,0:T(8,128)(2,1)S(1)}, u32[]{:S(2)}, u32[]{:S(2)}) %collective-permute-start.10) | collective-permute-done | bytes 40992 | tf_op jit(solution)/shard_map/ppermute | solution.py:596
  57.3 0.1 collective-permute-start.11
  57.4 1.8 %collective-permute-start.14 = (bf16[1,128,1024]{2,1,0:T(8,128)(2,1)S(1)}, bf16[1,128,1024]{2,1,0:T(8,128)(2,1)S(1)}, u32[]{:S(2)}, u32[]{:S(2)}) collective-permute-start(bf16[1,128,1024]{2,1,0:T(8,128)(2,1)S(1)} %slice_bitcast_fusion), channel_id=1, source_target_pairs={{0,16},{8,24},{16,0},{24,8},{1,17},{9,25},{17,1},{25,9},{2,18},{10... | collective-permute-start | bytes 786440 | tf_op jit(solution)/shard_map/ppermute | solution.py:599
  59.2 2.6 %collective-permute-done.11 = bf16[2,160,128]{2,1,0:T(8,128)(2,1)S(1)} collective-permute-done((bf16[2,160,128]{2,1,0:T(8,128)(2,1)S(1)}, bf16[2,160,128]{2,1,0:T(8,128)(2,1)S(1)}, u32[]{:S(2)}, u32[]{:S(2)}) %collective-permute-start.11) | collective-permute-done | bytes 81952 | tf_op jit(solution)/shard_map/ppermute | solution.py:596
  61.8 0.1 collective-permute-start.12
  61.9 1.9 %collective-permute-done.14.rest_4_ = bf16[1,128,1024]{2,1,0:T(8,128)(2,1)S(1)} collective-permute-done((bf16[1,128,1024]{2,1,0:T(8,128)(2,1)S(1)}, bf16[1,128,1024]{2,1,0:T(8,128)(2,1)S(1)}, u32[]{:S(2)}, u32[]{:S(2)}) %collective-permute-start.14) | collective-permute-done | bytes 262176 | tf_op jit(solution)/shard_map/ppermute | solution.py:599
  63.9 2.6 %shard_map.163 = (f32[64,1024]{1,0:T(8,128)}, f32[96,1024]{1,0:T(8,128)}) custom-call(bf16[4,160,128]{2,1,0:T(8,128)(2,1)S(1)} %pad_maximum_fusion.2.a_ref, bf16[4,160,128]{2,1,0:T(8,128)(2,1)S(1)} %collective-permute-done.12.b_ref, bf16[64,1024]{1,0:T(8,128)(2,1)S(1)} %copy-done.1, bf16[96,1024]{1,0:T(8,128)(2,1)S(1)} %bitcast.20, ...), custom_call_target="tpu_custom_call" | custom-call | tf_op jit(solution)/shard_map/pallas_call | solution.py:576
  (43 shorter events, 0.4 us)
Async XLA Ops:
  4.1 4.0 %collective-permute-start = (f32[1640,128]{1,0:T(8,128)S(1)}, f32[1640,128]{1,0:T(8,128)S(1)}, u32[]{:S(2)}, u32[]{:S(2)}) collective-permute-start(f32[1640,128]{1,0:T(8,128)S(1)} %get-tuple-element.13), channel_id=1, source_target_pairs={{0,1},{1,0},{2,3},{3,2},{4,5},{5,4},{6,7},{7,6},{8,9},{9,8},{10,11... | collective-permute-start | bytes 2519048 | tf_op jit(solution)/shard_map/ppermute | solution.py:596
  4.7 9.4 %collective-permute-start.3 = (bf16[128,1024]{1,0:T(8,128)(2,1)S(1)}, bf16[128,1024]{1,0:T(8,128)(2,1)S(1)}, u32[]{:S(2)}, u32[]{:S(2)}) collective-permute-start(bf16[128,1024]{1,0:T(8,128)(2,1)S(1)} %get-tuple-element.28), channel_id=1, source_target_pairs={{0,0},{1,1},{2,4},{3,5},{4,2},{5,3},{6,6},{7,7},{8,10},{9,11},{10,... | collective-permute-start | bytes 786440 | tf_op jit(solution)/shard_map/ppermute | solution.py:612
  5.3 8.8 %collective-permute-start.4 = (bf16[128,1024]{1,0:T(8,128)(2,1)S(1)}, bf16[128,1024]{1,0:T(8,128)(2,1)S(1)}, u32[]{:S(2)}, u32[]{:S(2)}) collective-permute-start(bf16[128,1024]{1,0:T(8,128)(2,1)S(1)} %get-tuple-element.29), channel_id=1, source_target_pairs={{0,1},{1,0},{2,5},{3,4},{4,3},{5,2},{6,7},{7,6},{8,11},{9,10},{10,... | collective-permute-start | bytes 786440 | tf_op jit(solution)/shard_map/ppermute | solution.py:612
  8.0 30.8 %copy-start.2 = (f32[2,2,64,128]{3,2,1,0:T(8,128)S(1)}, f32[2,2,64,128]{3,2,1,0:T(8,128)}, u32[]{:S(2)}) copy-start(f32[2,2,64,128]{3,2,1,0:T(8,128)} %param.26) | copy-start | bytes 393220
  8.0 30.8 %copy-start.3 = (bf16[128,128]{1,0:T(8,128)(2,1)S(1)}, bf16[128,128]{1,0:T(8,128)(2,1)}, u32[]{:S(2)}) copy-start(bf16[128,128]{1,0:T(8,128)(2,1)} %a_ref.1) | copy-start | bytes 98308
  8.0 30.8 %copy-start.4 = (s32[32]{0:T(128)S(1)}, s32[32]{0:T(128)}, u32[]{:S(2)}) copy-start(s32[32]{0:T(128)} %slots_ref.3) | copy-start | bytes 388
  8.0 30.8 %copy-start.5 = (s32[8]{0:T(128)S(1)}, s32[8]{0:T(128)}, u32[]{:S(2)}) copy-start(s32[8]{0:T(128)} %held_ref.3) | copy-start | bytes 100
  8.1 30.8 %copy-start.6 = (f32[2]{0:T(128)S(1)}, f32[2]{0:T(128)}, u32[]{:S(2)}) copy-start(f32[2]{0:T(128)} %bias_ref.5) | copy-start | bytes 28
  8.1 30.8 %copy-start.7 = (f32[2]{0:T(128)S(1)}, f32[2]{0:T(128)}, u32[]{:S(2)}) copy-start(f32[2]{0:T(128)} %rate_ref.5) | copy-start | bytes 28
  8.1 30.8 %copy-start.9 = (s32[8]{0:T(128)S(1)}, s32[8]{0:T(128)}, u32[]{:S(2)}) copy-start(s32[8]{0:T(128)} %tenants_ref.1) | copy-start | bytes 100
  8.1 36.4 %copy-start.8 = (f32[128]{0:T(128)S(1)}, f32[128]{0:T(128)}, u32[]{:S(2)}) copy-start(f32[128]{0:T(128)} %param.25) | copy-start | bytes 1540
  8.1 36.4 %copy-start.10 = (f32[2]{0:T(128)S(1)}, f32[2]{0:T(128)}, u32[]{:S(2)}) copy-start(f32[2]{0:T(128)} %skip_ref.1) | copy-start | bytes 28
  8.3 55.6 %copy-start = (bf16[3,32,1024]{2,1,0:T(8,128)(2,1)S(1)}, bf16[3,32,1024]{2,1,0:T(8,128)(2,1)}, u32[]{:S(2)}) copy-start(bf16[3,32,1024]{2,1,0:T(8,128)(2,1)} %param.16) | copy-start | bytes 589828
  8.3 55.5 %copy-start.1 = (bf16[64,1024]{1,0:T(8,128)(2,1)S(1)}, bf16[64,1024]{1,0:T(8,128)(2,1)}, u32[]{:S(2)}) copy-start(bf16[64,1024]{1,0:T(8,128)(2,1)} %up_ref.5) | copy-start | bytes 393220
  8.4 18.2 %collective-permute-start.1 = (f16[1000,128]{1,0:T(8,128)(2,1)S(1)}, f16[1000,128]{1,0:T(8,128)(2,1)S(1)}, u32[]{:S(2)}, u32[]{:S(2)}) collective-permute-start(f16[1000,128]{1,0:T(8,128)(2,1)S(1)} %pad_maximum_fusion), channel_id=1, source_target_pairs={{0,2},{1,3},{2,0},{3,1},{4,6},{5,7},{6,4},{7,5},{8,10},{9,11},{10,... | collective-permute-start | bytes 768008 | tf_op jit(solution)/shard_map/ppermute | solution.py:596
  14.2 23.6 %collective-permute-start.5 = (bf16[1,2,128,1024]{3,2,1,0:T(8,128)(2,1)S(1)}, bf16[1,2,128,1024]{3,2,1,0:T(8,128)(2,1)S(1)}, u32[]{:S(2)}, u32[]{:S(2)}) collective-permute-start(bf16[1,2,128,1024]{3,2,1,0:T(8,128)(2,1)S(1)} %maximum_bitcast_fusion.rest_0_), channel_id=1, source_target_pairs={{0,8},{8,0},{16,24},{24,16},{1,9},{9,1},{17,25},{25,17},{2,10},{10... | collective-permute-start | bytes 1572872 | tf_op jit(solution)/shard_map/ppermute | solution.py:599
  24.1 14.7 %collective-permute-start.6 = (bf16[1,2,128,1024]{3,2,1,0:T(8,128)(2,1)S(1)}, bf16[1,2,128,1024]{3,2,1,0:T(8,128)(2,1)S(1)}, u32[]{:S(2)}, u32[]{:S(2)}) collective-permute-start(bf16[1,2,128,1024]{3,2,1,0:T(8,128)(2,1)S(1)} %maximum_bitcast_fusion.rest_0_), channel_id=1, source_target_pairs={{0,16},{8,24},{16,0},{24,8},{1,17},{9,25},{17,1},{25,9},{2,18},{10... | collective-permute-start | bytes 1572872 | tf_op jit(solution)/shard_map/ppermute | solution.py:599
  26.9 10.8 %collective-permute-start.2 = (f16[680,128]{1,0:T(8,128)(2,1)S(1)}, f16[680,128]{1,0:T(8,128)(2,1)S(1)}, u32[]{:S(2)}, u32[]{:S(2)}) collective-permute-start(f16[680,128]{1,0:T(8,128)(2,1)S(1)} %pad_maximum_fusion.1), channel_id=1, source_target_pairs={{0,4},{1,5},{2,6},{3,7},{4,0},{5,1},{6,2},{7,3},{8,12},{9,13},{10,... | collective-permute-start | bytes 522248 | tf_op jit(solution)/shard_map/ppermute | solution.py:596
  39.7 5.9 %collective-permute-start.7 = (f32[2,128,128]{2,1,0:T(8,128)S(1)}, f32[2,128,128]{2,1,0:T(8,128)S(1)}, u32[]{:S(2)}, u32[]{:S(2)}) collective-permute-start(f32[2,128,128]{2,1,0:T(8,128)S(1)} %get-tuple-element.19.rest_0_), channel_id=1, source_target_pairs={{0,8},{8,0},{16,24},{24,16},{1,9},{9,1},{17,25},{25,17},{2,10},{10... | collective-permute-start | bytes 393224 | tf_op jit(solution)/shard_map/ppermute | solution.py:599
  42.0 7.1 %collective-permute-start.8 = (f32[2,128,128]{2,1,0:T(8,128)S(1)}, f32[2,128,128]{2,1,0:T(8,128)S(1)}, u32[]{:S(2)}, u32[]{:S(2)}) collective-permute-start(f32[2,128,128]{2,1,0:T(8,128)S(1)} %get-tuple-element.19.rest_0_), channel_id=1, source_target_pairs={{0,16},{8,24},{16,0},{24,8},{1,17},{9,25},{17,1},{25,9},{2,18},{10... | collective-permute-start | bytes 393224 | tf_op jit(solution)/shard_map/ppermute | solution.py:599
  44.5 5.9 %collective-permute-start.9 = (f32[2,128,128]{2,1,0:T(8,128)S(1)}, f32[2,128,128]{2,1,0:T(8,128)S(1)}, u32[]{:S(2)}, u32[]{:S(2)}) collective-permute-start(f32[2,128,128]{2,1,0:T(8,128)S(1)} %get-tuple-element.19.rest_0_), channel_id=1, source_target_pairs={{0,24},{8,16},{16,8},{24,0},{1,25},{9,17},{17,9},{25,1},{2,26},{10... | collective-permute-start | bytes 393224 | tf_op jit(solution)/shard_map/ppermute | solution.py:599
  51.8 5.5 %collective-permute-start.10 = (bf16[1,160,128]{2,1,0:T(8,128)(2,1)S(1)}, bf16[1,160,128]{2,1,0:T(8,128)(2,1)S(1)}, u32[]{:S(2)}, u32[]{:S(2)}) collective-permute-start(bf16[1,160,128]{2,1,0:T(8,128)(2,1)S(1)} %bitcast.23), channel_id=1, source_target_pairs={{0,4},{1,5},{2,6},{3,7},{4,0},{5,1},{6,2},{7,3},{8,12},{9,13},{10,... | collective-permute-start | bytes 122888 | tf_op jit(solution)/shard_map/ppermute | solution.py:596
  51.9 10.0 %collective-permute-start.13 = (bf16[1,128,1024]{2,1,0:T(8,128)(2,1)S(1)}, bf16[1,128,1024]{2,1,0:T(8,128)(2,1)S(1)}, u32[]{:S(2)}, u32[]{:S(2)}) collective-permute-start(bf16[1,128,1024]{2,1,0:T(8,128)(2,1)S(1)} %slice_bitcast_fusion.1), channel_id=1, source_target_pairs={{0,8},{8,0},{16,24},{24,16},{1,9},{9,1},{17,25},{25,17},{2,10},{10... | collective-permute-start | bytes 786440 | tf_op jit(solution)/shard_map/ppermute | solution.py:599
  57.3 4.5 %collective-permute-start.11 = (bf16[2,160,128]{2,1,0:T(8,128)(2,1)S(1)}, bf16[2,160,128]{2,1,0:T(8,128)(2,1)S(1)}, u32[]{:S(2)}, u32[]{:S(2)}) collective-permute-start(bf16[2,160,128]{2,1,0:T(8,128)(2,1)S(1)} %pad_maximum_fusion.3), channel_id=1, source_target_pairs={{0,2},{1,3},{2,0},{3,1},{4,6},{5,7},{6,4},{7,5},{8,10},{9,11},{10,... | collective-permute-start | bytes 245768 | tf_op jit(solution)/shard_map/ppermute | solution.py:596
  57.4 6.4 %collective-permute-start.14 = (bf16[1,128,1024]{2,1,0:T(8,128)(2,1)S(1)}, bf16[1,128,1024]{2,1,0:T(8,128)(2,1)S(1)}, u32[]{:S(2)}, u32[]{:S(2)}) collective-permute-start(bf16[1,128,1024]{2,1,0:T(8,128)(2,1)S(1)} %slice_bitcast_fusion), channel_id=1, source_target_pairs={{0,16},{8,24},{16,0},{24,8},{1,17},{9,25},{17,1},{25,9},{2,18},{10... | collective-permute-start | bytes 786440 | tf_op jit(solution)/shard_map/ppermute | solution.py:599
  61.8 2.0 %collective-permute-start.12 = (bf16[4,160,128]{2,1,0:T(8,128)(2,1)S(1)}, bf16[4,160,128]{2,1,0:T(8,128)(2,1)S(1)}, u32[]{:S(2)}, u32[]{:S(2)}) collective-permute-start(bf16[4,160,128]{2,1,0:T(8,128)(2,1)S(1)} %pad_maximum_fusion.2.a_ref), channel_id=1, source_target_pairs={{0,1},{1,0},{2,3},{3,2},{4,5},{5,4},{6,7},{7,6},{8,9},{9,8},{10,11... | collective-permute-start | bytes 491528 | tf_op jit(solution)/shard_map/ppermute | solution.py:596

commit v4 on v3

--- a/solution.py
+++ b/solution.py
@@ -550,28 +550,39 @@
     parts = len(weights)
     per_part = chips // parts
     tile = width // 4 if width % 512 == 0 else width
+    tiles = width // tile
     flat = [w for part in weights for w in part]
 
     def body(a_ref, b_ref, up_ref, ud_ref, *rest):
-        w_refs, (op_ref, od_ref) = list(rest[: len(flat)]), rest[len(flat) :]
-        total = jnp.zeros((rows, tile), F32)
+        w_refs = rest[: len(flat)]
+        op_ref, od_ref, total_ref, sems = rest[len(flat) :]
+        lefts, rights, at = [], [], 0
         for j in range(parts):
-            mine = [w_refs.pop(0) for _ in weights[j]]
             for k in range(per_part):
                 chip = looked_up(sources[k], lax.axis_index("grp") ^ j, lax.axis_index("head") // 2)
-                if len(mine) == 1:
-                    pair = jnp.concatenate([a_ref[chip], b_ref[chip]], axis=1)
-                    total = total + mxu(pair, mine[0][k].reshape(pair.shape[1], tile))
+                if len(weights[j]) == 1:
+                    lefts.append(jnp.concatenate([a_ref[chip], b_ref[chip]], axis=1))
+                    rights.append((w_refs[at], (k,), 2))
                 else:
-                    total = total + mxu(a_ref[chip], mine[0][k]) + mxu(b_ref[chip], mine[1][k])
-        op_ref[...] = up_ref[...].astype(F32) + total[:prefill]
-        od_ref[...] = ud_ref[...].astype(F32) + total[prefill:]
-
-    def column(shape):
-        return pl.BlockSpec(shape, lambda i, *_: (0,) * (len(shape) - 1) + (i,))
-
-    def whole(shape):
-        return pl.BlockSpec(shape, lambda i, *_: (0,) * len(shape))
+                    lefts.extend([a_ref[chip], b_ref[chip]])
+                    rights.extend([(w_refs[at], (k,), 1), (w_refs[at + 1], (k,), 1)])
+            at += len(weights[j])
+        copies = []
+        for t in range(tiles):
+            columns = slice(t * tile, (t + 1) * tile)
+            total = jnp.concatenate([up_ref[:, columns], ud_ref[:, columns]], axis=0).astype(F32)
+            for left, (w_ref, (k,), cores) in zip(lefts, rights):
+                if cores == 2:
+                    total = total + mxu(left, w_ref[k, :, :, columns].reshape(left.shape[1], tile))
+                else:
+                    total = total + mxu(left, w_ref[k, :, columns])
+            total_ref[t] = total
+            copies.append(pltpu.make_async_copy(total_ref.at[t, :prefill], op_ref.at[:, columns], sems.at[2 * t]))
+            copies.append(pltpu.make_async_copy(total_ref.at[t, prefill:], od_ref.at[:, columns], sems.at[2 * t + 1]))
+            copies[-2].start()
+            copies[-1].start()
+        for copy in copies:
+            copy.wait()
 
     return pl.pallas_call(
         body,
@@ -579,10 +590,9 @@
             jax.ShapeDtypeStruct(prefill_rows.shape, F32),
             jax.ShapeDtypeStruct(decode_rows.shape, F32),
         ),
-        grid=(width // tile,),
-        in_specs=[whole(near.shape), whole(far.shape), column((prefill, tile)), column((rows - prefill, tile))]
-        + [column(w.shape[:-1] + (tile,)) for w in flat],
-        out_specs=(column((prefill, tile)), column((rows - prefill, tile))),
+        in_specs=[VMEM] * (4 + len(flat)),
+        out_specs=(pl.BlockSpec(memory_space=pltpu.HBM),) * 2,
+        scratch_shapes=[pltpu.VMEM((tiles, rows, tile), F32), pltpu.SemaphoreType.DMA((2 * tiles,))],
         compiler_params=pltpu.CompilerParams(vmem_limit_bytes=BIG),
     )(near, far, prefill_rows, decode_rows, *flat)
 

time: 66.6 us -> 65.4 us (0.982)
  Pallas kernels: 11.7 us -> 10.6 us
    pallas_call x1, Pallas kernels: 2.56 us -> 1.4 us  [output_rows(): pl.pallas_call(body, out_shape=(jax.ShapeDtypeStruct(prefill_rows.shape,...]
where the time goes in v4:
time: 65.4 us; the launch traced here: 65.3 us
  starting transfers between devices  27.5 us (42%)
  waiting for transfers between devices  25.6 us (39%)
  Pallas kernels  10.6 us (16%)
  between operations  0.95 us (1%)
    ppermute x7, starting transfers between devices, over_groups(): return lax.ppermute(x, 'grp', [(i, i ^ distance) for i in range(groups)])  20.2 us
    ppermute x6, waiting for transfers between devices, across(): return lax.ppermute(x, 'head', [(i, i ^ distance) for i in range(heads)])  17.6 us
    ppermute x7, waiting for transfers between devices, over_groups(): return lax.ppermute(x, 'grp', [(i, i ^ distance) for i in range(groups)])  7.94 us
    ppermute x6, starting transfers between devices, across(): return lax.ppermute(x, 'head', [(i, i ^ distance) for i in range(heads)])  6.53 us
    pallas_call x1, Pallas kernels, project(): pl.pallas_call(send_body, out_shape=(jax.ShapeDtypeStruct((total, LANES),...  3.46 us
    pallas_call x1, Pallas kernels, project(): pl.pallas_call(keep_body, out_shape=jax.ShapeDtypeStruct((base, LANES), F...  2.54 us
    pallas_call x1, Pallas kernels, decode_rows_out(): pl.pallas_call(body, out_shape=jax.ShapeDtypeStruct((rows, LANES), BF16),...  1.41 us
    pallas_call x1, Pallas kernels, output_rows(): pl.pallas_call(body, out_shape=(jax.ShapeDtypeStruct(prefill_rows.shape,...  1.4 us
  transfers between devices with their start and end apart: 15, of which 8 were waited for; matrix products, arithmetic and copies ran while one was open for 1% of the time, Pallas kernels for 5%

profile of v4, /device:TPU:0, one launch (start us, length us, event | category | flops | bytes accessed | tf_op | source)
XLA Modules:
  0.0 65.3 jit_solution(11360454386297663853)
XLA Ops:
  0.6 3.5 %shard_map.159 = (f32[1640,128]{1,0:T(8,128)S(1)}, bf16[1,2,128,1024]{3,2,1,0:T(8,128)(2,1)S(1)}) custom-call(s32[32]{0:T(128)} %slots_ref.3, s32[8]{0:T(128)} %held_ref.3, s32[8]{0:T(128)} %tenants_ref.1, bf16[64,1024]{1,0:T(8,128)(2,1)} %up_ref.5, bf16[96,1024]{1,0:T(8,128)(2,1)} %bitcast.18, bf16[1024,2048]{1,0:T(8,128)(2,1)} %w_ref.3, ...), custom_call_target="tpu_custom_call" | custom-call | flops 335544320 | bytes 2097152 | tf_op jit(solution)/shard_map/pallas_call | solution.py:222
  4.1 0.5 collective-permute-start
  4.7 0.7 %collective-permute-start.3 = (bf16[128,1024]{1,0:T(8,128)(2,1)S(1)}, bf16[128,1024]{1,0:T(8,128)(2,1)S(1)}, u32[]{:S(2)}, u32[]{:S(2)}) collective-permute-start(bf16[128,1024]{1,0:T(8,128)(2,1)S(1)} %get-tuple-element.28), channel_id=1, source_target_pairs={{0,0},{1,1},{2,4},{3,5},{4,2},{5,3},{6,6},{7,7},{8,10},{9,11},{10,... | collective-permute-start | bytes 786440 | tf_op jit(solution)/shard_map/ppermute | solution.py:622
  5.3 0.1 collective-permute-start.4
  5.5 2.5 %shard_map.158 = f32[1280,128]{1,0:T(8,128)S(1)} custom-call(bf16[64,1024]{1,0:T(8,128)(2,1)} %up_ref.5, bf16[96,1024]{1,0:T(8,128)(2,1)} %bitcast.19, bf16[1024,2048]{1,0:T(8,128)(2,1)} %w_ref.3), custom_call_target="tpu_custom_call" | custom-call | flops 335544320 | bytes 2097152 | tf_op jit(solution)/shard_map/pallas_call | solution.py:251
  8.1 0.1 fusion.1
  8.3 0.1 pad_maximum_fusion
  8.4 5.7 %collective-permute-start.1 = (f16[1000,128]{1,0:T(8,128)(2,1)S(1)}, f16[1000,128]{1,0:T(8,128)(2,1)S(1)}, u32[]{:S(2)}, u32[]{:S(2)}) collective-permute-start(f16[1000,128]{1,0:T(8,128)(2,1)S(1)} %pad_maximum_fusion), channel_id=1, source_target_pairs={{0,2},{1,3},{2,0},{3,1},{4,6},{5,7},{6,4},{7,5},{8,10},{9,11},{10,... | collective-permute-start | bytes 768008 | tf_op jit(solution)/shard_map/ppermute | solution.py:606
  14.2 9.9 %collective-permute-start.5 = (bf16[1,2,128,1024]{3,2,1,0:T(8,128)(2,1)S(1)}, bf16[1,2,128,1024]{3,2,1,0:T(8,128)(2,1)S(1)}, u32[]{:S(2)}, u32[]{:S(2)}) collective-permute-start(bf16[1,2,128,1024]{3,2,1,0:T(8,128)(2,1)S(1)} %maximum_bitcast_fusion.rest_0_), channel_id=1, source_target_pairs={{0,8},{8,0},{16,24},{24,16},{1,9},{9,1},{17,25},{25,17},{2,10},{10... | collective-permute-start | bytes 1572872 | tf_op jit(solution)/shard_map/ppermute | solution.py:609
  24.1 2.6 %collective-permute-start.6 = (bf16[1,2,128,1024]{3,2,1,0:T(8,128)(2,1)S(1)}, bf16[1,2,128,1024]{3,2,1,0:T(8,128)(2,1)S(1)}, u32[]{:S(2)}, u32[]{:S(2)}) collective-permute-start(bf16[1,2,128,1024]{3,2,1,0:T(8,128)(2,1)S(1)} %maximum_bitcast_fusion.rest_0_), channel_id=1, source_target_pairs={{0,16},{8,24},{16,0},{24,8},{1,17},{9,25},{17,1},{25,9},{2,18},{10... | collective-permute-start | bytes 1572872 | tf_op jit(solution)/shard_map/ppermute | solution.py:609
  26.7 0.1 fusion
  26.8 0.1 pad_maximum_fusion.1
  26.9 0.1 collective-permute-start.2
  26.9 10.7 %collective-permute-done.2 = f16[680,128]{1,0:T(8,128)(2,1)S(1)} collective-permute-done((f16[680,128]{1,0:T(8,128)(2,1)S(1)}, f16[680,128]{1,0:T(8,128)(2,1)S(1)}, u32[]{:S(2)}, u32[]{:S(2)}) %collective-permute-start.2) | collective-permute-done | bytes 174112 | tf_op jit(solution)/shard_map/ppermute | solution.py:606
  37.7 1.1 %collective-permute-done.6.rest_2_ = bf16[1,2,128,1024]{3,2,1,0:T(8,128)(2,1)S(1)} collective-permute-done((bf16[1,2,128,1024]{3,2,1,0:T(8,128)(2,1)S(1)}, bf16[1,2,128,1024]{3,2,1,0:T(8,128)(2,1)S(1)}, u32[]{:S(2)}, u32[]{:S(2)}) %collective-permute-start.6) | collective-permute-done | bytes 524320 | tf_op jit(solution)/shard_map/ppermute | solution.py:609
  38.9 0.8 %shard_map.160 = (f32[160,128]{1,0:T(8,128)S(1)}, f32[2,128,128]{2,1,0:T(8,128)S(1)}) custom-call(s32[32]{0:T(128)S(1)} %copy-done.4, s32[8]{0:T(128)S(1)} %copy-done.5, s32[8]{0:T(128)S(1)} %copy-done.9, f32[2]{0:T(128)S(1)} %copy-done.6, f32[2]{0:T(128)S(1)} %copy-done.7, f32[680,128]{1,0:T(8,128)S(1)} %slice_add_fusion.1.x_ref, ...), custom_call_target="tpu_custom_call" | custom-call | tf_op jit(solution)/shard_map/pallas_call | solution.py:429
  39.7 2.3 %collective-permute-start.7 = (f32[2,128,128]{2,1,0:T(8,128)S(1)}, f32[2,128,128]{2,1,0:T(8,128)S(1)}, u32[]{:S(2)}, u32[]{:S(2)}) collective-permute-start(f32[2,128,128]{2,1,0:T(8,128)S(1)} %get-tuple-element.19.rest_0_), channel_id=1, source_target_pairs={{0,8},{8,0},{16,24},{24,16},{1,9},{9,1},{17,25},{25,17},{2,10},{10... | collective-permute-start | bytes 393224 | tf_op jit(solution)/shard_map/ppermute | solution.py:609
  42.0 2.5 %collective-permute-start.8 = (f32[2,128,128]{2,1,0:T(8,128)S(1)}, f32[2,128,128]{2,1,0:T(8,128)S(1)}, u32[]{:S(2)}, u32[]{:S(2)}) collective-permute-start(f32[2,128,128]{2,1,0:T(8,128)S(1)} %get-tuple-element.19.rest_0_), channel_id=1, source_target_pairs={{0,16},{8,24},{16,0},{24,8},{1,17},{9,25},{17,1},{25,9},{2,18},{10... | collective-permute-start | bytes 393224 | tf_op jit(solution)/shard_map/ppermute | solution.py:609
  44.5 1.0 %shard_map.161 = (bf16[64,128]{1,0:T(8,128)(2,1)S(1)}, f32[96,128]{1,0:T(8,128)S(1)}) custom-call(f32[2]{0:T(128)S(1)} %copy-done.6, f32[2]{0:T(128)S(1)} %copy-done.7, f32[2]{0:T(128)S(1)} %copy-done.10, f32[680,128]{1,0:T(8,128)S(1)} %slice_add_fusion.1.x_ref, f32[160,128]{1,0:T(8,128)S(1)} %get-tuple-element.16.v_ref, f32[2,128,128]{2,1,0:T(8,128)S(1)} %bitcast.22, ...), custom_call_target="tpu_custom_call" | custom-call | tf_op jit(solution)/shard_map/pallas_call | solution.py:493
  45.5 0.1 collective-permute-done.7.rest_1_
  45.6 3.6 %collective-permute-done.8.rest_2_ = f32[2,128,128]{2,1,0:T(8,128)S(1)} collective-permute-done((f32[2,128,128]{2,1,0:T(8,128)S(1)}, f32[2,128,128]{2,1,0:T(8,128)S(1)}, u32[]{:S(2)}, u32[]{:S(2)}) %collective-permute-start.8) | collective-permute-done | bytes 131104 | tf_op jit(solution)/shard_map/ppermute | solution.py:609
  49.2 1.2 %collective-permute-done.9.rest_3_ = f32[2,128,128]{2,1,0:T(8,128)S(1)} collective-permute-done((f32[2,128,128]{2,1,0:T(8,128)S(1)}, f32[2,128,128]{2,1,0:T(8,128)S(1)}, u32[]{:S(2)}, u32[]{:S(2)}) %collective-permute-start.9) | collective-permute-done | bytes 131104 | tf_op jit(solution)/shard_map/ppermute | solution.py:609
  50.4 1.4 %shard_map.162 = bf16[160,128]{1,0:T(8,128)(2,1)S(1)} custom-call(s32[32]{0:T(128)S(1)} %copy-done.4, s32[8]{0:T(128)S(1)} %copy-done.5, f32[2]{0:T(128)S(1)} %copy-done.6, f32[2]{0:T(128)S(1)} %copy-done.7, f32[680,128]{1,0:T(8,128)S(1)} %slice_add_fusion.1.x_ref, f32[96,128]{1,0:T(8,128)S(1)} %get-tuple-element.17.y_ref, ...), custom_call_target="tpu_custom_call" | custom-call | tf_op jit(solution)/shard_map/pallas_call | solution.py:538
  51.8 0.1 collective-permute-start.10
  51.9 1.1 %collective-permute-start.13 = (bf16[1,128,1024]{2,1,0:T(8,128)(2,1)S(1)}, bf16[1,128,1024]{2,1,0:T(8,128)(2,1)S(1)}, u32[]{:S(2)}, u32[]{:S(2)}) collective-permute-start(bf16[1,128,1024]{2,1,0:T(8,128)(2,1)S(1)} %slice_bitcast_fusion.1), channel_id=1, source_target_pairs={{0,8},{8,0},{16,24},{24,16},{1,9},{9,1},{17,25},{25,17},{2,10},{10... | collective-permute-start | bytes 786440 | tf_op jit(solution)/shard_map/ppermute | solution.py:609
  53.0 4.3 %collective-permute-done.10 = bf16[1,160,128]{2,1,0:T(8,128)(2,1)S(1)} collective-permute-done((bf16[1,160,128]{2,1,0:T(8,128)(2,1)S(1)}, bf16[1,160,128]{2,1,0:T(8,128)(2,1)S(1)}, u32[]{:S(2)}, u32[]{:S(2)}) %collective-permute-start.10) | collective-permute-done | bytes 40992 | tf_op jit(solution)/shard_map/ppermute | solution.py:606
  57.3 0.1 collective-permute-start.11
  57.4 1.8 %collective-permute-start.14 = (bf16[1,128,1024]{2,1,0:T(8,128)(2,1)S(1)}, bf16[1,128,1024]{2,1,0:T(8,128)(2,1)S(1)}, u32[]{:S(2)}, u32[]{:S(2)}) collective-permute-start(bf16[1,128,1024]{2,1,0:T(8,128)(2,1)S(1)} %slice_bitcast_fusion), channel_id=1, source_target_pairs={{0,16},{8,24},{16,0},{24,8},{1,17},{9,25},{17,1},{25,9},{2,18},{10... | collective-permute-start | bytes 786440 | tf_op jit(solution)/shard_map/ppermute | solution.py:609
  59.2 2.6 %collective-permute-done.11 = bf16[2,160,128]{2,1,0:T(8,128)(2,1)S(1)} collective-permute-done((bf16[2,160,128]{2,1,0:T(8,128)(2,1)S(1)}, bf16[2,160,128]{2,1,0:T(8,128)(2,1)S(1)}, u32[]{:S(2)}, u32[]{:S(2)}) %collective-permute-start.11) | collective-permute-done | bytes 81952 | tf_op jit(solution)/shard_map/ppermute | solution.py:606
  61.8 0.1 collective-permute-start.12
  61.9 1.9 %collective-permute-done.14.rest_4_ = bf16[1,128,1024]{2,1,0:T(8,128)(2,1)S(1)} collective-permute-done((bf16[1,128,1024]{2,1,0:T(8,128)(2,1)S(1)}, bf16[1,128,1024]{2,1,0:T(8,128)(2,1)S(1)}, u32[]{:S(2)}, u32[]{:S(2)}) %collective-permute-start.14) | collective-permute-done | bytes 262176 | tf_op jit(solution)/shard_map/ppermute | solution.py:609
  63.9 1.4 %shard_map.163 = (f32[64,1024]{1,0:T(8,128)}, f32[96,1024]{1,0:T(8,128)}) custom-call(bf16[4,160,128]{2,1,0:T(8,128)(2,1)S(1)} %pad_maximum_fusion.2.a_ref, bf16[4,160,128]{2,1,0:T(8,128)(2,1)S(1)} %collective-permute-done.12.b_ref, bf16[64,1024]{1,0:T(8,128)(2,1)S(1)} %copy-done.1, bf16[96,1024]{1,0:T(8,128)(2,1)S(1)} %bitcast.20, ...), custom_call_target="tpu_custom_call" | custom-call | tf_op jit(solution)/shard_map/pallas_call | solution.py:587
  (43 shorter events, 0.4 us)
Async XLA Ops:
  4.1 4.0 %collective-permute-start = (f32[1640,128]{1,0:T(8,128)S(1)}, f32[1640,128]{1,0:T(8,128)S(1)}, u32[]{:S(2)}, u32[]{:S(2)}) collective-permute-start(f32[1640,128]{1,0:T(8,128)S(1)} %get-tuple-element.13), channel_id=1, source_target_pairs={{0,1},{1,0},{2,3},{3,2},{4,5},{5,4},{6,7},{7,6},{8,9},{9,8},{10,11... | collective-permute-start | bytes 2519048 | tf_op jit(solution)/shard_map/ppermute | solution.py:606
  4.7 9.4 %collective-permute-start.3 = (bf16[128,1024]{1,0:T(8,128)(2,1)S(1)}, bf16[128,1024]{1,0:T(8,128)(2,1)S(1)}, u32[]{:S(2)}, u32[]{:S(2)}) collective-permute-start(bf16[128,1024]{1,0:T(8,128)(2,1)S(1)} %get-tuple-element.28), channel_id=1, source_target_pairs={{0,0},{1,1},{2,4},{3,5},{4,2},{5,3},{6,6},{7,7},{8,10},{9,11},{10,... | collective-permute-start | bytes 786440 | tf_op jit(solution)/shard_map/ppermute | solution.py:622
  5.3 8.8 %collective-permute-start.4 = (bf16[128,1024]{1,0:T(8,128)(2,1)S(1)}, bf16[128,1024]{1,0:T(8,128)(2,1)S(1)}, u32[]{:S(2)}, u32[]{:S(2)}) collective-permute-start(bf16[128,1024]{1,0:T(8,128)(2,1)S(1)} %get-tuple-element.29), channel_id=1, source_target_pairs={{0,1},{1,0},{2,5},{3,4},{4,3},{5,2},{6,7},{7,6},{8,11},{9,10},{10,... | collective-permute-start | bytes 786440 | tf_op jit(solution)/shard_map/ppermute | solution.py:622
  8.0 30.8 %copy-start.2 = (f32[2,2,64,128]{3,2,1,0:T(8,128)S(1)}, f32[2,2,64,128]{3,2,1,0:T(8,128)}, u32[]{:S(2)}) copy-start(f32[2,2,64,128]{3,2,1,0:T(8,128)} %param.26) | copy-start | bytes 393220
  8.0 30.8 %copy-start.3 = (bf16[128,128]{1,0:T(8,128)(2,1)S(1)}, bf16[128,128]{1,0:T(8,128)(2,1)}, u32[]{:S(2)}) copy-start(bf16[128,128]{1,0:T(8,128)(2,1)} %a_ref.1) | copy-start | bytes 98308
  8.0 30.8 %copy-start.4 = (s32[32]{0:T(128)S(1)}, s32[32]{0:T(128)}, u32[]{:S(2)}) copy-start(s32[32]{0:T(128)} %slots_ref.3) | copy-start | bytes 388
  8.0 30.8 %copy-start.5 = (s32[8]{0:T(128)S(1)}, s32[8]{0:T(128)}, u32[]{:S(2)}) copy-start(s32[8]{0:T(128)} %held_ref.3) | copy-start | bytes 100
  8.1 30.8 %copy-start.6 = (f32[2]{0:T(128)S(1)}, f32[2]{0:T(128)}, u32[]{:S(2)}) copy-start(f32[2]{0:T(128)} %bias_ref.5) | copy-start | bytes 28
  8.1 30.8 %copy-start.7 = (f32[2]{0:T(128)S(1)}, f32[2]{0:T(128)}, u32[]{:S(2)}) copy-start(f32[2]{0:T(128)} %rate_ref.5) | copy-start | bytes 28
  8.1 30.8 %copy-start.9 = (s32[8]{0:T(128)S(1)}, s32[8]{0:T(128)}, u32[]{:S(2)}) copy-start(s32[8]{0:T(128)} %tenants_ref.1) | copy-start | bytes 100
  8.1 36.4 %copy-start.8 = (f32[128]{0:T(128)S(1)}, f32[128]{0:T(128)}, u32[]{:S(2)}) copy-start(f32[128]{0:T(128)} %param.25) | copy-start | bytes 1540
  8.1 36.4 %copy-start.10 = (f32[2]{0:T(128)S(1)}, f32[2]{0:T(128)}, u32[]{:S(2)}) copy-start(f32[2]{0:T(128)} %skip_ref.1) | copy-start | bytes 28
  8.3 55.6 %copy-start = (bf16[3,32,1024]{2,1,0:T(8,128)(2,1)S(1)}, bf16[3,32,1024]{2,1,0:T(8,128)(2,1)}, u32[]{:S(2)}) copy-start(bf16[3,32,1024]{2,1,0:T(8,128)(2,1)} %param.16) | copy-start | bytes 589828
  8.3 55.5 %copy-start.1 = (bf16[64,1024]{1,0:T(8,128)(2,1)S(1)}, bf16[64,1024]{1,0:T(8,128)(2,1)}, u32[]{:S(2)}) copy-start(bf16[64,1024]{1,0:T(8,128)(2,1)} %up_ref.5) | copy-start | bytes 393220
  8.4 18.2 %collective-permute-start.1 = (f16[1000,128]{1,0:T(8,128)(2,1)S(1)}, f16[1000,128]{1,0:T(8,128)(2,1)S(1)}, u32[]{:S(2)}, u32[]{:S(2)}) collective-permute-start(f16[1000,128]{1,0:T(8,128)(2,1)S(1)} %pad_maximum_fusion), channel_id=1, source_target_pairs={{0,2},{1,3},{2,0},{3,1},{4,6},{5,7},{6,4},{7,5},{8,10},{9,11},{10,... | collective-permute-start | bytes 768008 | tf_op jit(solution)/shard_map/ppermute | solution.py:606
  14.2 23.6 %collective-permute-start.5 = (bf16[1,2,128,1024]{3,2,1,0:T(8,128)(2,1)S(1)}, bf16[1,2,128,1024]{3,2,1,0:T(8,128)(2,1)S(1)}, u32[]{:S(2)}, u32[]{:S(2)}) collective-permute-start(bf16[1,2,128,1024]{3,2,1,0:T(8,128)(2,1)S(1)} %maximum_bitcast_fusion.rest_0_), channel_id=1, source_target_pairs={{0,8},{8,0},{16,24},{24,16},{1,9},{9,1},{17,25},{25,17},{2,10},{10... | collective-permute-start | bytes 1572872 | tf_op jit(solution)/shard_map/ppermute | solution.py:609
  24.1 14.7 %collective-permute-start.6 = (bf16[1,2,128,1024]{3,2,1,0:T(8,128)(2,1)S(1)}, bf16[1,2,128,1024]{3,2,1,0:T(8,128)(2,1)S(1)}, u32[]{:S(2)}, u32[]{:S(2)}) collective-permute-start(bf16[1,2,128,1024]{3,2,1,0:T(8,128)(2,1)S(1)} %maximum_bitcast_fusion.rest_0_), channel_id=1, source_target_pairs={{0,16},{8,24},{16,0},{24,8},{1,17},{9,25},{17,1},{25,9},{2,18},{10... | collective-permute-start | bytes 1572872 | tf_op jit(solution)/shard_map/ppermute | solution.py:609
  26.9 10.8 %collective-permute-start.2 = (f16[680,128]{1,0:T(8,128)(2,1)S(1)}, f16[680,128]{1,0:T(8,128)(2,1)S(1)}, u32[]{:S(2)}, u32[]{:S(2)}) collective-permute-start(f16[680,128]{1,0:T(8,128)(2,1)S(1)} %pad_maximum_fusion.1), channel_id=1, source_target_pairs={{0,4},{1,5},{2,6},{3,7},{4,0},{5,1},{6,2},{7,3},{8,12},{9,13},{10,... | collective-permute-start | bytes 522248 | tf_op jit(solution)/shard_map/ppermute | solution.py:606
  39.7 5.9 %collective-permute-start.7 = (f32[2,128,128]{2,1,0:T(8,128)S(1)}, f32[2,128,128]{2,1,0:T(8,128)S(1)}, u32[]{:S(2)}, u32[]{:S(2)}) collective-permute-start(f32[2,128,128]{2,1,0:T(8,128)S(1)} %get-tuple-element.19.rest_0_), channel_id=1, source_target_pairs={{0,8},{8,0},{16,24},{24,16},{1,9},{9,1},{17,25},{25,17},{2,10},{10... | collective-permute-start | bytes 393224 | tf_op jit(solution)/shard_map/ppermute | solution.py:609
  42.0 7.1 %collective-permute-start.8 = (f32[2,128,128]{2,1,0:T(8,128)S(1)}, f32[2,128,128]{2,1,0:T(8,128)S(1)}, u32[]{:S(2)}, u32[]{:S(2)}) collective-permute-start(f32[2,128,128]{2,1,0:T(8,128)S(1)} %get-tuple-element.19.rest_0_), channel_id=1, source_target_pairs={{0,16},{8,24},{16,0},{24,8},{1,17},{9,25},{17,1},{25,9},{2,18},{10... | collective-permute-start | bytes 393224 | tf_op jit(solution)/shard_map/ppermute | solution.py:609
  44.5 5.9 %collective-permute-start.9 = (f32[2,128,128]{2,1,0:T(8,128)S(1)}, f32[2,128,128]{2,1,0:T(8,128)S(1)}, u32[]{:S(2)}, u32[]{:S(2)}) collective-permute-start(f32[2,128,128]{2,1,0:T(8,128)S(1)} %get-tuple-element.19.rest_0_), channel_id=1, source_target_pairs={{0,24},{8,16},{16,8},{24,0},{1,25},{9,17},{17,9},{25,1},{2,26},{10... | collective-permute-start | bytes 393224 | tf_op jit(solution)/shard_map/ppermute | solution.py:609
  51.8 5.5 %collective-permute-start.10 = (bf16[1,160,128]{2,1,0:T(8,128)(2,1)S(1)}, bf16[1,160,128]{2,1,0:T(8,128)(2,1)S(1)}, u32[]{:S(2)}, u32[]{:S(2)}) collective-permute-start(bf16[1,160,128]{2,1,0:T(8,128)(2,1)S(1)} %bitcast.23), channel_id=1, source_target_pairs={{0,4},{1,5},{2,6},{3,7},{4,0},{5,1},{6,2},{7,3},{8,12},{9,13},{10,... | collective-permute-start | bytes 122888 | tf_op jit(solution)/shard_map/ppermute | solution.py:606
  51.9 10.0 %collective-permute-start.13 = (bf16[1,128,1024]{2,1,0:T(8,128)(2,1)S(1)}, bf16[1,128,1024]{2,1,0:T(8,128)(2,1)S(1)}, u32[]{:S(2)}, u32[]{:S(2)}) collective-permute-start(bf16[1,128,1024]{2,1,0:T(8,128)(2,1)S(1)} %slice_bitcast_fusion.1), channel_id=1, source_target_pairs={{0,8},{8,0},{16,24},{24,16},{1,9},{9,1},{17,25},{25,17},{2,10},{10... | collective-permute-start | bytes 786440 | tf_op jit(solution)/shard_map/ppermute | solution.py:609
  57.3 4.5 %collective-permute-start.11 = (bf16[2,160,128]{2,1,0:T(8,128)(2,1)S(1)}, bf16[2,160,128]{2,1,0:T(8,128)(2,1)S(1)}, u32[]{:S(2)}, u32[]{:S(2)}) collective-permute-start(bf16[2,160,128]{2,1,0:T(8,128)(2,1)S(1)} %pad_maximum_fusion.3), channel_id=1, source_target_pairs={{0,2},{1,3},{2,0},{3,1},{4,6},{5,7},{6,4},{7,5},{8,10},{9,11},{10,... | collective-permute-start | bytes 245768 | tf_op jit(solution)/shard_map/ppermute | solution.py:606
  57.4 6.4 %collective-permute-start.14 = (bf16[1,128,1024]{2,1,0:T(8,128)(2,1)S(1)}, bf16[1,128,1024]{2,1,0:T(8,128)(2,1)S(1)}, u32[]{:S(2)}, u32[]{:S(2)}) collective-permute-start(bf16[1,128,1024]{2,1,0:T(8,128)(2,1)S(1)} %slice_bitcast_fusion), channel_id=1, source_target_pairs={{0,16},{8,24},{16,0},{24,8},{1,17},{9,25},{17,1},{25,9},{2,18},{10... | collective-permute-start | bytes 786440 | tf_op jit(solution)/shard_map/ppermute | solution.py:609
  61.8 2.0 %collective-permute-start.12 = (bf16[4,160,128]{2,1,0:T(8,128)(2,1)S(1)}, bf16[4,160,128]{2,1,0:T(8,128)(2,1)S(1)}, u32[]{:S(2)}, u32[]{:S(2)}) collective-permute-start(bf16[4,160,128]{2,1,0:T(8,128)(2,1)S(1)} %pad_maximum_fusion.2.a_ref), channel_id=1, source_target_pairs={{0,1},{1,0},{2,3},{3,2},{4,5},{5,4},{6,7},{7,6},{8,9},{9,8},{10,11... | collective-permute-start | bytes 491528 | tf_op jit(solution)/shard_map/ppermute | solution.py:606

commit v5 on v4

--- a/solution.py
+++ b/solution.py
@@ -20,6 +20,7 @@
 F16 = jnp.float16
 EXACT = lax.Precision.HIGHEST
 VMEM = pl.BlockSpec(memory_space=pltpu.VMEM)
+PAD = 16
 BIG = 24 * 1024 * 1024
 
 
@@ -402,6 +403,7 @@
     slot_count = slots.shape[0]
 
     def body(slots_ref, held_ref, tenants_ref, bias_ref, rate_ref, x_ref, a_ref, s_ref, v_ref, f_ref):
+        corner = row_ids(LANES, LANES) == lane_ids(LANES)
         group = lax.axis_index("grp")
         mixed = mixed_rows(x_ref, rows)
         lanes = lane_ids(rows)
@@ -422,15 +424,19 @@
             ends = [columns[h][hi - 1 : hi] for h in range(HEAD_DEV)]
             tails = [jnp.exp(ends[h] - columns[h][lo:hi]) * lengths[h][lo:hi] for h in range(HEAD_DEV)]
             added = dot_tn(by_head(tails[0], tails[1], STRETCH) * values[lo:hi], piece(x_ref, 2, rows, slice(lo, hi)))
-            for h in range(HEAD_DEV):
-                at = slice(h * HEAD_CHANNELS, (h + 1) * HEAD_CHANNELS)
-                f_ref[i, at] = jnp.exp(ends[h]) * s_ref[i, at] + added[at]
+            kept = jnp.where(row_ids(LANES) < HEAD_CHANNELS, jnp.exp(ends[0]), jnp.exp(ends[1]))
+            state = kept * s_ref[i] + added
+            largest = jnp.max(jnp.abs(state), axis=1, keepdims=True)
+            power = jnp.ceil(jnp.log2(jnp.maximum(largest, 1e-30)))
+            f_ref[i * LANES : (i + 1) * LANES] = state * jnp.exp2(-power)
+            line = jnp.sum(jnp.where(corner, power, 0.0), axis=0, keepdims=True)
+            f_ref[owned * LANES + i * PAD : owned * LANES + (i + 1) * PAD] = jnp.broadcast_to(line, (PAD, LANES))
 
     return pl.pallas_call(
         body,
         out_shape=(
             jax.ShapeDtypeStruct((rows, LANES), F32),
-            jax.ShapeDtypeStruct((owned, LANES, STATE), F32),
+            jax.ShapeDtypeStruct((owned * (LANES + PAD), STATE), F32),
         ),
         in_specs=[VMEM] * 8,
         out_specs=(VMEM, VMEM),
@@ -505,7 +511,7 @@
 def decode_rows_out(summed, within, prefill_normed, finals, bias, rate, norm_scale, slots, held):
     prefill = prefill_normed.shape[0]
     rows = prefill + within.shape[0]
-    owned = finals[0].shape[0]
+    owned = finals[0].shape[0] // (LANES + PAD)
     slot_count = slots.shape[0]
     parts = len(finals)
 
@@ -521,7 +527,9 @@
         for j in range(parts):
             for i in range(owned):
                 mine = prompts == entry(held, (group ^ j) * owned + i)
-                carried = carried + dot_nt(jnp.where(mine, reader, 0.0), f_refs[j][i])
+                part = dot_nt(jnp.where(mine, reader, 0.0), f_refs[j][i * LANES : (i + 1) * LANES])
+                at = owned * LANES + i * PAD
+                carried = carried + part * jnp.exp2(f_refs[j][at : at + 1])
         lengths = step_lengths(mixed_rows(x_ref, rows)[now], bias_ref)
         kept = []
         for h in range(HEAD_DEV):
@@ -629,7 +637,7 @@
         if groups != 4:
             return [(both,)] + [(over_groups(both, j),) for j in range(1, groups)], summed
         near, side = over_groups(both, 1), over_groups(both, 2)
-        summed, near, side = lax.optimization_barrier((summed, near, side))
+        summed, near = lax.optimization_barrier((summed, near))
         return [(both,), (near,), (side,), (over_groups(side[:, 0], 1), over_groups(near[:, 1], 2))], summed
 
     sources = [[[z ^ row.index(z) for z in range(chips)] for row in rows] for rows in routes]
@@ -674,7 +682,8 @@
             rows, summed, adapter_up_weight, head_step_bias, head_decay_rate, start,
             slot_sample_index, prompt_at_position, prompt_adapter_index,
         )
-        all_finals = [finals] + [over_groups(finals, j) for j in range(1, groups)]
+        message = finals.astype(F16)
+        all_finals = [finals] + [over_groups(message, j).astype(F32) for j in range(1, groups)]
         prefill_normed, within = rows_within(
             summed, values, start, head_step_bias, head_decay_rate, head_skip_scale, norm_scale
         )
@@ -685,6 +694,9 @@
         near = normed[None]
         have = [0]
         for distance in reversed(stages):
+            if distance == stages[0]:
+                near, last = lax.optimization_barrier((near, weights[-1][-1]))
+                weights = weights[:-1] + [weights[-1][:-1] + (last,)]
             near = jnp.concatenate([near, across(near, 2 * distance)])
             have = have + [c ^ distance for c in have]
         near = jnp.concatenate([near[have.index(c)][None] for c in range(chips)])

time: 65.4 us -> 64.1 us (0.980)
  waiting for transfers between devices: 25.6 us -> 16.9 us
  starting transfers between devices: 27.5 us -> 34.7 us
    ppermute x7, starting transfers between devices: 20.2 us -> 25.8 us  [over_groups(): return lax.ppermute(x, 'grp', [(i, i ^ distance) for i in range(groups)])]
    ppermute x6, waiting for transfers between devices: 17.6 us -> 13 us  [across(): return lax.ppermute(x, 'head', [(i, i ^ distance) for i in range(heads)])]
    ppermute x7, waiting for transfers between devices: 7.94 us -> 3.81 us  [over_groups(): return lax.ppermute(x, 'grp', [(i, i ^ distance) for i in range(groups)])]
    ppermute x6, starting transfers between devices: 6.53 us -> 8.07 us  [across(): return lax.ppermute(x, 'head', [(i, i ^ distance) for i in range(heads)])]
  transfers between devices with their start and end apart: 15 -> 15, of which waited for: 8 -> 7; matrix products, arithmetic and copies ran while one was open for 1% -> 1% of each run, Pallas kernels for 5% -> 9%
where the time goes in v5:
time: 64.1 us; the launch traced here: 64 us
  starting transfers between devices  34.7 us (54%)
  waiting for transfers between devices  16.9 us (26%)
  Pallas kernels  10.6 us (17%)
  between operations  0.98 us (2%)
    ppermute x7, starting transfers between devices, over_groups(): return lax.ppermute(x, 'grp', [(i, i ^ distance) for i in range(groups)])  25.8 us
    ppermute x6, waiting for transfers between devices, across(): return lax.ppermute(x, 'head', [(i, i ^ distance) for i in range(heads)])  13 us
    ppermute x6, starting transfers between devices, across(): return lax.ppermute(x, 'head', [(i, i ^ distance) for i in range(heads)])  8.07 us
    ppermute x7, waiting for transfers between devices, over_groups(): return lax.ppermute(x, 'grp', [(i, i ^ distance) for i in range(groups)])  3.81 us
    pallas_call x1, Pallas kernels, project(): pl.pallas_call(send_body, out_shape=(jax.ShapeDtypeStruct((total, LANES),...  3.46 us
    pallas_call x1, Pallas kernels, project(): pl.pallas_call(keep_body, out_shape=jax.ShapeDtypeStruct((base, LANES), F...  2.54 us
    pallas_call x1, Pallas kernels, output_rows(): pl.pallas_call(body, out_shape=(jax.ShapeDtypeStruct(prefill_rows.shape,...  1.4 us
    pallas_call x1, Pallas kernels, decode_rows_out(): pl.pallas_call(body, out_shape=jax.ShapeDtypeStruct((rows, LANES), BF16),...  1.33 us
  transfers between devices with their start and end apart: 15, of which 7 were waited for; matrix products, arithmetic and copies ran while one was open for 1% of the time, Pallas kernels for 9%

profile of v5, /device:TPU:0, one launch (start us, length us, event | category | flops | bytes accessed | tf_op | source)
XLA Modules:
  0.0 64.0 jit_solution(6169729295565041226)
XLA Ops:
  0.6 3.5 %shard_map.159 = (f32[1640,128]{1,0:T(8,128)S(1)}, bf16[1,2,128,1024]{3,2,1,0:T(8,128)(2,1)S(1)}) custom-call(s32[32]{0:T(128)} %slots_ref.3, s32[8]{0:T(128)} %held_ref.3, s32[8]{0:T(128)} %tenants_ref.1, bf16[64,1024]{1,0:T(8,128)(2,1)} %up_ref.5, bf16[96,1024]{1,0:T(8,128)(2,1)} %bitcast.18, bf16[1024,2048]{1,0:T(8,128)(2,1)} %w_ref.3, ...), custom_call_target="tpu_custom_call" | custom-call | flops 335544320 | bytes 2097152 | tf_op jit(solution)/shard_map/pallas_call | solution.py:223
  4.1 0.5 collective-permute-start
  4.7 0.7 %collective-permute-start.3 = (bf16[128,1024]{1,0:T(8,128)(2,1)S(1)}, bf16[128,1024]{1,0:T(8,128)(2,1)S(1)}, u32[]{:S(2)}, u32[]{:S(2)}) collective-permute-start(bf16[128,1024]{1,0:T(8,128)(2,1)S(1)} %get-tuple-element.30), channel_id=1, source_target_pairs={{0,0},{1,1},{2,4},{3,5},{4,2},{5,3},{6,6},{7,7},{8,10},{9,11},{10,... | collective-permute-start | bytes 786440 | tf_op jit(solution)/shard_map/ppermute | solution.py:630
  5.3 0.1 collective-permute-start.4
  5.5 2.5 %shard_map.158 = f32[1280,128]{1,0:T(8,128)S(1)} custom-call(bf16[64,1024]{1,0:T(8,128)(2,1)} %up_ref.5, bf16[96,1024]{1,0:T(8,128)(2,1)} %bitcast.19, bf16[1024,2048]{1,0:T(8,128)(2,1)} %w_ref.3), custom_call_target="tpu_custom_call" | custom-call | flops 335544320 | bytes 2097152 | tf_op jit(solution)/shard_map/pallas_call | solution.py:252
  8.1 0.1 fusion.1
  8.3 0.1 pad_maximum_fusion
  8.4 5.7 %collective-permute-start.1 = (f16[1000,128]{1,0:T(8,128)(2,1)S(1)}, f16[1000,128]{1,0:T(8,128)(2,1)S(1)}, u32[]{:S(2)}, u32[]{:S(2)}) collective-permute-start(f16[1000,128]{1,0:T(8,128)(2,1)S(1)} %pad_maximum_fusion), channel_id=1, source_target_pairs={{0,2},{1,3},{2,0},{3,1},{4,6},{5,7},{6,4},{7,5},{8,10},{9,11},{10,... | collective-permute-start | bytes 768008 | tf_op jit(solution)/shard_map/ppermute | solution.py:614
  14.1 0.1 maximum_bitcast_fusion.rest_0_
  14.2 9.9 %collective-permute-start.5 = (bf16[1,2,128,1024]{3,2,1,0:T(8,128)(2,1)S(1)}, bf16[1,2,128,1024]{3,2,1,0:T(8,128)(2,1)S(1)}, u32[]{:S(2)}, u32[]{:S(2)}) collective-permute-start(bf16[1,2,128,1024]{3,2,1,0:T(8,128)(2,1)S(1)} %maximum_bitcast_fusion.rest_0_), channel_id=1, source_target_pairs={{0,8},{8,0},{16,24},{24,16},{1,9},{9,1},{17,25},{25,17},{2,10},{10... | collective-permute-start | bytes 1572872 | tf_op jit(solution)/shard_map/ppermute | solution.py:617
  24.1 0.1 fusion
  24.3 0.1 pad_maximum_fusion.1
  24.3 1.7 %collective-permute-start.2 = (f16[680,128]{1,0:T(8,128)(2,1)S(1)}, f16[680,128]{1,0:T(8,128)(2,1)S(1)}, u32[]{:S(2)}, u32[]{:S(2)}) collective-permute-start(f16[680,128]{1,0:T(8,128)(2,1)S(1)} %pad_maximum_fusion.1), channel_id=1, source_target_pairs={{0,4},{1,5},{2,6},{3,7},{4,0},{5,1},{6,2},{7,3},{8,12},{9,13},{10,... | collective-permute-start | bytes 522248 | tf_op jit(solution)/shard_map/ppermute | solution.py:614
  26.0 5.7 %collective-permute-start.13 = (bf16[1,2,128,1024]{3,2,1,0:T(8,128)(2,1)S(1)}, bf16[1,2,128,1024]{3,2,1,0:T(8,128)(2,1)S(1)}, u32[]{:S(2)}, u32[]{:S(2)}) collective-permute-start(bf16[1,2,128,1024]{3,2,1,0:T(8,128)(2,1)S(1)} %maximum_bitcast_fusion.rest_0_), channel_id=1, source_target_pairs={{0,16},{8,24},{16,0},{24,8},{1,17},{9,25},{17,1},{25,9},{2,18},{10... | collective-permute-start | bytes 1572872 | tf_op jit(solution)/shard_map/ppermute | solution.py:617
  31.6 3.7 %collective-permute-done.2 = f16[680,128]{1,0:T(8,128)(2,1)S(1)} collective-permute-done((f16[680,128]{1,0:T(8,128)(2,1)S(1)}, f16[680,128]{1,0:T(8,128)(2,1)S(1)}, u32[]{:S(2)}, u32[]{:S(2)}) %collective-permute-start.2) | collective-permute-done | bytes 174112 | tf_op jit(solution)/shard_map/ppermute | solution.py:614
  35.3 1.1 %collective-permute-done.5.rest_1_ = bf16[1,2,128,1024]{3,2,1,0:T(8,128)(2,1)S(1)} collective-permute-done((bf16[1,2,128,1024]{3,2,1,0:T(8,128)(2,1)S(1)}, bf16[1,2,128,1024]{3,2,1,0:T(8,128)(2,1)S(1)}, u32[]{:S(2)}, u32[]{:S(2)}) %collective-permute-start.5) | collective-permute-done | bytes 524320 | tf_op jit(solution)/shard_map/ppermute | solution.py:617
  36.5 0.9 %shard_map.160 = (f32[160,128]{1,0:T(8,128)S(1)}, f32[288,128]{1,0:T(8,128)S(1)}) custom-call(s32[32]{0:T(128)S(1)} %copy-done.4, s32[8]{0:T(128)S(1)} %copy-done.5, s32[8]{0:T(128)S(1)} %copy-done.8, f32[2]{0:T(128)S(1)} %copy-done.6, f32[2]{0:T(128)S(1)} %copy-done.7, f32[680,128]{1,0:T(8,128)S(1)} %slice_add_fusion.1.x_ref, ...), custom_call_target="tpu_custom_call" | custom-call | tf_op jit(solution)/shard_map/pallas_call | solution.py:435
  37.5 4.8 %collective-permute-start.6 = (f16[288,128]{1,0:T(8,128)(2,1)S(1)}, f16[288,128]{1,0:T(8,128)(2,1)S(1)}, u32[]{:S(2)}, u32[]{:S(2)}) collective-permute-start(f16[288,128]{1,0:T(8,128)(2,1)S(1)} %convert_element_type.22), channel_id=1, source_target_pairs={{0,8},{8,0},{16,24},{24,16},{1,9},{9,1},{17,25},{25,17},{2,10},{10... | collective-permute-start | bytes 221192 | tf_op jit(solution)/shard_map/ppermute | solution.py:617
  42.2 2.5 %collective-permute-start.7 = (f16[288,128]{1,0:T(8,128)(2,1)S(1)}, f16[288,128]{1,0:T(8,128)(2,1)S(1)}, u32[]{:S(2)}, u32[]{:S(2)}) collective-permute-start(f16[288,128]{1,0:T(8,128)(2,1)S(1)} %convert_element_type.22), channel_id=1, source_target_pairs={{0,16},{8,24},{16,0},{24,8},{1,17},{9,25},{17,1},{25,9},{2,18},{10... | collective-permute-start | bytes 221192 | tf_op jit(solution)/shard_map/ppermute | solution.py:617
  44.7 1.6 %collective-permute-start.10 = (bf16[1,128,1024]{2,1,0:T(8,128)(2,1)S(1)}, bf16[1,128,1024]{2,1,0:T(8,128)(2,1)S(1)}, u32[]{:S(2)}, u32[]{:S(2)}) collective-permute-start(bf16[1,128,1024]{2,1,0:T(8,128)(2,1)S(1)} %slice_bitcast_fusion.1), channel_id=1, source_target_pairs={{0,16},{8,24},{16,0},{24,8},{1,17},{9,25},{17,1},{25,9},{2,18},{10... | collective-permute-start | bytes 786440 | tf_op jit(solution)/shard_map/ppermute | solution.py:617
  46.3 1.0 %shard_map.161 = (bf16[64,128]{1,0:T(8,128)(2,1)S(1)}, f32[96,128]{1,0:T(8,128)S(1)}) custom-call(f32[2]{0:T(128)S(1)} %copy-done.6, f32[2]{0:T(128)S(1)} %copy-done.7, f32[2]{0:T(128)S(1)} %copy-done.10, f32[680,128]{1,0:T(8,128)S(1)} %slice_add_fusion.1.x_ref, f32[160,128]{1,0:T(8,128)S(1)} %get-tuple-element.17.v_ref, f32[2,128,128]{2,1,0:T(8,128)S(1)} %bitcast.22, ...), custom_call_target="tpu_custom_call" | custom-call | tf_op jit(solution)/shard_map/pallas_call | solution.py:499
  47.3 1.3 %collective-permute-done.7 = f16[288,128]{1,0:T(8,128)(2,1)S(1)} collective-permute-done((f16[288,128]{1,0:T(8,128)(2,1)S(1)}, f16[288,128]{1,0:T(8,128)(2,1)S(1)}, u32[]{:S(2)}, u32[]{:S(2)}) %collective-permute-start.7) | collective-permute-done | bytes 73760 | tf_op jit(solution)/shard_map/ppermute | solution.py:617
  48.6 1.4 %collective-permute-done.8 = f16[288,128]{1,0:T(8,128)(2,1)S(1)} collective-permute-done((f16[288,128]{1,0:T(8,128)(2,1)S(1)}, f16[288,128]{1,0:T(8,128)(2,1)S(1)}, u32[]{:S(2)}, u32[]{:S(2)}) %collective-permute-start.8) | collective-permute-done | bytes 73760 | tf_op jit(solution)/shard_map/ppermute | solution.py:617
  50.1 1.3 %shard_map.162 = bf16[160,128]{1,0:T(8,128)(2,1)S(1)} custom-call(s32[32]{0:T(128)S(1)} %copy-done.4, s32[8]{0:T(128)S(1)} %copy-done.5, f32[2]{0:T(128)S(1)} %copy-done.6, f32[2]{0:T(128)S(1)} %copy-done.7, f32[680,128]{1,0:T(8,128)S(1)} %slice_add_fusion.1.x_ref, f32[96,128]{1,0:T(8,128)S(1)} %get-tuple-element.18.y_ref, ...), custom_call_target="tpu_custom_call" | custom-call | tf_op jit(solution)/shard_map/pallas_call | solution.py:546
  51.4 0.1 collective-permute-start.9
  51.5 1.4 %collective-permute-start.14 = (bf16[1,128,1024]{2,1,0:T(8,128)(2,1)S(1)}, bf16[1,128,1024]{2,1,0:T(8,128)(2,1)S(1)}, u32[]{:S(2)}, u32[]{:S(2)}) collective-permute-start(bf16[1,128,1024]{2,1,0:T(8,128)(2,1)S(1)} %slice_bitcast_fusion), channel_id=1, source_target_pairs={{0,8},{8,0},{16,24},{24,16},{1,9},{9,1},{17,25},{25,17},{2,10},{10... | collective-permute-start | bytes 786440 | tf_op jit(solution)/shard_map/ppermute | solution.py:617
  52.9 3.6 %collective-permute-done.9 = bf16[1,160,128]{2,1,0:T(8,128)(2,1)S(1)} collective-permute-done((bf16[1,160,128]{2,1,0:T(8,128)(2,1)S(1)}, bf16[1,160,128]{2,1,0:T(8,128)(2,1)S(1)}, u32[]{:S(2)}, u32[]{:S(2)}) %collective-permute-start.9) | collective-permute-done | bytes 40992 | tf_op jit(solution)/shard_map/ppermute | solution.py:614
  56.5 0.1 collective-permute-start.11
  56.6 4.4 %collective-permute-done.11 = bf16[2,160,128]{2,1,0:T(8,128)(2,1)S(1)} collective-permute-done((bf16[2,160,128]{2,1,0:T(8,128)(2,1)S(1)}, bf16[2,160,128]{2,1,0:T(8,128)(2,1)S(1)}, u32[]{:S(2)}, u32[]{:S(2)}) %collective-permute-start.11) | collective-permute-done | bytes 81952 | tf_op jit(solution)/shard_map/ppermute | solution.py:614
  61.1 0.1 collective-permute-start.12
  61.2 1.4 %collective-permute-done.12.b_ref = bf16[4,160,128]{2,1,0:T(8,128)(2,1)S(1)} collective-permute-done((bf16[4,160,128]{2,1,0:T(8,128)(2,1)S(1)}, bf16[4,160,128]{2,1,0:T(8,128)(2,1)S(1)}, u32[]{:S(2)}, u32[]{:S(2)}) %collective-permute-start.12) | collective-permute-done | bytes 163872 | tf_op jit(solution)/shard_map/ppermute | solution.py:614
  62.5 1.4 %shard_map.163 = (f32[64,1024]{1,0:T(8,128)}, f32[96,1024]{1,0:T(8,128)}) custom-call(bf16[4,160,128]{2,1,0:T(8,128)(2,1)S(1)} %pad_maximum_fusion.2.a_ref, bf16[4,160,128]{2,1,0:T(8,128)(2,1)S(1)} %collective-permute-done.12.b_ref, bf16[64,1024]{1,0:T(8,128)(2,1)S(1)} %copy-done.1, bf16[96,1024]{1,0:T(8,128)(2,1)S(1)} %bitcast.20, ...), custom_call_target="tpu_custom_call" | custom-call | tf_op jit(solution)/shard_map/pallas_call | solution.py:595
  (48 shorter events, 0.4 us)
Async XLA Ops:
  4.1 4.0 %collective-permute-start = (f32[1640,128]{1,0:T(8,128)S(1)}, f32[1640,128]{1,0:T(8,128)S(1)}, u32[]{:S(2)}, u32[]{:S(2)}) collective-permute-start(f32[1640,128]{1,0:T(8,128)S(1)} %get-tuple-element.14), channel_id=1, source_target_pairs={{0,1},{1,0},{2,3},{3,2},{4,5},{5,4},{6,7},{7,6},{8,9},{9,8},{10,11... | collective-permute-start | bytes 2519048 | tf_op jit(solution)/shard_map/ppermute | solution.py:614
  4.7 9.4 %collective-permute-start.3 = (bf16[128,1024]{1,0:T(8,128)(2,1)S(1)}, bf16[128,1024]{1,0:T(8,128)(2,1)S(1)}, u32[]{:S(2)}, u32[]{:S(2)}) collective-permute-start(bf16[128,1024]{1,0:T(8,128)(2,1)S(1)} %get-tuple-element.30), channel_id=1, source_target_pairs={{0,0},{1,1},{2,4},{3,5},{4,2},{5,3},{6,6},{7,7},{8,10},{9,11},{10,... | collective-permute-start | bytes 786440 | tf_op jit(solution)/shard_map/ppermute | solution.py:630
  5.3 8.7 %collective-permute-start.4 = (bf16[128,1024]{1,0:T(8,128)(2,1)S(1)}, bf16[128,1024]{1,0:T(8,128)(2,1)S(1)}, u32[]{:S(2)}, u32[]{:S(2)}) collective-permute-start(bf16[128,1024]{1,0:T(8,128)(2,1)S(1)} %get-tuple-element.31), channel_id=1, source_target_pairs={{0,1},{1,0},{2,5},{3,4},{4,3},{5,2},{6,7},{7,6},{8,11},{9,10},{10,... | collective-permute-start | bytes 786440 | tf_op jit(solution)/shard_map/ppermute | solution.py:630
  8.0 28.4 %copy-start.2 = (f32[2,2,64,128]{3,2,1,0:T(8,128)S(1)}, f32[2,2,64,128]{3,2,1,0:T(8,128)}, u32[]{:S(2)}) copy-start(f32[2,2,64,128]{3,2,1,0:T(8,128)} %param.26) | copy-start | bytes 393220
  8.0 28.4 %copy-start.3 = (bf16[128,128]{1,0:T(8,128)(2,1)S(1)}, bf16[128,128]{1,0:T(8,128)(2,1)}, u32[]{:S(2)}) copy-start(bf16[128,128]{1,0:T(8,128)(2,1)} %a_ref.1) | copy-start | bytes 98308
  8.0 28.4 %copy-start.4 = (s32[32]{0:T(128)S(1)}, s32[32]{0:T(128)}, u32[]{:S(2)}) copy-start(s32[32]{0:T(128)} %slots_ref.3) | copy-start | bytes 388
  8.0 28.4 %copy-start.5 = (s32[8]{0:T(128)S(1)}, s32[8]{0:T(128)}, u32[]{:S(2)}) copy-start(s32[8]{0:T(128)} %held_ref.3) | copy-start | bytes 100
  8.1 28.4 %copy-start.6 = (f32[2]{0:T(128)S(1)}, f32[2]{0:T(128)}, u32[]{:S(2)}) copy-start(f32[2]{0:T(128)} %bias_ref.5) | copy-start | bytes 28
  8.1 28.4 %copy-start.7 = (f32[2]{0:T(128)S(1)}, f32[2]{0:T(128)}, u32[]{:S(2)}) copy-start(f32[2]{0:T(128)} %rate_ref.5) | copy-start | bytes 28
  8.1 28.4 %copy-start.8 = (s32[8]{0:T(128)S(1)}, s32[8]{0:T(128)}, u32[]{:S(2)}) copy-start(s32[8]{0:T(128)} %tenants_ref.1) | copy-start | bytes 100
  8.1 38.2 %copy-start.9 = (f32[128]{0:T(128)S(1)}, f32[128]{0:T(128)}, u32[]{:S(2)}) copy-start(f32[128]{0:T(128)} %param.25) | copy-start | bytes 1540
  8.1 38.2 %copy-start.10 = (f32[2]{0:T(128)S(1)}, f32[2]{0:T(128)}, u32[]{:S(2)}) copy-start(f32[2]{0:T(128)} %skip_ref.1) | copy-start | bytes 28
  8.4 15.7 %collective-permute-start.1 = (f16[1000,128]{1,0:T(8,128)(2,1)S(1)}, f16[1000,128]{1,0:T(8,128)(2,1)S(1)}, u32[]{:S(2)}, u32[]{:S(2)}) collective-permute-start(f16[1000,128]{1,0:T(8,128)(2,1)S(1)} %pad_maximum_fusion), channel_id=1, source_target_pairs={{0,2},{1,3},{2,0},{3,1},{4,6},{5,7},{6,4},{7,5},{8,10},{9,11},{10,... | collective-permute-start | bytes 768008 | tf_op jit(solution)/shard_map/ppermute | solution.py:614
  14.1 48.4 %copy-start = (bf16[3,32,1024]{2,1,0:T(8,128)(2,1)S(1)}, bf16[3,32,1024]{2,1,0:T(8,128)(2,1)}, u32[]{:S(2)}) copy-start(bf16[3,32,1024]{2,1,0:T(8,128)(2,1)} %param.16) | copy-start | bytes 589828
  14.1 48.4 %copy-start.1 = (bf16[64,1024]{1,0:T(8,128)(2,1)S(1)}, bf16[64,1024]{1,0:T(8,128)(2,1)}, u32[]{:S(2)}) copy-start(bf16[64,1024]{1,0:T(8,128)(2,1)} %up_ref.5) | copy-start | bytes 393220
  14.2 22.3 %collective-permute-start.5 = (bf16[1,2,128,1024]{3,2,1,0:T(8,128)(2,1)S(1)}, bf16[1,2,128,1024]{3,2,1,0:T(8,128)(2,1)S(1)}, u32[]{:S(2)}, u32[]{:S(2)}) collective-permute-start(bf16[1,2,128,1024]{3,2,1,0:T(8,128)(2,1)S(1)} %maximum_bitcast_fusion.rest_0_), channel_id=1, source_target_pairs={{0,8},{8,0},{16,24},{24,16},{1,9},{9,1},{17,25},{25,17},{2,10},{10... | collective-permute-start | bytes 1572872 | tf_op jit(solution)/shard_map/ppermute | solution.py:617
  24.3 11.0 %collective-permute-start.2 = (f16[680,128]{1,0:T(8,128)(2,1)S(1)}, f16[680,128]{1,0:T(8,128)(2,1)S(1)}, u32[]{:S(2)}, u32[]{:S(2)}) collective-permute-start(f16[680,128]{1,0:T(8,128)(2,1)S(1)} %pad_maximum_fusion.1), channel_id=1, source_target_pairs={{0,4},{1,5},{2,6},{3,7},{4,0},{5,1},{6,2},{7,3},{8,12},{9,13},{10,... | collective-permute-start | bytes 522248 | tf_op jit(solution)/shard_map/ppermute | solution.py:614
  26.0 25.5 %collective-permute-start.13 = (bf16[1,2,128,1024]{3,2,1,0:T(8,128)(2,1)S(1)}, bf16[1,2,128,1024]{3,2,1,0:T(8,128)(2,1)S(1)}, u32[]{:S(2)}, u32[]{:S(2)}) collective-permute-start(bf16[1,2,128,1024]{3,2,1,0:T(8,128)(2,1)S(1)} %maximum_bitcast_fusion.rest_0_), channel_id=1, source_target_pairs={{0,16},{8,24},{16,0},{24,8},{1,17},{9,25},{17,1},{25,9},{2,18},{10... | collective-permute-start | bytes 1572872 | tf_op jit(solution)/shard_map/ppermute | solution.py:617
  37.5 9.8 %collective-permute-start.6 = (f16[288,128]{1,0:T(8,128)(2,1)S(1)}, f16[288,128]{1,0:T(8,128)(2,1)S(1)}, u32[]{:S(2)}, u32[]{:S(2)}) collective-permute-start(f16[288,128]{1,0:T(8,128)(2,1)S(1)} %convert_element_type.22), channel_id=1, source_target_pairs={{0,8},{8,0},{16,24},{24,16},{1,9},{9,1},{17,25},{25,17},{2,10},{10... | collective-permute-start | bytes 221192 | tf_op jit(solution)/shard_map/ppermute | solution.py:617
  42.2 6.4 %collective-permute-start.7 = (f16[288,128]{1,0:T(8,128)(2,1)S(1)}, f16[288,128]{1,0:T(8,128)(2,1)S(1)}, u32[]{:S(2)}, u32[]{:S(2)}) collective-permute-start(f16[288,128]{1,0:T(8,128)(2,1)S(1)} %convert_element_type.22), channel_id=1, source_target_pairs={{0,16},{8,24},{16,0},{24,8},{1,17},{9,25},{17,1},{25,9},{2,18},{10... | collective-permute-start | bytes 221192 | tf_op jit(solution)/shard_map/ppermute | solution.py:617
  44.7 5.4 %collective-permute-start.8 = (f16[288,128]{1,0:T(8,128)(2,1)S(1)}, f16[288,128]{1,0:T(8,128)(2,1)S(1)}, u32[]{:S(2)}, u32[]{:S(2)}) collective-permute-start(f16[288,128]{1,0:T(8,128)(2,1)S(1)} %convert_element_type.22), channel_id=1, source_target_pairs={{0,24},{8,16},{16,8},{24,0},{1,25},{9,17},{17,9},{25,1},{2,26},{10... | collective-permute-start | bytes 221192 | tf_op jit(solution)/shard_map/ppermute | solution.py:617
  44.7 11.8 %collective-permute-start.10 = (bf16[1,128,1024]{2,1,0:T(8,128)(2,1)S(1)}, bf16[1,128,1024]{2,1,0:T(8,128)(2,1)S(1)}, u32[]{:S(2)}, u32[]{:S(2)}) collective-permute-start(bf16[1,128,1024]{2,1,0:T(8,128)(2,1)S(1)} %slice_bitcast_fusion.1), channel_id=1, source_target_pairs={{0,16},{8,24},{16,0},{24,8},{1,17},{9,25},{17,1},{25,9},{2,18},{10... | collective-permute-start | bytes 786440 | tf_op jit(solution)/shard_map/ppermute | solution.py:617
  51.4 5.1 %collective-permute-start.9 = (bf16[1,160,128]{2,1,0:T(8,128)(2,1)S(1)}, bf16[1,160,128]{2,1,0:T(8,128)(2,1)S(1)}, u32[]{:S(2)}, u32[]{:S(2)}) collective-permute-start(bf16[1,160,128]{2,1,0:T(8,128)(2,1)S(1)} %bitcast.23), channel_id=1, source_target_pairs={{0,4},{1,5},{2,6},{3,7},{4,0},{5,1},{6,2},{7,3},{8,12},{9,13},{10,... | collective-permute-start | bytes 122888 | tf_op jit(solution)/shard_map/ppermute | solution.py:614
  51.5 9.6 %collective-permute-start.14 = (bf16[1,128,1024]{2,1,0:T(8,128)(2,1)S(1)}, bf16[1,128,1024]{2,1,0:T(8,128)(2,1)S(1)}, u32[]{:S(2)}, u32[]{:S(2)}) collective-permute-start(bf16[1,128,1024]{2,1,0:T(8,128)(2,1)S(1)} %slice_bitcast_fusion), channel_id=1, source_target_pairs={{0,8},{8,0},{16,24},{24,16},{1,9},{9,1},{17,25},{25,17},{2,10},{10... | collective-permute-start | bytes 786440 | tf_op jit(solution)/shard_map/ppermute | solution.py:617
  56.5 4.5 %collective-permute-start.11 = (bf16[2,160,128]{2,1,0:T(8,128)(2,1)S(1)}, bf16[2,160,128]{2,1,0:T(8,128)(2,1)S(1)}, u32[]{:S(2)}, u32[]{:S(2)}) collective-permute-start(bf16[2,160,128]{2,1,0:T(8,128)(2,1)S(1)} %pad_maximum_fusion.3), channel_id=1, source_target_pairs={{0,2},{1,3},{2,0},{3,1},{4,6},{5,7},{6,4},{7,5},{8,10},{9,11},{10,... | collective-permute-start | bytes 245768 | tf_op jit(solution)/shard_map/ppermute | solution.py:614
  61.1 1.5 %collective-permute-start.12 = (bf16[4,160,128]{2,1,0:T(8,128)(2,1)S(1)}, bf16[4,160,128]{2,1,0:T(8,128)(2,1)S(1)}, u32[]{:S(2)}, u32[]{:S(2)}) collective-permute-start(bf16[4,160,128]{2,1,0:T(8,128)(2,1)S(1)} %pad_maximum_fusion.2.a_ref), channel_id=1, source_target_pairs={{0,1},{1,0},{2,3},{3,2},{4,5},{5,4},{6,7},{7,6},{8,9},{9,8},{10,11... | collective-permute-start | bytes 491528 | tf_op jit(solution)/shard_map/ppermute | solution.py:614

commit v6 on v5

--- a/solution.py
+++ b/solution.py
@@ -18,7 +18,6 @@
 F32 = jnp.float32
 BF16 = jnp.bfloat16
 F16 = jnp.float16
-EXACT = lax.Precision.HIGHEST
 VMEM = pl.BlockSpec(memory_space=pltpu.VMEM)
 PAD = 16
 BIG = 24 * 1024 * 1024
@@ -32,12 +31,22 @@
     return pltpu.with_memory_space_constraint(x, pltpu.HBM)
 
 
+def split_dot(a, b, dims):
+    a_high, b_high = a.astype(BF16), b.astype(BF16)
+    a_low, b_low = (a - a_high.astype(F32)).astype(BF16), (b - b_high.astype(F32)).astype(BF16)
+
+    def part(x, y):
+        return lax.dot_general(x, y, (dims, ((), ())), preferred_element_type=F32)
+
+    return part(a_high, b_high) + (part(a_high, b_low) + part(a_low, b_high))
+
+
 def dot_nt(a, b):
-    return lax.dot_general(a, b, (((1,), (1,)), ((), ())), precision=EXACT, preferred_element_type=F32)
+    return split_dot(a, b, ((1,), (1,)))
 
 
 def dot_tn(a, b):
-    return lax.dot_general(a, b, (((0,), (0,)), ((), ())), precision=EXACT, preferred_element_type=F32)
+    return split_dot(a, b, ((0,), (0,)))
 
 
 def lane_ids(rows):
@@ -471,7 +480,7 @@
         sums = []
         for h in range(HEAD_DEV):
             weights = jnp.where(later, jnp.exp(jnp.where(later, columns[h] - lines[h], 0.0)), 0.0) * steps[h]
-            sums.append(jnp.dot(weights * scores, values, precision=EXACT, preferred_element_type=F32))
+            sums.append(split_dot(weights * scores, values, ((1,), (0,))))
         result = by_head(sums[0], sums[1], prefill)
         carried = jnp.concatenate(
             [dot_nt(piece(x_ref, 3, rows, slice(i * STRETCH, (i + 1) * STRETCH)), s_ref[i]) for i in range(owned)], axis=0

time: 64.1 us -> 63.6 us (level)
  transfers between devices with their start and end apart: 15 -> 15, of which waited for: 7 -> 7; matrix products, arithmetic and copies ran while one was open for 1% -> 1% of each run, Pallas kernels for 9% -> 8%
where the time goes in v6:
time: 63.6 us; the launch traced here: 63.5 us
  starting transfers between devices  34.8 us (55%)
  waiting for transfers between devices  16.8 us (26%)
  Pallas kernels  10 us (16%)
  between operations  0.98 us (2%)
    ppermute x7, starting transfers between devices, over_groups(): return lax.ppermute(x, 'grp', [(i, i ^ distance) for i in range(groups)])  25.9 us
    ppermute x6, waiting for transfers between devices, across(): return lax.ppermute(x, 'head', [(i, i ^ distance) for i in range(heads)])  12.8 us
    ppermute x6, starting transfers between devices, across(): return lax.ppermute(x, 'head', [(i, i ^ distance) for i in range(heads)])  8.14 us
    ppermute x7, waiting for transfers between devices, over_groups(): return lax.ppermute(x, 'grp', [(i, i ^ distance) for i in range(groups)])  3.97 us
    pallas_call x1, Pallas kernels, project(): pl.pallas_call(send_body, out_shape=(jax.ShapeDtypeStruct((total, LANES),...  3.46 us
    pallas_call x1, Pallas kernels, project(): pl.pallas_call(keep_body, out_shape=jax.ShapeDtypeStruct((base, LANES), F...  2.54 us
    pallas_call x1, Pallas kernels, output_rows(): pl.pallas_call(body, out_shape=(jax.ShapeDtypeStruct(prefill_rows.shape,...  1.4 us
  transfers between devices with their start and end apart: 15, of which 7 were waited for; matrix products, arithmetic and copies ran while one was open for 1% of the time, Pallas kernels for 8%

profile of v6, /device:TPU:0, one launch (start us, length us, event | category | flops | bytes accessed | tf_op | source)
XLA Modules:
  0.0 63.5 jit_solution(15864029375305053241)
XLA Ops:
  0.6 3.5 %shard_map.159 = (f32[1640,128]{1,0:T(8,128)S(1)}, bf16[1,2,128,1024]{3,2,1,0:T(8,128)(2,1)S(1)}) custom-call(s32[32]{0:T(128)} %slots_ref.3, s32[8]{0:T(128)} %held_ref.3, s32[8]{0:T(128)} %tenants_ref.1, bf16[64,1024]{1,0:T(8,128)(2,1)} %up_ref.5, bf16[96,1024]{1,0:T(8,128)(2,1)} %bitcast.18, bf16[1024,2048]{1,0:T(8,128)(2,1)} %w_ref.3, ...), custom_call_target="tpu_custom_call" | custom-call | flops 335544320 | bytes 2097152 | tf_op jit(solution)/shard_map/pallas_call | solution.py:232
  4.1 0.5 collective-permute-start
  4.7 0.7 %collective-permute-start.3 = (bf16[128,1024]{1,0:T(8,128)(2,1)S(1)}, bf16[128,1024]{1,0:T(8,128)(2,1)S(1)}, u32[]{:S(2)}, u32[]{:S(2)}) collective-permute-start(bf16[128,1024]{1,0:T(8,128)(2,1)S(1)} %get-tuple-element.30), channel_id=1, source_target_pairs={{0,0},{1,1},{2,4},{3,5},{4,2},{5,3},{6,6},{7,7},{8,10},{9,11},{10,... | collective-permute-start | bytes 786440 | tf_op jit(solution)/shard_map/ppermute | solution.py:639
  5.3 0.1 collective-permute-start.4
  5.5 2.5 %shard_map.158 = f32[1280,128]{1,0:T(8,128)S(1)} custom-call(bf16[64,1024]{1,0:T(8,128)(2,1)} %up_ref.5, bf16[96,1024]{1,0:T(8,128)(2,1)} %bitcast.19, bf16[1024,2048]{1,0:T(8,128)(2,1)} %w_ref.3), custom_call_target="tpu_custom_call" | custom-call | flops 335544320 | bytes 2097152 | tf_op jit(solution)/shard_map/pallas_call | solution.py:261
  8.1 0.1 fusion.1
  8.3 0.1 pad_maximum_fusion
  8.4 5.7 %collective-permute-start.1 = (f16[1000,128]{1,0:T(8,128)(2,1)S(1)}, f16[1000,128]{1,0:T(8,128)(2,1)S(1)}, u32[]{:S(2)}, u32[]{:S(2)}) collective-permute-start(f16[1000,128]{1,0:T(8,128)(2,1)S(1)} %pad_maximum_fusion), channel_id=1, source_target_pairs={{0,2},{1,3},{2,0},{3,1},{4,6},{5,7},{6,4},{7,5},{8,10},{9,11},{10,... | collective-permute-start | bytes 768008 | tf_op jit(solution)/shard_map/ppermute | solution.py:623
  14.1 0.1 maximum_bitcast_fusion.rest_0_
  14.2 9.9 %collective-permute-start.5 = (bf16[1,2,128,1024]{3,2,1,0:T(8,128)(2,1)S(1)}, bf16[1,2,128,1024]{3,2,1,0:T(8,128)(2,1)S(1)}, u32[]{:S(2)}, u32[]{:S(2)}) collective-permute-start(bf16[1,2,128,1024]{3,2,1,0:T(8,128)(2,1)S(1)} %maximum_bitcast_fusion.rest_0_), channel_id=1, source_target_pairs={{0,8},{8,0},{16,24},{24,16},{1,9},{9,1},{17,25},{25,17},{2,10},{10... | collective-permute-start | bytes 1572872 | tf_op jit(solution)/shard_map/ppermute | solution.py:626
  24.1 0.1 fusion
  24.3 0.1 pad_maximum_fusion.1
  24.3 1.7 %collective-permute-start.2 = (f16[680,128]{1,0:T(8,128)(2,1)S(1)}, f16[680,128]{1,0:T(8,128)(2,1)S(1)}, u32[]{:S(2)}, u32[]{:S(2)}) collective-permute-start(f16[680,128]{1,0:T(8,128)(2,1)S(1)} %pad_maximum_fusion.1), channel_id=1, source_target_pairs={{0,4},{1,5},{2,6},{3,7},{4,0},{5,1},{6,2},{7,3},{8,12},{9,13},{10,... | collective-permute-start | bytes 522248 | tf_op jit(solution)/shard_map/ppermute | solution.py:623
  26.0 5.7 %collective-permute-start.13 = (bf16[1,2,128,1024]{3,2,1,0:T(8,128)(2,1)S(1)}, bf16[1,2,128,1024]{3,2,1,0:T(8,128)(2,1)S(1)}, u32[]{:S(2)}, u32[]{:S(2)}) collective-permute-start(bf16[1,2,128,1024]{3,2,1,0:T(8,128)(2,1)S(1)} %maximum_bitcast_fusion.rest_0_), channel_id=1, source_target_pairs={{0,16},{8,24},{16,0},{24,8},{1,17},{9,25},{17,1},{25,9},{2,18},{10... | collective-permute-start | bytes 1572872 | tf_op jit(solution)/shard_map/ppermute | solution.py:626
  31.6 3.7 %collective-permute-done.2 = f16[680,128]{1,0:T(8,128)(2,1)S(1)} collective-permute-done((f16[680,128]{1,0:T(8,128)(2,1)S(1)}, f16[680,128]{1,0:T(8,128)(2,1)S(1)}, u32[]{:S(2)}, u32[]{:S(2)}) %collective-permute-start.2) | collective-permute-done | bytes 174112 | tf_op jit(solution)/shard_map/ppermute | solution.py:623
  35.3 1.1 %collective-permute-done.5.rest_1_ = bf16[1,2,128,1024]{3,2,1,0:T(8,128)(2,1)S(1)} collective-permute-done((bf16[1,2,128,1024]{3,2,1,0:T(8,128)(2,1)S(1)}, bf16[1,2,128,1024]{3,2,1,0:T(8,128)(2,1)S(1)}, u32[]{:S(2)}, u32[]{:S(2)}) %collective-permute-start.5) | collective-permute-done | bytes 524320 | tf_op jit(solution)/shard_map/ppermute | solution.py:626
  36.5 0.9 %shard_map.160 = (f32[160,128]{1,0:T(8,128)S(1)}, f32[288,128]{1,0:T(8,128)S(1)}) custom-call(s32[32]{0:T(128)S(1)} %copy-done.4, s32[8]{0:T(128)S(1)} %copy-done.5, s32[8]{0:T(128)S(1)} %copy-done.8, f32[2]{0:T(128)S(1)} %copy-done.6, f32[2]{0:T(128)S(1)} %copy-done.7, f32[680,128]{1,0:T(8,128)S(1)} %slice_add_fusion.1.x_ref, ...), custom_call_target="tpu_custom_call" | custom-call | tf_op jit(solution)/shard_map/pallas_call | solution.py:444
  37.4 4.8 %collective-permute-start.6 = (f16[288,128]{1,0:T(8,128)(2,1)S(1)}, f16[288,128]{1,0:T(8,128)(2,1)S(1)}, u32[]{:S(2)}, u32[]{:S(2)}) collective-permute-start(f16[288,128]{1,0:T(8,128)(2,1)S(1)} %convert_element_type.22), channel_id=1, source_target_pairs={{0,8},{8,0},{16,24},{24,16},{1,9},{9,1},{17,25},{25,17},{2,10},{10... | collective-permute-start | bytes 221192 | tf_op jit(solution)/shard_map/ppermute | solution.py:626
  42.2 2.5 %collective-permute-start.7 = (f16[288,128]{1,0:T(8,128)(2,1)S(1)}, f16[288,128]{1,0:T(8,128)(2,1)S(1)}, u32[]{:S(2)}, u32[]{:S(2)}) collective-permute-start(f16[288,128]{1,0:T(8,128)(2,1)S(1)} %convert_element_type.22), channel_id=1, source_target_pairs={{0,16},{8,24},{16,0},{24,8},{1,17},{9,25},{17,1},{25,9},{2,18},{10... | collective-permute-start | bytes 221192 | tf_op jit(solution)/shard_map/ppermute | solution.py:626
  44.7 1.6 %collective-permute-start.10 = (bf16[1,128,1024]{2,1,0:T(8,128)(2,1)S(1)}, bf16[1,128,1024]{2,1,0:T(8,128)(2,1)S(1)}, u32[]{:S(2)}, u32[]{:S(2)}) collective-permute-start(bf16[1,128,1024]{2,1,0:T(8,128)(2,1)S(1)} %slice_bitcast_fusion.1), channel_id=1, source_target_pairs={{0,16},{8,24},{16,0},{24,8},{1,17},{9,25},{17,1},{25,9},{2,18},{10... | collective-permute-start | bytes 786440 | tf_op jit(solution)/shard_map/ppermute | solution.py:626
  46.3 0.8 %shard_map.161 = (bf16[64,128]{1,0:T(8,128)(2,1)S(1)}, f32[96,128]{1,0:T(8,128)S(1)}) custom-call(f32[2]{0:T(128)S(1)} %copy-done.6, f32[2]{0:T(128)S(1)} %copy-done.7, f32[2]{0:T(128)S(1)} %copy-done.10, f32[680,128]{1,0:T(8,128)S(1)} %slice_add_fusion.1.x_ref, f32[160,128]{1,0:T(8,128)S(1)} %get-tuple-element.17.v_ref, f32[2,128,128]{2,1,0:T(8,128)S(1)} %bitcast.22, ...), custom_call_target="tpu_custom_call" | custom-call | tf_op jit(solution)/shard_map/pallas_call | solution.py:508
  47.1 1.4 %collective-permute-done.7 = f16[288,128]{1,0:T(8,128)(2,1)S(1)} collective-permute-done((f16[288,128]{1,0:T(8,128)(2,1)S(1)}, f16[288,128]{1,0:T(8,128)(2,1)S(1)}, u32[]{:S(2)}, u32[]{:S(2)}) %collective-permute-start.7) | collective-permute-done | bytes 73760 | tf_op jit(solution)/shard_map/ppermute | solution.py:626
  48.6 1.4 %collective-permute-done.8 = f16[288,128]{1,0:T(8,128)(2,1)S(1)} collective-permute-done((f16[288,128]{1,0:T(8,128)(2,1)S(1)}, f16[288,128]{1,0:T(8,128)(2,1)S(1)}, u32[]{:S(2)}, u32[]{:S(2)}) %collective-permute-start.8) | collective-permute-done | bytes 73760 | tf_op jit(solution)/shard_map/ppermute | solution.py:626
  50.0 1.0 %shard_map.162 = bf16[160,128]{1,0:T(8,128)(2,1)S(1)} custom-call(s32[32]{0:T(128)S(1)} %copy-done.4, s32[8]{0:T(128)S(1)} %copy-done.5, f32[2]{0:T(128)S(1)} %copy-done.6, f32[2]{0:T(128)S(1)} %copy-done.7, f32[680,128]{1,0:T(8,128)S(1)} %slice_add_fusion.1.x_ref, f32[96,128]{1,0:T(8,128)S(1)} %get-tuple-element.18.y_ref, ...), custom_call_target="tpu_custom_call" | custom-call | tf_op jit(solution)/shard_map/pallas_call | solution.py:555
  51.0 0.1 collective-permute-start.9
  51.1 1.4 %collective-permute-start.14 = (bf16[1,128,1024]{2,1,0:T(8,128)(2,1)S(1)}, bf16[1,128,1024]{2,1,0:T(8,128)(2,1)S(1)}, u32[]{:S(2)}, u32[]{:S(2)}) collective-permute-start(bf16[1,128,1024]{2,1,0:T(8,128)(2,1)S(1)} %slice_bitcast_fusion), channel_id=1, source_target_pairs={{0,8},{8,0},{16,24},{24,16},{1,9},{9,1},{17,25},{25,17},{2,10},{10... | collective-permute-start | bytes 786440 | tf_op jit(solution)/shard_map/ppermute | solution.py:626
  52.5 3.5 %collective-permute-done.9 = bf16[1,160,128]{2,1,0:T(8,128)(2,1)S(1)} collective-permute-done((bf16[1,160,128]{2,1,0:T(8,128)(2,1)S(1)}, bf16[1,160,128]{2,1,0:T(8,128)(2,1)S(1)}, u32[]{:S(2)}, u32[]{:S(2)}) %collective-permute-start.9) | collective-permute-done | bytes 40992 | tf_op jit(solution)/shard_map/ppermute | solution.py:623
  56.0 0.2 collective-permute-start.11
  56.2 4.3 %collective-permute-done.11 = bf16[2,160,128]{2,1,0:T(8,128)(2,1)S(1)} collective-permute-done((bf16[2,160,128]{2,1,0:T(8,128)(2,1)S(1)}, bf16[2,160,128]{2,1,0:T(8,128)(2,1)S(1)}, u32[]{:S(2)}, u32[]{:S(2)}) %collective-permute-start.11) | collective-permute-done | bytes 81952 | tf_op jit(solution)/shard_map/ppermute | solution.py:623
  60.6 0.1 collective-permute-start.12
  60.7 1.4 %collective-permute-done.12.b_ref = bf16[4,160,128]{2,1,0:T(8,128)(2,1)S(1)} collective-permute-done((bf16[4,160,128]{2,1,0:T(8,128)(2,1)S(1)}, bf16[4,160,128]{2,1,0:T(8,128)(2,1)S(1)}, u32[]{:S(2)}, u32[]{:S(2)}) %collective-permute-start.12) | collective-permute-done | bytes 163872 | tf_op jit(solution)/shard_map/ppermute | solution.py:623
  62.0 1.4 %shard_map.163 = (f32[64,1024]{1,0:T(8,128)}, f32[96,1024]{1,0:T(8,128)}) custom-call(bf16[4,160,128]{2,1,0:T(8,128)(2,1)S(1)} %pad_maximum_fusion.2.a_ref, bf16[4,160,128]{2,1,0:T(8,128)(2,1)S(1)} %collective-permute-done.12.b_ref, bf16[64,1024]{1,0:T(8,128)(2,1)S(1)} %copy-done.1, bf16[96,1024]{1,0:T(8,128)(2,1)S(1)} %bitcast.20, ...), custom_call_target="tpu_custom_call" | custom-call | tf_op jit(solution)/shard_map/pallas_call | solution.py:604
  (48 shorter events, 0.4 us)
Async XLA Ops:
  4.1 4.0 %collective-permute-start = (f32[1640,128]{1,0:T(8,128)S(1)}, f32[1640,128]{1,0:T(8,128)S(1)}, u32[]{:S(2)}, u32[]{:S(2)}) collective-permute-start(f32[1640,128]{1,0:T(8,128)S(1)} %get-tuple-element.14), channel_id=1, source_target_pairs={{0,1},{1,0},{2,3},{3,2},{4,5},{5,4},{6,7},{7,6},{8,9},{9,8},{10,11... | collective-permute-start | bytes 2519048 | tf_op jit(solution)/shard_map/ppermute | solution.py:623
  4.7 9.4 %collective-permute-start.3 = (bf16[128,1024]{1,0:T(8,128)(2,1)S(1)}, bf16[128,1024]{1,0:T(8,128)(2,1)S(1)}, u32[]{:S(2)}, u32[]{:S(2)}) collective-permute-start(bf16[128,1024]{1,0:T(8,128)(2,1)S(1)} %get-tuple-element.30), channel_id=1, source_target_pairs={{0,0},{1,1},{2,4},{3,5},{4,2},{5,3},{6,6},{7,7},{8,10},{9,11},{10,... | collective-permute-start | bytes 786440 | tf_op jit(solution)/shard_map/ppermute | solution.py:639
  5.3 8.7 %collective-permute-start.4 = (bf16[128,1024]{1,0:T(8,128)(2,1)S(1)}, bf16[128,1024]{1,0:T(8,128)(2,1)S(1)}, u32[]{:S(2)}, u32[]{:S(2)}) collective-permute-start(bf16[128,1024]{1,0:T(8,128)(2,1)S(1)} %get-tuple-element.31), channel_id=1, source_target_pairs={{0,1},{1,0},{2,5},{3,4},{4,3},{5,2},{6,7},{7,6},{8,11},{9,10},{10,... | collective-permute-start | bytes 786440 | tf_op jit(solution)/shard_map/ppermute | solution.py:639
  8.0 28.4 %copy-start.2 = (f32[2,2,64,128]{3,2,1,0:T(8,128)S(1)}, f32[2,2,64,128]{3,2,1,0:T(8,128)}, u32[]{:S(2)}) copy-start(f32[2,2,64,128]{3,2,1,0:T(8,128)} %param.26) | copy-start | bytes 393220
  8.0 28.4 %copy-start.3 = (bf16[128,128]{1,0:T(8,128)(2,1)S(1)}, bf16[128,128]{1,0:T(8,128)(2,1)}, u32[]{:S(2)}) copy-start(bf16[128,128]{1,0:T(8,128)(2,1)} %a_ref.1) | copy-start | bytes 98308
  8.0 28.4 %copy-start.4 = (s32[32]{0:T(128)S(1)}, s32[32]{0:T(128)}, u32[]{:S(2)}) copy-start(s32[32]{0:T(128)} %slots_ref.3) | copy-start | bytes 388
  8.0 28.4 %copy-start.5 = (s32[8]{0:T(128)S(1)}, s32[8]{0:T(128)}, u32[]{:S(2)}) copy-start(s32[8]{0:T(128)} %held_ref.3) | copy-start | bytes 100
  8.1 28.4 %copy-start.6 = (f32[2]{0:T(128)S(1)}, f32[2]{0:T(128)}, u32[]{:S(2)}) copy-start(f32[2]{0:T(128)} %bias_ref.5) | copy-start | bytes 28
  8.1 28.4 %copy-start.7 = (f32[2]{0:T(128)S(1)}, f32[2]{0:T(128)}, u32[]{:S(2)}) copy-start(f32[2]{0:T(128)} %rate_ref.5) | copy-start | bytes 28
  8.1 28.4 %copy-start.8 = (s32[8]{0:T(128)S(1)}, s32[8]{0:T(128)}, u32[]{:S(2)}) copy-start(s32[8]{0:T(128)} %tenants_ref.1) | copy-start | bytes 100
  8.1 38.2 %copy-start.9 = (f32[128]{0:T(128)S(1)}, f32[128]{0:T(128)}, u32[]{:S(2)}) copy-start(f32[128]{0:T(128)} %param.25) | copy-start | bytes 1540
  8.1 38.2 %copy-start.10 = (f32[2]{0:T(128)S(1)}, f32[2]{0:T(128)}, u32[]{:S(2)}) copy-start(f32[2]{0:T(128)} %skip_ref.1) | copy-start | bytes 28
  8.4 15.7 %collective-permute-start.1 = (f16[1000,128]{1,0:T(8,128)(2,1)S(1)}, f16[1000,128]{1,0:T(8,128)(2,1)S(1)}, u32[]{:S(2)}, u32[]{:S(2)}) collective-permute-start(f16[1000,128]{1,0:T(8,128)(2,1)S(1)} %pad_maximum_fusion), channel_id=1, source_target_pairs={{0,2},{1,3},{2,0},{3,1},{4,6},{5,7},{6,4},{7,5},{8,10},{9,11},{10,... | collective-permute-start | bytes 768008 | tf_op jit(solution)/shard_map/ppermute | solution.py:623
  14.1 47.9 %copy-start = (bf16[3,32,1024]{2,1,0:T(8,128)(2,1)S(1)}, bf16[3,32,1024]{2,1,0:T(8,128)(2,1)}, u32[]{:S(2)}) copy-start(bf16[3,32,1024]{2,1,0:T(8,128)(2,1)} %param.16) | copy-start | bytes 589828
  14.1 47.9 %copy-start.1 = (bf16[64,1024]{1,0:T(8,128)(2,1)S(1)}, bf16[64,1024]{1,0:T(8,128)(2,1)}, u32[]{:S(2)}) copy-start(bf16[64,1024]{1,0:T(8,128)(2,1)} %up_ref.5) | copy-start | bytes 393220
  14.2 22.3 %collective-permute-start.5 = (bf16[1,2,128,1024]{3,2,1,0:T(8,128)(2,1)S(1)}, bf16[1,2,128,1024]{3,2,1,0:T(8,128)(2,1)S(1)}, u32[]{:S(2)}, u32[]{:S(2)}) collective-permute-start(bf16[1,2,128,1024]{3,2,1,0:T(8,128)(2,1)S(1)} %maximum_bitcast_fusion.rest_0_), channel_id=1, source_target_pairs={{0,8},{8,0},{16,24},{24,16},{1,9},{9,1},{17,25},{25,17},{2,10},{10... | collective-permute-start | bytes 1572872 | tf_op jit(solution)/shard_map/ppermute | solution.py:626
  24.3 11.0 %collective-permute-start.2 = (f16[680,128]{1,0:T(8,128)(2,1)S(1)}, f16[680,128]{1,0:T(8,128)(2,1)S(1)}, u32[]{:S(2)}, u32[]{:S(2)}) collective-permute-start(f16[680,128]{1,0:T(8,128)(2,1)S(1)} %pad_maximum_fusion.1), channel_id=1, source_target_pairs={{0,4},{1,5},{2,6},{3,7},{4,0},{5,1},{6,2},{7,3},{8,12},{9,13},{10,... | collective-permute-start | bytes 522248 | tf_op jit(solution)/shard_map/ppermute | solution.py:623
  26.0 25.1 %collective-permute-start.13 = (bf16[1,2,128,1024]{3,2,1,0:T(8,128)(2,1)S(1)}, bf16[1,2,128,1024]{3,2,1,0:T(8,128)(2,1)S(1)}, u32[]{:S(2)}, u32[]{:S(2)}) collective-permute-start(bf16[1,2,128,1024]{3,2,1,0:T(8,128)(2,1)S(1)} %maximum_bitcast_fusion.rest_0_), channel_id=1, source_target_pairs={{0,16},{8,24},{16,0},{24,8},{1,17},{9,25},{17,1},{25,9},{2,18},{10... | collective-permute-start | bytes 1572872 | tf_op jit(solution)/shard_map/ppermute | solution.py:626
  37.4 9.7 %collective-permute-start.6 = (f16[288,128]{1,0:T(8,128)(2,1)S(1)}, f16[288,128]{1,0:T(8,128)(2,1)S(1)}, u32[]{:S(2)}, u32[]{:S(2)}) collective-permute-start(f16[288,128]{1,0:T(8,128)(2,1)S(1)} %convert_element_type.22), channel_id=1, source_target_pairs={{0,8},{8,0},{16,24},{24,16},{1,9},{9,1},{17,25},{25,17},{2,10},{10... | collective-permute-start | bytes 221192 | tf_op jit(solution)/shard_map/ppermute | solution.py:626
  42.2 6.4 %collective-permute-start.7 = (f16[288,128]{1,0:T(8,128)(2,1)S(1)}, f16[288,128]{1,0:T(8,128)(2,1)S(1)}, u32[]{:S(2)}, u32[]{:S(2)}) collective-permute-start(f16[288,128]{1,0:T(8,128)(2,1)S(1)} %convert_element_type.22), channel_id=1, source_target_pairs={{0,16},{8,24},{16,0},{24,8},{1,17},{9,25},{17,1},{25,9},{2,18},{10... | collective-permute-start | bytes 221192 | tf_op jit(solution)/shard_map/ppermute | solution.py:626
  44.6 5.4 %collective-permute-start.8 = (f16[288,128]{1,0:T(8,128)(2,1)S(1)}, f16[288,128]{1,0:T(8,128)(2,1)S(1)}, u32[]{:S(2)}, u32[]{:S(2)}) collective-permute-start(f16[288,128]{1,0:T(8,128)(2,1)S(1)} %convert_element_type.22), channel_id=1, source_target_pairs={{0,24},{8,16},{16,8},{24,0},{1,25},{9,17},{17,9},{25,1},{2,26},{10... | collective-permute-start | bytes 221192 | tf_op jit(solution)/shard_map/ppermute | solution.py:626
  44.7 11.4 %collective-permute-start.10 = (bf16[1,128,1024]{2,1,0:T(8,128)(2,1)S(1)}, bf16[1,128,1024]{2,1,0:T(8,128)(2,1)S(1)}, u32[]{:S(2)}, u32[]{:S(2)}) collective-permute-start(bf16[1,128,1024]{2,1,0:T(8,128)(2,1)S(1)} %slice_bitcast_fusion.1), channel_id=1, source_target_pairs={{0,16},{8,24},{16,0},{24,8},{1,17},{9,25},{17,1},{25,9},{2,18},{10... | collective-permute-start | bytes 786440 | tf_op jit(solution)/shard_map/ppermute | solution.py:626
  51.0 5.0 %collective-permute-start.9 = (bf16[1,160,128]{2,1,0:T(8,128)(2,1)S(1)}, bf16[1,160,128]{2,1,0:T(8,128)(2,1)S(1)}, u32[]{:S(2)}, u32[]{:S(2)}) collective-permute-start(bf16[1,160,128]{2,1,0:T(8,128)(2,1)S(1)} %bitcast.23), channel_id=1, source_target_pairs={{0,4},{1,5},{2,6},{3,7},{4,0},{5,1},{6,2},{7,3},{8,12},{9,13},{10,... | collective-permute-start | bytes 122888 | tf_op jit(solution)/shard_map/ppermute | solution.py:623
  51.1 9.6 %collective-permute-start.14 = (bf16[1,128,1024]{2,1,0:T(8,128)(2,1)S(1)}, bf16[1,128,1024]{2,1,0:T(8,128)(2,1)S(1)}, u32[]{:S(2)}, u32[]{:S(2)}) collective-permute-start(bf16[1,128,1024]{2,1,0:T(8,128)(2,1)S(1)} %slice_bitcast_fusion), channel_id=1, source_target_pairs={{0,8},{8,0},{16,24},{24,16},{1,9},{9,1},{17,25},{25,17},{2,10},{10... | collective-permute-start | bytes 786440 | tf_op jit(solution)/shard_map/ppermute | solution.py:626
  56.0 4.5 %collective-permute-start.11 = (bf16[2,160,128]{2,1,0:T(8,128)(2,1)S(1)}, bf16[2,160,128]{2,1,0:T(8,128)(2,1)S(1)}, u32[]{:S(2)}, u32[]{:S(2)}) collective-permute-start(bf16[2,160,128]{2,1,0:T(8,128)(2,1)S(1)} %pad_maximum_fusion.3), channel_id=1, source_target_pairs={{0,2},{1,3},{2,0},{3,1},{4,6},{5,7},{6,4},{7,5},{8,10},{9,11},{10,... | collective-permute-start | bytes 245768 | tf_op jit(solution)/shard_map/ppermute | solution.py:623
  60.6 1.5 %collective-permute-start.12 = (bf16[4,160,128]{2,1,0:T(8,128)(2,1)S(1)}, bf16[4,160,128]{2,1,0:T(8,128)(2,1)S(1)}, u32[]{:S(2)}, u32[]{:S(2)}) collective-permute-start(bf16[4,160,128]{2,1,0:T(8,128)(2,1)S(1)} %pad_maximum_fusion.2.a_ref), channel_id=1, source_target_pairs={{0,1},{1,0},{2,3},{3,2},{4,5},{5,4},{6,7},{7,6},{8,9},{9,8},{10,11... | collective-permute-start | bytes 491528 | tf_op jit(solution)/shard_map/ppermute | solution.py:623

commit v7 on v6

--- a/solution.py
+++ b/solution.py
@@ -561,38 +561,56 @@
     )(slots, held, bias, rate, summed, within, prefill_normed, norm_scale, *finals)
 
 
+def core_products(sources, weights, core, x_ref, w_refs):
+    pairs, at = [], 0
+    for j, part in enumerate(weights):
+        for k in range(len(sources)):
+            chip = looked_up(sources[k], lax.axis_index("grp") ^ j, lax.axis_index("head") // 2)
+            place = (w_refs[at], (k, core)) if len(part) == 1 else (w_refs[at + core], (k,))
+            pairs.append((x_ref[chip], place))
+        at += len(part)
+    return pairs
+
+
+def near_rows(sources, near, weights, prefill_rows, decode_rows):
+    width = prefill_rows.shape[1]
+    rows = near.shape[1]
+    flat = [w for part in weights for w in part]
+
+    def body(a_ref, up_ref, ud_ref, *rest):
+        w_refs, o_ref = rest[:-1], rest[-1]
+        total = jnp.concatenate([up_ref[...], ud_ref[...]], axis=0).astype(F32)
+        for left, (w_ref, at) in core_products(sources, weights, 0, a_ref, w_refs):
+            total = total + mxu(left, w_ref[at])
+        o_ref[...] = total
+
+    return pl.pallas_call(
+        body,
+        out_shape=jax.ShapeDtypeStruct((rows, width), F32),
+        in_specs=[VMEM] * (3 + len(flat)),
+        out_specs=VMEM,
+        compiler_params=pltpu.CompilerParams(vmem_limit_bytes=BIG),
+    )(near, prefill_rows, decode_rows, *flat)
+
+
 def output_rows(sources, near, far, weights, prefill_rows, decode_rows):
-    chips, rows, _ = near.shape
+    rows = near.shape[1]
     prefill, width = prefill_rows.shape
-    parts = len(weights)
-    per_part = chips // parts
     tile = width // 4 if width % 512 == 0 else width
     tiles = width // tile
     flat = [w for part in weights for w in part]
-
-    def body(a_ref, b_ref, up_ref, ud_ref, *rest):
+    begun = near_rows(sources, near, weights, prefill_rows, decode_rows)
+
+    def body(b_ref, t_ref, *rest):
         w_refs = rest[: len(flat)]
         op_ref, od_ref, total_ref, sems = rest[len(flat) :]
-        lefts, rights, at = [], [], 0
-        for j in range(parts):
-            for k in range(per_part):
-                chip = looked_up(sources[k], lax.axis_index("grp") ^ j, lax.axis_index("head") // 2)
-                if len(weights[j]) == 1:
-                    lefts.append(jnp.concatenate([a_ref[chip], b_ref[chip]], axis=1))
-                    rights.append((w_refs[at], (k,), 2))
-                else:
-                    lefts.extend([a_ref[chip], b_ref[chip]])
-                    rights.extend([(w_refs[at], (k,), 1), (w_refs[at + 1], (k,), 1)])
-            at += len(weights[j])
+        pairs = core_products(sources, weights, 1, b_ref, w_refs)
         copies = []
         for t in range(tiles):
             columns = slice(t * tile, (t + 1) * tile)
-            total = jnp.concatenate([up_ref[:, columns], ud_ref[:, columns]], axis=0).astype(F32)
-            for left, (w_ref, (k,), cores) in zip(lefts, rights):
-                if cores == 2:
-                    total = total + mxu(left, w_ref[k, :, :, columns].reshape(left.shape[1], tile))
-                else:
-                    total = total + mxu(left, w_ref[k, :, columns])
+            total = t_ref[:, columns]
+            for left, (w_ref, at) in pairs:
+                total = total + mxu(left, w_ref[at + (slice(None), columns)])
             total_ref[t] = total
             copies.append(pltpu.make_async_copy(total_ref.at[t, :prefill], op_ref.at[:, columns], sems.at[2 * t]))
             copies.append(pltpu.make_async_copy(total_ref.at[t, prefill:], od_ref.at[:, columns], sems.at[2 * t + 1]))
@@ -607,11 +625,11 @@
             jax.ShapeDtypeStruct(prefill_rows.shape, F32),
             jax.ShapeDtypeStruct(decode_rows.shape, F32),
         ),
-        in_specs=[VMEM] * (4 + len(flat)),
+        in_specs=[VMEM] * (2 + len(flat)),
         out_specs=(pl.BlockSpec(memory_space=pltpu.HBM),) * 2,
         scratch_shapes=[pltpu.VMEM((tiles, rows, tile), F32), pltpu.SemaphoreType.DMA((2 * tiles,))],
         compiler_params=pltpu.CompilerParams(vmem_limit_bytes=BIG),
-    )(near, far, prefill_rows, decode_rows, *flat)
+    )(far, begun, *flat)
 
 
 def solution(mesh):

time: 63.6 us -> 63.5 us (level)
  transfers between devices with their start and end apart: 15 -> 15, of which waited for: 7 -> 7; matrix products, arithmetic and copies ran while one was open for 1% -> 1% of each run, Pallas kernels for 8% -> 9%
where the time goes in v7:
time: 63.5 us; the launch traced here: 63.3 us
  starting transfers between devices  34.8 us (55%)
  waiting for transfers between devices  16.3 us (26%)
  Pallas kernels  10.4 us (16%)
  between operations  1 us (2%)
    ppermute x7, starting transfers between devices, over_groups(): return lax.ppermute(x, 'grp', [(i, i ^ distance) for i in range(groups)])  25.9 us
    ppermute x6, waiting for transfers between devices, across(): return lax.ppermute(x, 'head', [(i, i ^ distance) for i in range(heads)])  12.3 us
    ppermute x6, starting transfers between devices, across(): return lax.ppermute(x, 'head', [(i, i ^ distance) for i in range(heads)])  8.14 us
    ppermute x7, waiting for transfers between devices, over_groups(): return lax.ppermute(x, 'grp', [(i, i ^ distance) for i in range(groups)])  4 us
    pallas_call x1, Pallas kernels, project(): pl.pallas_call(send_body, out_shape=(jax.ShapeDtypeStruct((total, LANES),...  3.46 us
    pallas_call x1, Pallas kernels, project(): pl.pallas_call(keep_body, out_shape=jax.ShapeDtypeStruct((base, LANES), F...  2.54 us
    pallas_call x1, Pallas kernels, output_rows(): pl.pallas_call(body, out_shape=(jax.ShapeDtypeStruct(prefill_rows.shape,...  1.29 us
  transfers between devices with their start and end apart: 15, of which 7 were waited for; matrix products, arithmetic and copies ran while one was open for 1% of the time, Pallas kernels for 9%

profile of v7, /device:TPU:0, one launch (start us, length us, event | category | flops | bytes accessed | tf_op | source)
XLA Modules:
  0.0 63.3 jit_solution(9611899187507044892)
XLA Ops:
  0.6 3.5 %shard_map.159 = (f32[1640,128]{1,0:T(8,128)S(1)}, bf16[1,2,128,1024]{3,2,1,0:T(8,128)(2,1)S(1)}) custom-call(s32[32]{0:T(128)} %slots_ref.3, s32[8]{0:T(128)} %held_ref.3, s32[8]{0:T(128)} %tenants_ref.1, bf16[64,1024]{1,0:T(8,128)(2,1)} %up_ref.5, bf16[96,1024]{1,0:T(8,128)(2,1)} %bitcast.18, bf16[1024,2048]{1,0:T(8,128)(2,1)} %w_ref.3, ...), custom_call_target="tpu_custom_call" | custom-call | flops 335544320 | bytes 2097152 | tf_op jit(solution)/shard_map/pallas_call | solution.py:232
  4.1 0.5 collective-permute-start
  4.7 0.7 %collective-permute-start.3 = (bf16[128,1024]{1,0:T(8,128)(2,1)S(1)}, bf16[128,1024]{1,0:T(8,128)(2,1)S(1)}, u32[]{:S(2)}, u32[]{:S(2)}) collective-permute-start(bf16[128,1024]{1,0:T(8,128)(2,1)S(1)} %get-tuple-element.30), channel_id=1, source_target_pairs={{0,0},{1,1},{2,4},{3,5},{4,2},{5,3},{6,6},{7,7},{8,10},{9,11},{10,... | collective-permute-start | bytes 786440 | tf_op jit(solution)/shard_map/ppermute | solution.py:657
  5.3 0.1 collective-permute-start.4
  5.5 2.5 %shard_map.158 = f32[1280,128]{1,0:T(8,128)S(1)} custom-call(bf16[64,1024]{1,0:T(8,128)(2,1)} %up_ref.5, bf16[96,1024]{1,0:T(8,128)(2,1)} %bitcast.19, bf16[1024,2048]{1,0:T(8,128)(2,1)} %w_ref.3), custom_call_target="tpu_custom_call" | custom-call | flops 335544320 | bytes 2097152 | tf_op jit(solution)/shard_map/pallas_call | solution.py:261
  8.1 0.1 fusion.1
  8.3 0.1 pad_maximum_fusion
  8.4 5.7 %collective-permute-start.1 = (f16[1000,128]{1,0:T(8,128)(2,1)S(1)}, f16[1000,128]{1,0:T(8,128)(2,1)S(1)}, u32[]{:S(2)}, u32[]{:S(2)}) collective-permute-start(f16[1000,128]{1,0:T(8,128)(2,1)S(1)} %pad_maximum_fusion), channel_id=1, source_target_pairs={{0,2},{1,3},{2,0},{3,1},{4,6},{5,7},{6,4},{7,5},{8,10},{9,11},{10,... | collective-permute-start | bytes 768008 | tf_op jit(solution)/shard_map/ppermute | solution.py:641
  14.2 9.9 %collective-permute-start.5 = (bf16[1,2,128,1024]{3,2,1,0:T(8,128)(2,1)S(1)}, bf16[1,2,128,1024]{3,2,1,0:T(8,128)(2,1)S(1)}, u32[]{:S(2)}, u32[]{:S(2)}) collective-permute-start(bf16[1,2,128,1024]{3,2,1,0:T(8,128)(2,1)S(1)} %maximum_bitcast_fusion.rest_0_), channel_id=1, source_target_pairs={{0,8},{8,0},{16,24},{24,16},{1,9},{9,1},{17,25},{25,17},{2,10},{10... | collective-permute-start | bytes 1572872 | tf_op jit(solution)/shard_map/ppermute | solution.py:644
  24.1 0.1 fusion
  24.2 0.1 pad_maximum_fusion.1
  24.3 1.7 %collective-permute-start.2 = (f16[680,128]{1,0:T(8,128)(2,1)S(1)}, f16[680,128]{1,0:T(8,128)(2,1)S(1)}, u32[]{:S(2)}, u32[]{:S(2)}) collective-permute-start(f16[680,128]{1,0:T(8,128)(2,1)S(1)} %pad_maximum_fusion.1), channel_id=1, source_target_pairs={{0,4},{1,5},{2,6},{3,7},{4,0},{5,1},{6,2},{7,3},{8,12},{9,13},{10,... | collective-permute-start | bytes 522248 | tf_op jit(solution)/shard_map/ppermute | solution.py:641
  26.0 5.7 %collective-permute-start.13 = (bf16[1,2,128,1024]{3,2,1,0:T(8,128)(2,1)S(1)}, bf16[1,2,128,1024]{3,2,1,0:T(8,128)(2,1)S(1)}, u32[]{:S(2)}, u32[]{:S(2)}) collective-permute-start(bf16[1,2,128,1024]{3,2,1,0:T(8,128)(2,1)S(1)} %maximum_bitcast_fusion.rest_0_), channel_id=1, source_target_pairs={{0,16},{8,24},{16,0},{24,8},{1,17},{9,25},{17,1},{25,9},{2,18},{10... | collective-permute-start | bytes 1572872 | tf_op jit(solution)/shard_map/ppermute | solution.py:644
  31.6 3.7 %collective-permute-done.2 = f16[680,128]{1,0:T(8,128)(2,1)S(1)} collective-permute-done((f16[680,128]{1,0:T(8,128)(2,1)S(1)}, f16[680,128]{1,0:T(8,128)(2,1)S(1)}, u32[]{:S(2)}, u32[]{:S(2)}) %collective-permute-start.2) | collective-permute-done | bytes 174112 | tf_op jit(solution)/shard_map/ppermute | solution.py:641
  35.3 1.1 %collective-permute-done.5.rest_1_ = bf16[1,2,128,1024]{3,2,1,0:T(8,128)(2,1)S(1)} collective-permute-done((bf16[1,2,128,1024]{3,2,1,0:T(8,128)(2,1)S(1)}, bf16[1,2,128,1024]{3,2,1,0:T(8,128)(2,1)S(1)}, u32[]{:S(2)}, u32[]{:S(2)}) %collective-permute-start.5) | collective-permute-done | bytes 524320 | tf_op jit(solution)/shard_map/ppermute | solution.py:644
  36.5 0.9 %shard_map.160 = (f32[160,128]{1,0:T(8,128)S(1)}, f32[288,128]{1,0:T(8,128)S(1)}) custom-call(s32[32]{0:T(128)S(1)} %copy-done.4, s32[8]{0:T(128)S(1)} %copy-done.5, s32[8]{0:T(128)S(1)} %copy-done.8, f32[2]{0:T(128)S(1)} %copy-done.6, f32[2]{0:T(128)S(1)} %copy-done.7, f32[680,128]{1,0:T(8,128)S(1)} %slice_add_fusion.1.x_ref, ...), custom_call_target="tpu_custom_call" | custom-call | tf_op jit(solution)/shard_map/pallas_call | solution.py:444
  37.4 4.7 %collective-permute-start.6 = (f16[288,128]{1,0:T(8,128)(2,1)S(1)}, f16[288,128]{1,0:T(8,128)(2,1)S(1)}, u32[]{:S(2)}, u32[]{:S(2)}) collective-permute-start(f16[288,128]{1,0:T(8,128)(2,1)S(1)} %convert_element_type.22), channel_id=1, source_target_pairs={{0,8},{8,0},{16,24},{24,16},{1,9},{9,1},{17,25},{25,17},{2,10},{10... | collective-permute-start | bytes 221192 | tf_op jit(solution)/shard_map/ppermute | solution.py:644
  42.1 2.5 %collective-permute-start.7 = (f16[288,128]{1,0:T(8,128)(2,1)S(1)}, f16[288,128]{1,0:T(8,128)(2,1)S(1)}, u32[]{:S(2)}, u32[]{:S(2)}) collective-permute-start(f16[288,128]{1,0:T(8,128)(2,1)S(1)} %convert_element_type.22), channel_id=1, source_target_pairs={{0,16},{8,24},{16,0},{24,8},{1,17},{9,25},{17,1},{25,9},{2,18},{10... | collective-permute-start | bytes 221192 | tf_op jit(solution)/shard_map/ppermute | solution.py:644
  44.6 1.6 %collective-permute-start.10 = (bf16[1,128,1024]{2,1,0:T(8,128)(2,1)S(1)}, bf16[1,128,1024]{2,1,0:T(8,128)(2,1)S(1)}, u32[]{:S(2)}, u32[]{:S(2)}) collective-permute-start(bf16[1,128,1024]{2,1,0:T(8,128)(2,1)S(1)} %slice_bitcast_fusion.1), channel_id=1, source_target_pairs={{0,16},{8,24},{16,0},{24,8},{1,17},{9,25},{17,1},{25,9},{2,18},{10... | collective-permute-start | bytes 786440 | tf_op jit(solution)/shard_map/ppermute | solution.py:644
  46.2 0.8 %shard_map.161 = (bf16[64,128]{1,0:T(8,128)(2,1)S(1)}, f32[96,128]{1,0:T(8,128)S(1)}) custom-call(f32[2]{0:T(128)S(1)} %copy-done.6, f32[2]{0:T(128)S(1)} %copy-done.7, f32[2]{0:T(128)S(1)} %copy-done.10, f32[680,128]{1,0:T(8,128)S(1)} %slice_add_fusion.1.x_ref, f32[160,128]{1,0:T(8,128)S(1)} %get-tuple-element.17.v_ref, f32[2,128,128]{2,1,0:T(8,128)S(1)} %bitcast.22, ...), custom_call_target="tpu_custom_call" | custom-call | tf_op jit(solution)/shard_map/pallas_call | solution.py:508
  47.1 1.4 %collective-permute-done.7 = f16[288,128]{1,0:T(8,128)(2,1)S(1)} collective-permute-done((f16[288,128]{1,0:T(8,128)(2,1)S(1)}, f16[288,128]{1,0:T(8,128)(2,1)S(1)}, u32[]{:S(2)}, u32[]{:S(2)}) %collective-permute-start.7) | collective-permute-done | bytes 73760 | tf_op jit(solution)/shard_map/ppermute | solution.py:644
  48.5 1.4 %collective-permute-done.8 = f16[288,128]{1,0:T(8,128)(2,1)S(1)} collective-permute-done((f16[288,128]{1,0:T(8,128)(2,1)S(1)}, f16[288,128]{1,0:T(8,128)(2,1)S(1)}, u32[]{:S(2)}, u32[]{:S(2)}) %collective-permute-start.8) | collective-permute-done | bytes 73760 | tf_op jit(solution)/shard_map/ppermute | solution.py:644
  50.0 1.0 %shard_map.162 = bf16[160,128]{1,0:T(8,128)(2,1)S(1)} custom-call(s32[32]{0:T(128)S(1)} %copy-done.4, s32[8]{0:T(128)S(1)} %copy-done.5, f32[2]{0:T(128)S(1)} %copy-done.6, f32[2]{0:T(128)S(1)} %copy-done.7, f32[680,128]{1,0:T(8,128)S(1)} %slice_add_fusion.1.x_ref, f32[96,128]{1,0:T(8,128)S(1)} %get-tuple-element.18.y_ref, ...), custom_call_target="tpu_custom_call" | custom-call | tf_op jit(solution)/shard_map/pallas_call | solution.py:555
  51.0 0.1 collective-permute-start.9
  51.1 1.5 %collective-permute-start.14 = (bf16[1,128,1024]{2,1,0:T(8,128)(2,1)S(1)}, bf16[1,128,1024]{2,1,0:T(8,128)(2,1)S(1)}, u32[]{:S(2)}, u32[]{:S(2)}) collective-permute-start(bf16[1,128,1024]{2,1,0:T(8,128)(2,1)S(1)} %slice_bitcast_fusion), channel_id=1, source_target_pairs={{0,8},{8,0},{16,24},{24,16},{1,9},{9,1},{17,25},{25,17},{2,10},{10... | collective-permute-start | bytes 786440 | tf_op jit(solution)/shard_map/ppermute | solution.py:644
  52.5 3.5 %collective-permute-done.9 = bf16[1,160,128]{2,1,0:T(8,128)(2,1)S(1)} collective-permute-done((bf16[1,160,128]{2,1,0:T(8,128)(2,1)S(1)}, bf16[1,160,128]{2,1,0:T(8,128)(2,1)S(1)}, u32[]{:S(2)}, u32[]{:S(2)}) %collective-permute-start.9) | collective-permute-done | bytes 40992 | tf_op jit(solution)/shard_map/ppermute | solution.py:641
  56.0 0.2 collective-permute-start.11
  56.2 4.3 %collective-permute-done.11 = bf16[2,160,128]{2,1,0:T(8,128)(2,1)S(1)} collective-permute-done((bf16[2,160,128]{2,1,0:T(8,128)(2,1)S(1)}, bf16[2,160,128]{2,1,0:T(8,128)(2,1)S(1)}, u32[]{:S(2)}, u32[]{:S(2)}) %collective-permute-start.11) | collective-permute-done | bytes 81952 | tf_op jit(solution)/shard_map/ppermute | solution.py:641
  60.6 0.1 collective-permute-start.12
  60.7 0.5 shard_map.163.t_ref
  61.2 0.9 %collective-permute-done.12.b_ref = bf16[4,160,128]{2,1,0:T(8,128)(2,1)S(1)} collective-permute-done((bf16[4,160,128]{2,1,0:T(8,128)(2,1)S(1)}, bf16[4,160,128]{2,1,0:T(8,128)(2,1)S(1)}, u32[]{:S(2)}, u32[]{:S(2)}) %collective-permute-start.12) | collective-permute-done | bytes 163872 | tf_op jit(solution)/shard_map/ppermute | solution.py:641
  62.0 1.3 %shard_map.164 = (f32[64,1024]{1,0:T(8,128)}, f32[96,1024]{1,0:T(8,128)}) custom-call(bf16[4,160,128]{2,1,0:T(8,128)(2,1)S(1)} %collective-permute-done.12.b_ref, f32[160,1024]{1,0:T(8,128)S(1)} %shard_map.163.t_ref, bf16[1,2,128,1024]{3,2,1,0:T(8,128)(2,1)S(1)} %maximum_bitcast_fusion.rest_0_, bf16[1,2,128,1024]{3,2,1,0:T(8,128)(2,1)S(1)} %collective-permute-done.5.rest_1_, ...), custom_call_target="tpu_custom_call" | custom-call | tf_op jit(solution)/shard_map/pallas_call | solution.py:622
  (49 shorter events, 0.5 us)
Async XLA Ops:
  4.1 4.0 %collective-permute-start = (f32[1640,128]{1,0:T(8,128)S(1)}, f32[1640,128]{1,0:T(8,128)S(1)}, u32[]{:S(2)}, u32[]{:S(2)}) collective-permute-start(f32[1640,128]{1,0:T(8,128)S(1)} %get-tuple-element.14), channel_id=1, source_target_pairs={{0,1},{1,0},{2,3},{3,2},{4,5},{5,4},{6,7},{7,6},{8,9},{9,8},{10,11... | collective-permute-start | bytes 2519048 | tf_op jit(solution)/shard_map/ppermute | solution.py:641
  4.7 9.4 %collective-permute-start.3 = (bf16[128,1024]{1,0:T(8,128)(2,1)S(1)}, bf16[128,1024]{1,0:T(8,128)(2,1)S(1)}, u32[]{:S(2)}, u32[]{:S(2)}) collective-permute-start(bf16[128,1024]{1,0:T(8,128)(2,1)S(1)} %get-tuple-element.30), channel_id=1, source_target_pairs={{0,0},{1,1},{2,4},{3,5},{4,2},{5,3},{6,6},{7,7},{8,10},{9,11},{10,... | collective-permute-start | bytes 786440 | tf_op jit(solution)/shard_map/ppermute | solution.py:657
  5.3 8.7 %collective-permute-start.4 = (bf16[128,1024]{1,0:T(8,128)(2,1)S(1)}, bf16[128,1024]{1,0:T(8,128)(2,1)S(1)}, u32[]{:S(2)}, u32[]{:S(2)}) collective-permute-start(bf16[128,1024]{1,0:T(8,128)(2,1)S(1)} %get-tuple-element.31), channel_id=1, source_target_pairs={{0,1},{1,0},{2,5},{3,4},{4,3},{5,2},{6,7},{7,6},{8,11},{9,10},{10,... | collective-permute-start | bytes 786440 | tf_op jit(solution)/shard_map/ppermute | solution.py:657
  8.0 28.4 %copy-start.2 = (f32[2,2,64,128]{3,2,1,0:T(8,128)S(1)}, f32[2,2,64,128]{3,2,1,0:T(8,128)}, u32[]{:S(2)}) copy-start(f32[2,2,64,128]{3,2,1,0:T(8,128)} %param.26) | copy-start | bytes 393220
  8.0 28.4 %copy-start.3 = (bf16[128,128]{1,0:T(8,128)(2,1)S(1)}, bf16[128,128]{1,0:T(8,128)(2,1)}, u32[]{:S(2)}) copy-start(bf16[128,128]{1,0:T(8,128)(2,1)} %a_ref.1) | copy-start | bytes 98308
  8.0 28.4 %copy-start.4 = (s32[32]{0:T(128)S(1)}, s32[32]{0:T(128)}, u32[]{:S(2)}) copy-start(s32[32]{0:T(128)} %slots_ref.3) | copy-start | bytes 388
  8.0 28.4 %copy-start.5 = (s32[8]{0:T(128)S(1)}, s32[8]{0:T(128)}, u32[]{:S(2)}) copy-start(s32[8]{0:T(128)} %held_ref.3) | copy-start | bytes 100
  8.1 28.4 %copy-start.6 = (f32[2]{0:T(128)S(1)}, f32[2]{0:T(128)}, u32[]{:S(2)}) copy-start(f32[2]{0:T(128)} %bias_ref.5) | copy-start | bytes 28
  8.1 28.4 %copy-start.7 = (f32[2]{0:T(128)S(1)}, f32[2]{0:T(128)}, u32[]{:S(2)}) copy-start(f32[2]{0:T(128)} %rate_ref.5) | copy-start | bytes 28
  8.1 28.4 %copy-start.8 = (s32[8]{0:T(128)S(1)}, s32[8]{0:T(128)}, u32[]{:S(2)}) copy-start(s32[8]{0:T(128)} %tenants_ref.1) | copy-start | bytes 100
  8.1 38.2 %copy-start.9 = (f32[128]{0:T(128)S(1)}, f32[128]{0:T(128)}, u32[]{:S(2)}) copy-start(f32[128]{0:T(128)} %param.25) | copy-start | bytes 1540
  8.1 38.1 %copy-start.10 = (f32[2]{0:T(128)S(1)}, f32[2]{0:T(128)}, u32[]{:S(2)}) copy-start(f32[2]{0:T(128)} %skip_ref.1) | copy-start | bytes 28
  8.4 15.7 %collective-permute-start.1 = (f16[1000,128]{1,0:T(8,128)(2,1)S(1)}, f16[1000,128]{1,0:T(8,128)(2,1)S(1)}, u32[]{:S(2)}, u32[]{:S(2)}) collective-permute-start(f16[1000,128]{1,0:T(8,128)(2,1)S(1)} %pad_maximum_fusion), channel_id=1, source_target_pairs={{0,2},{1,3},{2,0},{3,1},{4,6},{5,7},{6,4},{7,5},{8,10},{9,11},{10,... | collective-permute-start | bytes 768008 | tf_op jit(solution)/shard_map/ppermute | solution.py:641
  14.1 46.5 %copy-start = (bf16[3,32,1024]{2,1,0:T(8,128)(2,1)S(1)}, bf16[3,32,1024]{2,1,0:T(8,128)(2,1)}, u32[]{:S(2)}) copy-start(bf16[3,32,1024]{2,1,0:T(8,128)(2,1)} %param.16) | copy-start | bytes 589828
  14.1 46.5 %copy-start.1 = (bf16[64,1024]{1,0:T(8,128)(2,1)S(1)}, bf16[64,1024]{1,0:T(8,128)(2,1)}, u32[]{:S(2)}) copy-start(bf16[64,1024]{1,0:T(8,128)(2,1)} %up_ref.5) | copy-start | bytes 393220
  14.2 22.3 %collective-permute-start.5 = (bf16[1,2,128,1024]{3,2,1,0:T(8,128)(2,1)S(1)}, bf16[1,2,128,1024]{3,2,1,0:T(8,128)(2,1)S(1)}, u32[]{:S(2)}, u32[]{:S(2)}) collective-permute-start(bf16[1,2,128,1024]{3,2,1,0:T(8,128)(2,1)S(1)} %maximum_bitcast_fusion.rest_0_), channel_id=1, source_target_pairs={{0,8},{8,0},{16,24},{24,16},{1,9},{9,1},{17,25},{25,17},{2,10},{10... | collective-permute-start | bytes 1572872 | tf_op jit(solution)/shard_map/ppermute | solution.py:644
  24.3 11.0 %collective-permute-start.2 = (f16[680,128]{1,0:T(8,128)(2,1)S(1)}, f16[680,128]{1,0:T(8,128)(2,1)S(1)}, u32[]{:S(2)}, u32[]{:S(2)}) collective-permute-start(f16[680,128]{1,0:T(8,128)(2,1)S(1)} %pad_maximum_fusion.1), channel_id=1, source_target_pairs={{0,4},{1,5},{2,6},{3,7},{4,0},{5,1},{6,2},{7,3},{8,12},{9,13},{10,... | collective-permute-start | bytes 522248 | tf_op jit(solution)/shard_map/ppermute | solution.py:641
  26.0 25.1 %collective-permute-start.13 = (bf16[1,2,128,1024]{3,2,1,0:T(8,128)(2,1)S(1)}, bf16[1,2,128,1024]{3,2,1,0:T(8,128)(2,1)S(1)}, u32[]{:S(2)}, u32[]{:S(2)}) collective-permute-start(bf16[1,2,128,1024]{3,2,1,0:T(8,128)(2,1)S(1)} %maximum_bitcast_fusion.rest_0_), channel_id=1, source_target_pairs={{0,16},{8,24},{16,0},{24,8},{1,17},{9,25},{17,1},{25,9},{2,18},{10... | collective-permute-start | bytes 1572872 | tf_op jit(solution)/shard_map/ppermute | solution.py:644
  37.4 9.7 %collective-permute-start.6 = (f16[288,128]{1,0:T(8,128)(2,1)S(1)}, f16[288,128]{1,0:T(8,128)(2,1)S(1)}, u32[]{:S(2)}, u32[]{:S(2)}) collective-permute-start(f16[288,128]{1,0:T(8,128)(2,1)S(1)} %convert_element_type.22), channel_id=1, source_target_pairs={{0,8},{8,0},{16,24},{24,16},{1,9},{9,1},{17,25},{25,17},{2,10},{10... | collective-permute-start | bytes 221192 | tf_op jit(solution)/shard_map/ppermute | solution.py:644
  42.1 6.4 %collective-permute-start.7 = (f16[288,128]{1,0:T(8,128)(2,1)S(1)}, f16[288,128]{1,0:T(8,128)(2,1)S(1)}, u32[]{:S(2)}, u32[]{:S(2)}) collective-permute-start(f16[288,128]{1,0:T(8,128)(2,1)S(1)} %convert_element_type.22), channel_id=1, source_target_pairs={{0,16},{8,24},{16,0},{24,8},{1,17},{9,25},{17,1},{25,9},{2,18},{10... | collective-permute-start | bytes 221192 | tf_op jit(solution)/shard_map/ppermute | solution.py:644
  44.6 5.4 %collective-permute-start.8 = (f16[288,128]{1,0:T(8,128)(2,1)S(1)}, f16[288,128]{1,0:T(8,128)(2,1)S(1)}, u32[]{:S(2)}, u32[]{:S(2)}) collective-permute-start(f16[288,128]{1,0:T(8,128)(2,1)S(1)} %convert_element_type.22), channel_id=1, source_target_pairs={{0,24},{8,16},{16,8},{24,0},{1,25},{9,17},{17,9},{25,1},{2,26},{10... | collective-permute-start | bytes 221192 | tf_op jit(solution)/shard_map/ppermute | solution.py:644
  44.6 11.4 %collective-permute-start.10 = (bf16[1,128,1024]{2,1,0:T(8,128)(2,1)S(1)}, bf16[1,128,1024]{2,1,0:T(8,128)(2,1)S(1)}, u32[]{:S(2)}, u32[]{:S(2)}) collective-permute-start(bf16[1,128,1024]{2,1,0:T(8,128)(2,1)S(1)} %slice_bitcast_fusion.1), channel_id=1, source_target_pairs={{0,16},{8,24},{16,0},{24,8},{1,17},{9,25},{17,1},{25,9},{2,18},{10... | collective-permute-start | bytes 786440 | tf_op jit(solution)/shard_map/ppermute | solution.py:644
  51.0 5.0 %collective-permute-start.9 = (bf16[1,160,128]{2,1,0:T(8,128)(2,1)S(1)}, bf16[1,160,128]{2,1,0:T(8,128)(2,1)S(1)}, u32[]{:S(2)}, u32[]{:S(2)}) collective-permute-start(bf16[1,160,128]{2,1,0:T(8,128)(2,1)S(1)} %bitcast.23), channel_id=1, source_target_pairs={{0,4},{1,5},{2,6},{3,7},{4,0},{5,1},{6,2},{7,3},{8,12},{9,13},{10,... | collective-permute-start | bytes 122888 | tf_op jit(solution)/shard_map/ppermute | solution.py:641
  51.1 9.6 %collective-permute-start.14 = (bf16[1,128,1024]{2,1,0:T(8,128)(2,1)S(1)}, bf16[1,128,1024]{2,1,0:T(8,128)(2,1)S(1)}, u32[]{:S(2)}, u32[]{:S(2)}) collective-permute-start(bf16[1,128,1024]{2,1,0:T(8,128)(2,1)S(1)} %slice_bitcast_fusion), channel_id=1, source_target_pairs={{0,8},{8,0},{16,24},{24,16},{1,9},{9,1},{17,25},{25,17},{2,10},{10... | collective-permute-start | bytes 786440 | tf_op jit(solution)/shard_map/ppermute | solution.py:644
  56.0 4.5 %collective-permute-start.11 = (bf16[2,160,128]{2,1,0:T(8,128)(2,1)S(1)}, bf16[2,160,128]{2,1,0:T(8,128)(2,1)S(1)}, u32[]{:S(2)}, u32[]{:S(2)}) collective-permute-start(bf16[2,160,128]{2,1,0:T(8,128)(2,1)S(1)} %pad_maximum_fusion.3), channel_id=1, source_target_pairs={{0,2},{1,3},{2,0},{3,1},{4,6},{5,7},{6,4},{7,5},{8,10},{9,11},{10,... | collective-permute-start | bytes 245768 | tf_op jit(solution)/shard_map/ppermute | solution.py:641
  60.6 1.5 %collective-permute-start.12 = (bf16[4,160,128]{2,1,0:T(8,128)(2,1)S(1)}, bf16[4,160,128]{2,1,0:T(8,128)(2,1)S(1)}, u32[]{:S(2)}, u32[]{:S(2)}) collective-permute-start(bf16[4,160,128]{2,1,0:T(8,128)(2,1)S(1)} %pad_maximum_fusion.2.a_ref), channel_id=1, source_target_pairs={{0,1},{1,0},{2,3},{3,2},{4,5},{5,4},{6,7},{7,6},{8,9},{9,8},{10,11... | collective-permute-start | bytes 491528 | tf_op jit(solution)/shard_map/ppermute | solution.py:641
